TPU v7x, 32 devices: a whole 2x2x4 slice. The times are simulated.
32 devices in a mesh: section: 2 (over core), shard: 4 (over z), replica: 4 (over y, x).
Axes of the slice: x: 2, y: 2, z: 4, core: 2. Of those that a mesh axis runs over, the one named last changes fastest.
Arguments:
- inputs: bfloat16 [2, 16, 256, 1152], P(None, ('shard', 'replica')), may hold values from -6 to 6
- cotangent: bfloat16 [2, 16, 256, 1152], P(None, ('shard', 'replica')), may hold values from -6 to 6
- timesteps: int32 [2, 16], P(None, ('shard', 'replica')), may hold values from 0 to 999
- labels: int32 [2, 16], P(None, ('shard', 'replica')), may hold values from 0 to 999
- class_table: bfloat16 [1000, 1152], replicated, may hold values from -6 to 6
- qkv_weight: bfloat16 [2, 1152, 3456], P('section', 'shard'), may hold values from -0.1875 to 0.1875
- qv_bias: bfloat16 [2, 2304], P('section', 'shard'), may hold values from -4 to 4
- proj_weight: bfloat16 [2, 1152, 1152], P('section', 'shard'), may hold values from -1 to 1
- proj_bias: bfloat16 [2, 1152], P('section', 'shard'), may hold values from -4 to 4
- up_projection_weight: bfloat16 [2, 1152, 4608], P('section', 'shard'), may hold values from -0.1875 to 0.1875
- up_bias: bfloat16 [2, 4608], P('section', 'shard'), may hold values from -4 to 4
- down_projection_weight: bfloat16 [2, 4608, 1152], P('section', 'shard'), may hold values from -0.09375 to 0.09375
- down_bias: bfloat16 [2, 1152], P('section', 'shard'), may hold values from -4 to 4
- ada_weight: bfloat16 [2, 1152, 6912], P('section', 'shard'), may hold values from -0.1875 to 0.1875
- ada_bias: bfloat16 [2, 6912], P('section', 'shard'), may hold values from -3.5 to 3.5
Outputs:
- block_outputs: bfloat16 [2, 2, 16, 256, 1152], P('section', None, ('shard', 'replica'))
- input_grads: float32 [2, 2, 16, 256, 1152], P('section', None, ('shard', 'replica'))
- table_grad: float32 [1000, 1152], P(('section', 'shard'))
- qkv_grad: float32 [2, 1152, 3456], P('section', 'shard')
- qv_bias_grad: float32 [2, 2304], P('section', 'shard')
- proj_grad: float32 [2, 1152, 1152], P('section', 'shard')
- proj_bias_grad: float32 [2, 1152], P('section', 'shard')
- up_grad: float32 [2, 1152, 4608], P('section', 'shard')
- up_bias_grad: float32 [2, 4608], P('section', 'shard')
- down_grad: float32 [2, 4608, 1152], P('section', 'shard')
- down_bias_grad: float32 [2, 1152], P('section', 'shard')
- ada_grad: float32 [2, 1152, 6912], P('section', 'shard')
- ada_bias_grad: float32 [2, 6912], P('section', 'shard')
All inputs are finite; a program needn't handle non-finite values.
Results may differ from a plain program's by a relative error of at most 0.035.
Values may be sent and summed in bfloat16 or wider, within the bound.
No kernel may reach another device: no remote copies, remote signals or barrier semaphores. Data moves between devices by JAX's collectives and lax.ppermute only.
A program may use at most 384 MiB of HBM per device.

v0:
```python
import functools
import math

import jax
import jax.numpy as jnp
from jax import lax
from jax.experimental import pallas as pl
from jax.experimental.pallas import tpu as pltpu
from jax.sharding import PartitionSpec as P

S = "section"
Z = "shard"
R = "replica"
ALL = (S, Z, R)
BF = jnp.bfloat16
F32 = jnp.float32
D = 1152
HEAD_DIM = 72
HEADS = 16
FF = 4608
HALF = 2304
ROWS = 288
PIECE = 144
NZ = 4
SHARDS = (1, 2, 3)
VMEM_LIMIT = 50 * 1024 * 1024


def move(value, to):
    ns, nz, nr = (lax.axis_size(a) for a in ALL)
    pairs = []
    for s in range(ns):
        for z in range(nz):
            for r in range(nr):
                there = to(s, z, r)
                if there is not None:
                    a, b, c = there
                    pairs.append(((s * nz + z) * nr + r, (a * nz + b) * nr + c))
    return lax.ppermute(value, ALL, pairs)


def swap(value):
    return move(value, lambda s, z, r: (1 - s, z, r))


def to_core(value, core):
    return move(value, lambda s, z, r: (core, z, r) if s != core else None)


def zshift(value, by=1):
    nz = lax.axis_size(Z)
    return move(value, lambda s, z, r: (s, (z + by) % nz, r))


def cross(value, bit):
    return move(value, lambda s, z, r: (s, z, r ^ bit))


def place():
    return lax.axis_index(S), lax.axis_index(Z), lax.rem(lax.axis_index(R), 4)


def assemble_kernel(block, by_rows, mine, other, *refs):
    own, far, out, sems = refs[:4], refs[4:8], refs[8], refs[9]
    c, z, r = place()
    copies = []
    height = D if by_rows else ROWS
    target = out.at[pl.ds(z * height, height), :]
    shard_mine = pltpu.make_async_copy(mine, target, sems.at[0])
    shard_other = pltpu.make_async_copy(other, target, sems.at[0])

    @pl.when(c == block)
    def _():
        shard_mine.start()

    @pl.when(c != block)
    def _():
        shard_other.start()

    for side, group in ((0, own), (1, far)):
        core = c if side == 0 else 1 - c
        for m in range(4):
            low = lax.rem(r + m, 2)
            high = lax.rem(r // 2 + m // 2, 2)
            for k in SHARDS:
                zp = lax.rem(z + NZ - k, NZ)
                if by_rows:
                    row = zp * D + core * (D // 2) + (high * 2 + low) * PIECE
                    spot = out.at[pl.ds(row, PIECE), :]
                else:
                    row = zp * ROWS + low * PIECE
                    col = pl.multiple_of((core * 2 + high) * D, D)
                    spot = out.at[pl.ds(row, PIECE), pl.ds(col, D)]
                n = 1 + (side * 4 + m) * 3 + k - 1
                copies.append(pltpu.make_async_copy(group[m].at[k - 1], spot, sems.at[n]))
    for copy in copies:
        copy.start()
    shard_mine.wait()
    for copy in copies:
        copy.wait()


def assemble(block, by_rows, mine, other, own, far):
    shape = (FF, D) if by_rows else (D, FF)
    return pl.pallas_call(
        functools.partial(assemble_kernel, block, by_rows),
        out_shape=jax.ShapeDtypeStruct(shape, BF),
        in_specs=[pl.BlockSpec(memory_space=pl.ANY)] * 10,
        out_specs=pl.BlockSpec(memory_space=pl.ANY),
        scratch_shapes=[pltpu.SemaphoreType.DMA((25,))],
        cost_estimate=pl.CostEstimate(flops=0, bytes_accessed=4 * D * FF, transcendentals=0),
    )(mine, other, *own, *far)


def own_piece(block, by_rows, mine, other):
    c, z, r = place()
    if by_rows:
        start = ((c * 4 + r) * PIECE, 0)
    else:
        start = (lax.rem(r, 2) * PIECE, (c * 2 + r // 2) * D)
    part = [lax.dynamic_slice(w, start, (PIECE, D)) for w in (mine, other)]
    return jnp.where(c == block, part[0], part[1])


def gather_item(block, by_rows, mine, other, x_first):
    first = own_piece(block, by_rows, mine, other)
    ring = []
    value = first
    for _ in SHARDS:
        value = zshift(value)
        ring.append(value)
    p0 = jnp.stack(ring)
    p1 = cross(p0, 1)
    p2 = cross(p0, 2)
    p3 = cross(p1, 2) if x_first else cross(p2, 1)
    own = (p0, p1, p2, p3)
    far = tuple(swap(p) for p in own)
    return assemble(block, by_rows, mine, other, own, far)


def wgrad_kernel(kind, lo, lx, ro, rx, g0, g1, g2, g3, acc):
    c, z, r = place()
    outs = (g0, g1, g2, g3)
    for g in range(2):
        u = lax.rem(g + r // 2, 2)
        if kind == 0:
            left = c * u
        elif kind == 1:
            left = 0
        else:
            left = u
        cols = pl.ds(0, D) if kind == 2 else pl.ds(pl.multiple_of(u * D, D), D)
        acc[...] = jnp.dot(lo[left], ro[:, cols], preferred_element_type=F32) + jnp.dot(
            lx[left], rx[:, cols], preferred_element_type=F32
        )
        for par in range(2):

            @pl.when(lax.rem(r, 2) == par)
            def _():
                for zp in range(NZ):
                    k = lax.rem(z - zp + NZ, NZ)
                    for h in range(2):
                        row = (zp * 2 + h) * PIECE
                        outs[g * 2 + (h ^ par)][k] = acc[row : row + PIECE, :].astype(BF)


def wgrad(kind, lo, lx, ro, rx):
    part = jax.ShapeDtypeStruct((NZ, PIECE, D), BF)
    return pl.pallas_call(
        functools.partial(wgrad_kernel, kind),
        out_shape=(part,) * 4,
        in_specs=[pl.BlockSpec(memory_space=pltpu.VMEM)] * 4,
        out_specs=(pl.BlockSpec(memory_space=pltpu.VMEM),) * 4,
        scratch_shapes=[pltpu.VMEM((D, D), F32)],
        compiler_params=pltpu.CompilerParams(vmem_limit_bytes=VMEM_LIMIT),
        cost_estimate=pl.CostEstimate(
            flops=2 * 512 * D * HALF, bytes_accessed=2 * D * HALF + 6 * 512 * D, transcendentals=0
        ),
    )(lo, lx, ro, rx)


def plus(a, b):
    return (a.astype(F32) + b.astype(F32)).astype(BF)


def reduce_item(parts, x_first):
    g0, g1, g2, g3 = parts
    if x_first:
        k0 = plus(g0, cross(g1, 1))
        k2 = plus(g2, cross(g3, 1))
        full = plus(k0, cross(k2, 2))
    else:
        k0 = plus(g0, cross(g2, 2))
        k1 = plus(g1, cross(g3, 2))
        full = plus(k0, cross(k1, 1))
    value = zshift(full[1])
    value = zshift(plus(value, full[2]))
    value = zshift(plus(value, full[3]))
    value = plus(value, full[0])
    bit = 4
    while bit < lax.axis_size(R):
        value = plus(value, cross(value, bit))
        bit *= 2
    p1 = cross(value, 1)
    p2 = cross(value, 2)
    p3 = cross(p1, 2) if x_first else cross(p2, 1)
    return (value, p1, p2, p3)


def finish_kernel(by_rows, *refs):
    sets = refs[:8], refs[8:16]
    outs = refs[16:]
    acc = outs[-1] if len(outs) == 3 else outs[0]
    c, z, r = place()
    for block in range(2):

        @pl.when(c == block)
        def _():
            for side in range(2):
                core = c if side == 0 else 1 - c
                for m in range(4):
                    low = lax.rem(r + m, 2)
                    high = lax.rem(r // 2 + m // 2, 2)
                    piece = sets[block][side * 4 + m][...].astype(F32)
                    if by_rows:
                        row = core * (D // 2) + (high * 2 + low) * PIECE
                        acc[pl.ds(row, PIECE), :] = piece
                    else:
                        col = pl.multiple_of((core * 2 + high) * D, D)
                        acc[pl.ds(low * PIECE, PIECE), pl.ds(col, D)] = piece

    if len(outs) == 3:
        outs[0][...] = acc[:, : 3 * D]
        outs[1][...] = acc[:, 3 * D :]


def finish(kind, parts):
    by_rows = kind == 2
    if kind == 0:
        shapes = ((ROWS, 3 * D), (ROWS, D))
        scratch = [pltpu.VMEM((ROWS, FF), F32)]
    else:
        shapes = ((D, D),) if by_rows else ((ROWS, FF),)
        scratch = []
    return pl.pallas_call(
        functools.partial(finish_kernel, by_rows),
        out_shape=tuple(jax.ShapeDtypeStruct(s, F32) for s in shapes),
        in_specs=[pl.BlockSpec(memory_space=pltpu.VMEM)] * 16,
        out_specs=(pl.BlockSpec(memory_space=pltpu.VMEM),) * len(shapes),
        scratch_shapes=scratch,
        compiler_params=pltpu.CompilerParams(vmem_limit_bytes=VMEM_LIMIT),
        cost_estimate=pl.CostEstimate(flops=0, bytes_accessed=8 * ROWS * FF, transcendentals=0),
    )(*parts[0], *parts[1])


def standard(v):
    mean = jnp.mean(v, axis=-1, keepdims=True)
    centred = v - mean
    rstd = lax.rsqrt(jnp.mean(centred * centred, axis=-1, keepdims=True) + 1e-06)
    return centred * rstd, rstd


def mm(a, b):
    return jnp.dot(a, b, preferred_element_type=F32)


def mmt(a, b):
    return lax.dot_general(a, b, (((1,), (1,)), ((), ())), preferred_element_type=F32)


def heads(v):
    return v.reshape(v.shape[0], HEADS, HEAD_DIM).transpose(1, 0, 2)


def joined(v):
    return v.transpose(1, 0, 2).reshape(v.shape[1], D)


def batched(a, b, ca, cb):
    return lax.dot_general(a, b, (((ca,), (cb,)), ((0,), (0,))), preferred_element_type=F32)


def forward(x, ada, weights, biases):
    wa, wu, wd = weights
    qv_bias, proj_bias, up_bias, down_bias = biases
    sh_a, sc_a, g_a, sh_m, sc_m, g_m = ada
    xf = x.astype(F32)
    n1, r1 = standard(xf)
    attn_in = (n1 * (1.0 + sc_a) + sh_a).astype(BF)
    proj = mm(attn_in, wa[:, : 3 * D])
    q = heads(((proj[:, :D] + qv_bias[:D]) * HEAD_DIM**-0.5).astype(BF))
    k = heads(proj[:, D : 2 * D].astype(BF))
    v = heads((proj[:, 2 * D :] + qv_bias[D:]).astype(BF))
    soft = jax.nn.softmax(batched(q, k, 2, 2), axis=-1)
    probs = soft.astype(BF)
    mixed = joined(batched(probs, v, 2, 1)).astype(BF)
    attended = mm(mixed, wa[:, 3 * D :]) + proj_bias
    mid = xf + g_a * attended
    n2, r2 = standard(mid)
    mlp_in = (n2 * (1.0 + sc_m) + sh_m).astype(BF)
    hidden = mm(mlp_in, wu) + up_bias
    act = jax.nn.gelu(hidden, approximate=True).astype(BF)
    branch = mm(act, wd) + down_bias
    out = (mid + g_m * branch).astype(BF)
    kept = (n1, r1, attn_in, q, k, v, soft, probs, mixed, attended, n2, r2, mlp_in, hidden, act, branch)
    return out, kept


def rows_sum(v):
    return jnp.sum(v.astype(F32), axis=0)


def norm_back(g, n, rstd):
    return rstd * (
        g - jnp.mean(g, axis=-1, keepdims=True) - n * jnp.mean(g * n, axis=-1, keepdims=True)
    )


def backward(grad, ada, weights, kept):
    wa, wu, wd = weights
    sh_a, sc_a, g_a, sh_m, sc_m, g_m = ada
    (n1, r1, attn_in, q, k, v, soft, probs, mixed, attended, n2, r2, mlp_in, hidden, act, branch) = kept
    d_branch = (g_m * grad).astype(BF)
    d_gate_m = rows_sum(grad * branch)
    d_act = mmt(d_branch, wd)
    _, back = jax.vjp(functools.partial(jax.nn.gelu, approximate=True), hidden)
    d_hidden = back(d_act)[0].astype(BF)
    d_mlp_in = mmt(d_hidden, wu)
    d_shift_m = rows_sum(d_mlp_in)
    d_scale_m = rows_sum(d_mlp_in * n2)
    d_mid = grad + norm_back(d_mlp_in * (1.0 + sc_m), n2, r2)
    d_att = (g_a * d_mid).astype(BF)
    d_gate_a = rows_sum(d_mid * attended)
    d_mixed = heads(mmt(d_att, wa[:, 3 * D :]).astype(BF))
    d_v = batched(probs, d_mixed, 1, 1).astype(BF)
    d_probs = batched(d_mixed, v, 2, 2)
    d_s = (soft * (d_probs - jnp.sum(d_probs * soft, axis=-1, keepdims=True))).astype(BF)
    d_q = (batched(d_s, k, 2, 1) * HEAD_DIM**-0.5).astype(BF)
    d_k = batched(d_s, q, 1, 1).astype(BF)
    d_qkv = jnp.concatenate([joined(d_q), joined(d_k), joined(d_v)], axis=-1)
    d_attn_in = mmt(d_qkv, wa[:, : 3 * D])
    d_shift_a = rows_sum(d_attn_in)
    d_scale_a = rows_sum(d_attn_in * n1)
    d_x = d_mid + norm_back(d_attn_in * (1.0 + sc_a), n1, r1)
    d_ada = jnp.concatenate(
        [d_shift_a, d_scale_a, d_gate_a, d_shift_m, d_scale_m, d_gate_m]
    ).astype(BF)
    sums_qkv = rows_sum(d_qkv)
    sums = jnp.concatenate(
        [sums_qkv[:D], sums_qkv[2 * D :], rows_sum(d_att), rows_sum(d_hidden), rows_sum(d_branch)]
    )
    lefts = (jnp.stack([attn_in.T, mixed.T]), mlp_in.T[None], act.T)
    rights = (jnp.concatenate([d_qkv, d_att], axis=-1), d_hidden, d_branch)
    return d_x, d_ada, sums, lefts, rights


def item_grads(kind, left, right):
    c = lax.axis_index(S)
    if kind == 2:
        groups = left.reshape(NZ, 2, 2, ROWS, left.shape[-1])

        def part(core):
            half = lax.dynamic_index_in_dim(groups, core, 1, keepdims=False)
            return half.transpose(1, 0, 2, 3).reshape(2, D, left.shape[-1])

        lo, lx = part(c), swap(part(1 - c))
        ro, rx = right, swap(right)
    else:
        lo, lx = left, swap(left)
        ro = lax.dynamic_slice_in_dim(right, c * HALF, HALF, 1)
        rx = swap(lax.dynamic_slice_in_dim(right, (1 - c) * HALF, HALF, 1))
    return wgrad(kind, lo, lx, ro, rx)


def embed_time(steps):
    half = D // 2
    freq = jnp.exp(-math.log(10000.0) * jnp.arange(half, dtype=F32) / half)
    angles = steps.astype(F32)[:, None] * freq[None, :]
    return jnp.concatenate([jnp.cos(angles), jnp.sin(angles)], axis=-1)


def by_shard(rel):
    z = lax.axis_index(Z)
    order = lax.rem(z - jnp.arange(NZ) + NZ, NZ)
    return jnp.take(rel, order, axis=0)


def per_device(
    inputs,
    cotangent,
    timesteps,
    labels,
    class_table,
    qkv_weight,
    qv_bias,
    proj_weight,
    proj_bias,
    up_weight,
    up_bias,
    down_weight,
    down_bias,
    ada_weight,
    ada_bias,
):
    c = lax.axis_index(S)
    z = lax.axis_index(Z)
    is_first = c == 0

    ids = jnp.concatenate([timesteps, labels], axis=1)
    ids_rel = jnp.stack([ids] + [zshift(ids, k) for k in SHARDS])
    vectors = jnp.concatenate(
        [qv_bias[0], proj_bias[0], up_bias[0], down_bias[0], ada_bias[0]]
    )[None]
    vec_rel = jnp.concatenate([vectors] + [zshift(vectors, k) for k in SHARDS])
    vec_mine = by_shard(vec_rel).astype(F32)
    vec_other = by_shard(swap(vec_rel)).astype(F32)

    def cond_of(steps, classes):
        return embed_time(steps) + jnp.take(class_table, classes, axis=0).astype(F32)

    cond_rel = cond_of(ids_rel[..., 0].reshape(-1), ids_rel[..., 1].reshape(-1))
    silu_rel = jax.nn.silu(cond_rel).astype(BF)
    rows_rel = lax.dynamic_slice_in_dim(silu_rel, z * ROWS, ROWS, 1)
    partial_rel = mm(rows_rel, ada_weight[0]).reshape(NZ, 2, -1)
    ada_sum = partial_rel[0]
    for k in SHARDS:
        ada_sum = ada_sum + zshift(partial_rel[k], -k)
    lengths = (qv_bias.shape[1], proj_bias.shape[1], up_bias.shape[1], down_bias.shape[1], ada_bias.shape[1])

    def split_vectors(vec):
        out = []
        at = 0
        for n in lengths:
            out.append(vec[:, at : at + n].reshape(-1))
            at += n
        return out

    mine_split = split_vectors(vec_mine)
    other_split = split_vectors(vec_other)
    ada_sum = ada_sum + mine_split[4][None]
    ada_keep = lax.dynamic_index_in_dim(ada_sum, c, 0, keepdims=False)
    ada_got = swap(lax.dynamic_index_in_dim(ada_sum, 1 - c, 0, keepdims=False))
    adas = []
    biases = []
    for block in range(2):
        here = c == block
        adas.append(jnp.split(jnp.where(here, ada_keep, ada_got), 6))
        biases.append(
            [jnp.where(here, a, b) for a, b in zip(mine_split[:4], other_split[:4])]
        )

    mine = (
        jnp.concatenate([qkv_weight[0], proj_weight[0]], axis=1),
        up_weight[0],
        down_weight[0],
    )
    other = tuple(swap(w) for w in mine)
    weights = []
    for block in range(2):
        weights.append(
            [
                gather_item(block, kind == 2, mine[kind], other[kind], (block + kind) % 2 == 0)
                for kind in range(3)
            ]
        )

    x = lax.dynamic_index_in_dim(inputs, c, 0, keepdims=False)[0]
    cot = lax.dynamic_index_in_dim(cotangent, c, 0, keepdims=False)[0]
    y0, kept0 = forward(x, adas[0], weights[0], biases[0])
    y1, kept1 = forward(y0, adas[1], weights[1], biases[1])
    dx1, dada1, sums1, lefts1, rights1 = backward(cot.astype(F32), adas[1], weights[1], kept1)
    dx1 = dx1.astype(BF)
    reduced = {}
    for kind in (2, 1, 0):
        reduced[1, kind] = reduce_item(item_grads(kind, lefts1[kind], rights1[kind]), kind % 2 == 0)
    dx0, dada0, sums0, lefts0, rights0 = backward(dx1.astype(F32), adas[0], weights[0], kept0)
    for kind in (2, 1, 0):
        reduced[0, kind] = reduce_item(item_grads(kind, lefts0[kind], rights0[kind]), kind % 2 == 1)
    grads = []
    for kind in range(3):
        parts = []
        for block in range(2):
            own = reduced[block, kind]
            parts.append(own + tuple(to_core(p, block) for p in own))
        grads.append(finish(kind, parts))
    (qkv_grad, proj_grad), (up_grad,), (down_grad,) = grads

    def both_micros(v0, v1):
        keep = jnp.where(is_first, v0, v1)
        got = swap(jnp.where(is_first, v1, v0))
        return jnp.stack([jnp.where(is_first, keep, got), jnp.where(is_first, got, keep)])

    block_outputs = both_micros(y0, y1)[None, :, None]
    input_grads = both_micros(dx0, dx1.astype(F32))[None, :, None]

    sums = lax.psum(jnp.stack([sums0, sums1]), ALL)
    sums = lax.dynamic_index_in_dim(sums, c, 0, keepdims=False)

    def own_slice(vec):
        n = vec.shape[0] // NZ
        return lax.dynamic_slice_in_dim(vec, z * n, n, 0)[None]

    qv_bias_grad = own_slice(sums[: 2 * D])
    proj_bias_grad = own_slice(sums[2 * D : 3 * D])
    up_bias_grad = own_slice(sums[3 * D : 3 * D + FF])
    down_bias_grad = own_slice(sums[3 * D + FF :])

    ids_all = lax.all_gather(ids, (Z, R), axis=1, tiled=False).reshape(2, -1, 2)
    cond_all = cond_of(ids_all[..., 0].reshape(-1), ids_all[..., 1].reshape(-1))
    labels_all = ids_all[..., 1].reshape(-1)
    dada_all = lax.all_gather(jnp.stack([dada0, dada1]), ALL, axis=0, tiled=False)
    dada_own = lax.dynamic_index_in_dim(dada_all, c, 1, keepdims=False)
    cond_rows = lax.dynamic_slice_in_dim(cond_all, z * ROWS, ROWS, 1)
    silu_rows = jax.nn.silu(cond_rows).astype(BF)
    ada_grad = lax.dot_general(
        silu_rows, dada_own, (((0,), (0,)), ((), ())), preferred_element_type=F32
    )
    ada_bias_grad = own_slice(rows_sum(dada_own))
    d_silu = mmt(dada_own, ada_weight[0])
    _, silu_back = jax.vjp(jax.nn.silu, cond_rows)
    d_cond = silu_back(d_silu)[0]
    d_cond = d_cond + swap(d_cond)
    cond_rel_all = jnp.stack([d_cond] + [zshift(d_cond, k) for k in SHARDS])
    d_cond_all = by_shard(cond_rel_all).transpose(1, 0, 2).reshape(-1, D)
    row_count = class_table.shape[0] // (2 * NZ)
    row_ids = (c * NZ + z) * row_count + jnp.arange(row_count, dtype=jnp.int32)
    owner = (row_ids[:, None] == labels_all[None, :]).astype(F32)
    table_grad = jnp.dot(owner, d_cond_all, precision=lax.Precision.HIGHEST)

    return (
        block_outputs,
        input_grads,
        table_grad,
        qkv_grad[None],
        qv_bias_grad,
        proj_grad[None],
        proj_bias_grad,
        up_grad[None],
        up_bias_grad,
        down_grad[None],
        down_bias_grad,
        ada_grad[None],
        ada_bias_grad,
    )


def solution(mesh):
    rows = P(None, (Z, R), None, None)
    matrix = P(S, Z, None)
    vector = P(S, Z)
    pair = P(None, (Z, R))
    in_specs = (rows, rows, pair, pair, P()) + (matrix, vector) * 5
    acts = P(S, None, (Z, R), None, None)
    out_specs = (acts, acts, P((S, Z), None)) + (matrix, vector) * 5
    return jax.shard_map(
        per_device, mesh=mesh, in_specs=in_specs, out_specs=out_specs, check_vma=False
    )
```

profile of v0, /device:TPU:0, one launch (start us, length us, event | category | flops | bytes accessed | tf_op | source)
XLA Modules:
  0.0 3294.7 jit_solution(7059129317459314819)
XLA Ops:
  22.0 38.3 %all-gather.2 = s32[16,2,2]{2,1,0:T(2,128)S(1)} all-gather(s32[1,2,2]{2,1,0:T(2,128)S(1)} %get-tuple-element.230), channel_id=2, replica_groups=mesh['section'=2,'shard'=4,'replica'=4] {'shard','replica'}, dimensions={0}, use_global_device_ids=true | all-gather | bytes 272 | tf_op jit(solution)/shard_map/all_gather | solution.py:508
  112.6 31.1 collective-permute-done.13
  150.0 21.6 collective-permute-done.24
  239.3 18.9 collective-permute-done.16.refs_3_
  264.6 16.8 collective-permute-done.28.refs_3_
  281.9 322.9 %shard_map.246 = bf16[1152,4608]{1,0:T(8,128)(2,1)} custom-call(bf16[288,4608]{1,0:T(8,128)(2,1)} %pad_maximum_fusion.mine, bf16[288,4608]{1,0:T(8,128)(2,1)} %collective-permute-done.10.other, bf16[3,144,1152]{2,1,0:T(8,128)(2,1)} %copy-done.62, bf16[3,144,1152]{2,1,0:T(8,128)(2,1)} %collective-permute-done.14.refs_1_, ...), custom_call_target="tpu_custom_call" | custom-call | bytes 21233664 | tf_op jit(solution)/shard_map/pallas_call | solution.py:105
  619.6 14.4 dot_general.128
  638.9 323.0 %shard_map.247 = bf16[1152,4608]{1,0:T(8,128)(2,1)} custom-call(bf16[288,4608]{1,0:T(8,128)(2,1)} %bitcast.382, bf16[288,4608]{1,0:T(8,128)(2,1)} %collective-permute-done.22.other, bf16[3,144,1152]{2,1,0:T(8,128)(2,1)} %copy-done.63, bf16[3,144,1152]{2,1,0:T(8,128)(2,1)} %collective-permute-done.26.refs_1_, ...), custom_call_target="tpu_custom_call" | custom-call | bytes 21233664 | tf_op jit(solution)/shard_map/pallas_call | solution.py:105
  993.2 322.9 %shard_map.248 = bf16[4608,1152]{1,0:T(8,128)(2,1)} custom-call(bf16[1152,1152]{1,0:T(8,128)(2,1)} %bitcast.386, bf16[1152,1152]{1,0:T(8,128)(2,1)} %collective-permute-done.33.other, bf16[3,144,1152]{2,1,0:T(8,128)(2,1)} %pad_maximum_fusion.9.refs_0_, bf16[3,144,1152]{2,1,0:T(8,128)(2,1)} %collective-permute-done.37.refs_1_, ...), custom_call_target="tpu_custom_call" | custom-call | bytes 21233664 | tf_op jit(solution)/shard_map/pallas_call | solution.py:105
  1332.4 322.9 %shard_map.249 = bf16[1152,4608]{1,0:T(8,128)(2,1)} custom-call(bf16[288,4608]{1,0:T(8,128)(2,1)} %pad_maximum_fusion.mine, bf16[288,4608]{1,0:T(8,128)(2,1)} %collective-permute-done.10.other, bf16[3,144,1152]{2,1,0:T(8,128)(2,1)} %pad_maximum_fusion.10.refs_0_, bf16[3,144,1152]{2,1,0:T(8,128)(2,1)} %collective-permute-done.47.refs_1_, ...), custom_call_target="tpu_custom_call" | custom-call | bytes 21233664 | tf_op jit(solution)/shard_map/pallas_call | solution.py:105
  1668.2 14.4 dot_general.129
  1691.9 15.5 collective-permute-done.69.refs_3_
  1708.0 322.9 %shard_map.250 = bf16[1152,4608]{1,0:T(8,128)(2,1)} custom-call(bf16[288,4608]{1,0:T(8,128)(2,1)} %bitcast.383, bf16[288,4608]{1,0:T(8,128)(2,1)} %collective-permute-done.22.other, bf16[3,144,1152]{2,1,0:T(8,128)(2,1)} %pad_maximum_fusion.11.refs_0_, bf16[3,144,1152]{2,1,0:T(8,128)(2,1)} %collective-permute-done.57.refs_1_, ...), custom_call_target="tpu_custom_call" | custom-call | bytes 21233664 | tf_op jit(solution)/shard_map/pallas_call | solution.py:105
  2041.5 323.0 %shard_map.251 = bf16[4608,1152]{1,0:T(8,128)(2,1)} custom-call(bf16[1152,1152]{1,0:T(8,128)(2,1)} %bitcast.387, bf16[1152,1152]{1,0:T(8,128)(2,1)} %collective-permute-done.33.other, bf16[3,144,1152]{2,1,0:T(8,128)(2,1)} %pad_maximum_fusion.12.refs_0_, bf16[3,144,1152]{2,1,0:T(8,128)(2,1)} %collective-permute-done.67.refs_1_, ...), custom_call_target="tpu_custom_call" | custom-call | bytes 21233664 | tf_op jit(solution)/shard_map/pallas_call | solution.py:105
  2469.0 68.5 %all-gather.3 = bf16[32,2,6912]{2,1,0:T(2,128)(2,1)S(1)} all-gather(bf16[1,2,6912]{2,1,0:T(2,128)(2,1)S(1)} %maximum_bitcast_fusion.2), channel_id=3, replica_groups=mesh['section'=2,'shard'=4,'replica'=4] {'section','shard','replica'}, dimensions={0}, use_global_device_ids=true | all-gather | bytes 912384 | tf_op jit(solution)/shard_map/all_gather | solution.py:511
  2672.1 25.8 collective-permute-done.113
  2709.0 27.4 collective-permute-done.143
  2742.0 16.3 collective-permute-done.84
  2760.9 25.9 collective-permute-done.97
  2791.1 24.1 collective-permute-done.112
  2827.9 15.8 collective-permute-done.129
  2854.7 17.4 collective-permute-done.144
  2874.3 25.1 collective-permute-done.157
  3131.4 98.5 %all-reduce.2.cloned.1.call-done = f32[2,9216]{1,0:T(2,128)} async-done(((f32[2,9216]{1,0:T(2,128)}), f32[2,9216]{1,0:T(2,128)}) %all-reduce.2.cloned.1.call-update) | async-done | bytes 73744 | tf_op jit(solution)/shard_map/psum | solution.py:496
  (1081 shorter events, 823.9 us)
Async XLA Ops:
  7.2 3222.7 %all-reduce.2.cloned.1.call-start = ((), (), s32[]{:S(2)}) async-start(), calls=%async_computation | async-start | bytes 147456 | tf_op jit(solution)/shard_map/psum | solution.py:496
  263.8 370.5 %collective-permute-start.29 = (bf16[3,144,1152]{2,1,0:T(8,128)(2,1)S(1)}, bf16[3,144,1152]{2,1,0:T(8,128)(2,1)}, u32[]{:S(2)}, u32[]{:S(2)}) collective-permute-start(bf16[3,144,1152]{2,1,0:T(8,128)(2,1)S(1)} %pad_maximum_fusion.8.refs_0_), channel_id=1, source_target_pairs={{0,16},{1,17},{2,18},{3,19},{4,20},{5,21},{6,22},{7,23},{8,24},{9,... | collective-permute-start | bytes 2985992 | tf_op jit(solution)/shard_map/ppermute | solution.py:39
  264.4 369.5 %collective-permute-start.37 = (bf16[3,144,1152]{2,1,0:T(8,128)(2,1)}, bf16[3,144,1152]{2,1,0:T(8,128)(2,1)}, u32[]{:S(2)}, u32[]{:S(2)}) collective-permute-start(bf16[3,144,1152]{2,1,0:T(8,128)(2,1)} %pad_maximum_fusion.9.refs_0_), channel_id=1, source_target_pairs={{0,1},{1,0},{2,3},{3,2},{4,5},{5,4},{6,7},{7,6},{8,9},{9,8},{10,11... | collective-permute-start | bytes 2985992 | tf_op jit(solution)/shard_map/ppermute | solution.py:39
  264.4 371.7 %collective-permute-start.31 = (bf16[3,144,1152]{2,1,0:T(8,128)(2,1)}, bf16[3,144,1152]{2,1,0:T(8,128)(2,1)}, u32[]{:S(2)}, u32[]{:S(2)}) collective-permute-start(bf16[3,144,1152]{2,1,0:T(8,128)(2,1)} %collective-permute-done.27.refs_2_), channel_id=1, source_target_pairs={{0,16},{1,17},{2,18},{3,19},{4,20},{5,21},{6,22},{7,23},{8,24},{9,... | collective-permute-start | bytes 2985992 | tf_op jit(solution)/shard_map/ppermute | solution.py:39
  281.4 353.0 %collective-permute-start.30 = (bf16[3,144,1152]{2,1,0:T(8,128)(2,1)}, bf16[3,144,1152]{2,1,0:T(8,128)(2,1)}, u32[]{:S(2)}, u32[]{:S(2)}) collective-permute-start(bf16[3,144,1152]{2,1,0:T(8,128)(2,1)} %collective-permute-done.26.refs_1_), channel_id=1, source_target_pairs={{0,16},{1,17},{2,18},{3,19},{4,20},{5,21},{6,22},{7,23},{8,24},{9,... | collective-permute-start | bytes 2985992 | tf_op jit(solution)/shard_map/ppermute | solution.py:39
  281.4 357.4 %collective-permute-start.32 = (bf16[3,144,1152]{2,1,0:T(8,128)(2,1)}, bf16[3,144,1152]{2,1,0:T(8,128)(2,1)}, u32[]{:S(2)}, u32[]{:S(2)}) collective-permute-start(bf16[3,144,1152]{2,1,0:T(8,128)(2,1)} %collective-permute-done.28.refs_3_), channel_id=1, source_target_pairs={{0,16},{1,17},{2,18},{3,19},{4,20},{5,21},{6,22},{7,23},{8,24},{9,... | collective-permute-start | bytes 2985992 | tf_op jit(solution)/shard_map/ppermute | solution.py:39
  634.4 332.3 %collective-permute-start.48 = (bf16[3,144,1152]{2,1,0:T(8,128)(2,1)}, bf16[3,144,1152]{2,1,0:T(8,128)(2,1)}, u32[]{:S(2)}, u32[]{:S(2)}) collective-permute-start(bf16[3,144,1152]{2,1,0:T(8,128)(2,1)} %pad_maximum_fusion.10.refs_0_), channel_id=1, source_target_pairs={{0,2},{1,3},{2,0},{3,1},{4,6},{5,7},{6,4},{7,5},{8,10},{9,11},{10,... | collective-permute-start | bytes 2985992 | tf_op jit(solution)/shard_map/ppermute | solution.py:39
  636.1 332.5 %collective-permute-start.39 = (bf16[3,144,1152]{2,1,0:T(8,128)(2,1)}, bf16[3,144,1152]{2,1,0:T(8,128)(2,1)}, u32[]{:S(2)}, u32[]{:S(2)}) collective-permute-start(bf16[3,144,1152]{2,1,0:T(8,128)(2,1)} %collective-permute-done.37.refs_1_), channel_id=1, source_target_pairs={{0,2},{1,3},{2,0},{3,1},{4,6},{5,7},{6,4},{7,5},{8,10},{9,11},{10,... | collective-permute-start | bytes 2985992 | tf_op jit(solution)/shard_map/ppermute | solution.py:39
  638.8 340.2 %collective-permute-start.47 = (bf16[3,144,1152]{2,1,0:T(8,128)(2,1)}, bf16[3,144,1152]{2,1,0:T(8,128)(2,1)}, u32[]{:S(2)}, u32[]{:S(2)}) collective-permute-start(bf16[3,144,1152]{2,1,0:T(8,128)(2,1)} %pad_maximum_fusion.10.refs_0_), channel_id=1, source_target_pairs={{0,1},{1,0},{2,3},{3,2},{4,5},{5,4},{6,7},{7,6},{8,9},{9,8},{10,11... | collective-permute-start | bytes 2985992 | tf_op jit(solution)/shard_map/ppermute | solution.py:39
  979.0 347.5 %collective-permute-start.50 = (bf16[3,144,1152]{2,1,0:T(8,128)(2,1)}, bf16[3,144,1152]{2,1,0:T(8,128)(2,1)}, u32[]{:S(2)}, u32[]{:S(2)}) collective-permute-start(bf16[3,144,1152]{2,1,0:T(8,128)(2,1)} %pad_maximum_fusion.10.refs_0_), channel_id=1, source_target_pairs={{0,16},{1,17},{2,18},{3,19},{4,20},{5,21},{6,22},{7,23},{8,24},{9,... | collective-permute-start | bytes 2985992 | tf_op jit(solution)/shard_map/ppermute | solution.py:39
  979.5 349.1 %collective-permute-start.57 = (bf16[3,144,1152]{2,1,0:T(8,128)(2,1)}, bf16[3,144,1152]{2,1,0:T(8,128)(2,1)}, u32[]{:S(2)}, u32[]{:S(2)}) collective-permute-start(bf16[3,144,1152]{2,1,0:T(8,128)(2,1)} %pad_maximum_fusion.11.refs_0_), channel_id=1, source_target_pairs={{0,1},{1,0},{2,3},{3,2},{4,5},{5,4},{6,7},{7,6},{8,9},{9,8},{10,11... | collective-permute-start | bytes 2985992 | tf_op jit(solution)/shard_map/ppermute | solution.py:39
  979.6 351.0 %collective-permute-start.52 = (bf16[3,144,1152]{2,1,0:T(8,128)(2,1)}, bf16[3,144,1152]{2,1,0:T(8,128)(2,1)}, u32[]{:S(2)}, u32[]{:S(2)}) collective-permute-start(bf16[3,144,1152]{2,1,0:T(8,128)(2,1)} %collective-permute-done.48.refs_2_), channel_id=1, source_target_pairs={{0,16},{1,17},{2,18},{3,19},{4,20},{5,21},{6,22},{7,23},{8,24},{9,... | collective-permute-start | bytes 2985992 | tf_op jit(solution)/shard_map/ppermute | solution.py:39
  991.7 338.6 %collective-permute-start.51 = (bf16[3,144,1152]{2,1,0:T(8,128)(2,1)}, bf16[3,144,1152]{2,1,0:T(8,128)(2,1)}, u32[]{:S(2)}, u32[]{:S(2)}) collective-permute-start(bf16[3,144,1152]{2,1,0:T(8,128)(2,1)} %collective-permute-done.47.refs_1_), channel_id=1, source_target_pairs={{0,16},{1,17},{2,18},{3,19},{4,20},{5,21},{6,22},{7,23},{8,24},{9,... | collective-permute-start | bytes 2985992 | tf_op jit(solution)/shard_map/ppermute | solution.py:39
  992.7 337.9 %collective-permute-start.53 = (bf16[3,144,1152]{2,1,0:T(8,128)(2,1)S(1)}, bf16[3,144,1152]{2,1,0:T(8,128)(2,1)}, u32[]{:S(2)}, u32[]{:S(2)}) collective-permute-start(bf16[3,144,1152]{2,1,0:T(8,128)(2,1)S(1)} %collective-permute-done.49.refs_3_), channel_id=1, source_target_pairs={{0,16},{1,17},{2,18},{3,19},{4,20},{5,21},{6,22},{7,23},{8,24},{9,... | collective-permute-start | bytes 2985992 | tf_op jit(solution)/shard_map/ppermute | solution.py:39
  1326.5 356.0 %collective-permute-start.67 = (bf16[3,144,1152]{2,1,0:T(8,128)(2,1)}, bf16[3,144,1152]{2,1,0:T(8,128)(2,1)}, u32[]{:S(2)}, u32[]{:S(2)}) collective-permute-start(bf16[3,144,1152]{2,1,0:T(8,128)(2,1)} %pad_maximum_fusion.12.refs_0_), channel_id=1, source_target_pairs={{0,1},{1,0},{2,3},{3,2},{4,5},{5,4},{6,7},{7,6},{8,9},{9,8},{10,11... | collective-permute-start | bytes 2985992 | tf_op jit(solution)/shard_map/ppermute | solution.py:39
  1328.6 354.2 %collective-permute-start.68 = (bf16[3,144,1152]{2,1,0:T(8,128)(2,1)}, bf16[3,144,1152]{2,1,0:T(8,128)(2,1)}, u32[]{:S(2)}, u32[]{:S(2)}) collective-permute-start(bf16[3,144,1152]{2,1,0:T(8,128)(2,1)} %pad_maximum_fusion.12.refs_0_), channel_id=1, source_target_pairs={{0,2},{1,3},{2,0},{3,1},{4,6},{5,7},{6,4},{7,5},{8,10},{9,11},{10,... | collective-permute-start | bytes 2985992 | tf_op jit(solution)/shard_map/ppermute | solution.py:39
  1330.3 352.6 %collective-permute-start.58 = (bf16[3,144,1152]{2,1,0:T(8,128)(2,1)}, bf16[3,144,1152]{2,1,0:T(8,128)(2,1)}, u32[]{:S(2)}, u32[]{:S(2)}) collective-permute-start(bf16[3,144,1152]{2,1,0:T(8,128)(2,1)} %pad_maximum_fusion.11.refs_0_), channel_id=1, source_target_pairs={{0,2},{1,3},{2,0},{3,1},{4,6},{5,7},{6,4},{7,5},{8,10},{9,11},{10,... | collective-permute-start | bytes 2985992 | tf_op jit(solution)/shard_map/ppermute | solution.py:39
  1330.6 360.9 %collective-permute-start.60 = (bf16[3,144,1152]{2,1,0:T(8,128)(2,1)}, bf16[3,144,1152]{2,1,0:T(8,128)(2,1)}, u32[]{:S(2)}, u32[]{:S(2)}) collective-permute-start(bf16[3,144,1152]{2,1,0:T(8,128)(2,1)} %pad_maximum_fusion.11.refs_0_), channel_id=1, source_target_pairs={{0,16},{1,17},{2,18},{3,19},{4,20},{5,21},{6,22},{7,23},{8,24},{9,... | collective-permute-start | bytes 2985992 | tf_op jit(solution)/shard_map/ppermute | solution.py:39
  1330.6 352.6 %collective-permute-start.59 = (bf16[3,144,1152]{2,1,0:T(8,128)(2,1)}, bf16[3,144,1152]{2,1,0:T(8,128)(2,1)}, u32[]{:S(2)}, u32[]{:S(2)}) collective-permute-start(bf16[3,144,1152]{2,1,0:T(8,128)(2,1)} %collective-permute-done.57.refs_1_), channel_id=1, source_target_pairs={{0,2},{1,3},{2,0},{3,1},{4,6},{5,7},{6,4},{7,5},{8,10},{9,11},{10,... | collective-permute-start | bytes 2985992 | tf_op jit(solution)/shard_map/ppermute | solution.py:39
  1691.6 349.9 %collective-permute-start.70 = (bf16[3,144,1152]{2,1,0:T(8,128)(2,1)}, bf16[3,144,1152]{2,1,0:T(8,128)(2,1)}, u32[]{:S(2)}, u32[]{:S(2)}) collective-permute-start(bf16[3,144,1152]{2,1,0:T(8,128)(2,1)} %pad_maximum_fusion.12.refs_0_), channel_id=1, source_target_pairs={{0,16},{1,17},{2,18},{3,19},{4,20},{5,21},{6,22},{7,23},{8,24},{9,... | collective-permute-start | bytes 2985992 | tf_op jit(solution)/shard_map/ppermute | solution.py:39
  1707.4 334.1 %collective-permute-start.72 = (bf16[3,144,1152]{2,1,0:T(8,128)(2,1)}, bf16[3,144,1152]{2,1,0:T(8,128)(2,1)}, u32[]{:S(2)}, u32[]{:S(2)}) collective-permute-start(bf16[3,144,1152]{2,1,0:T(8,128)(2,1)} %collective-permute-done.68.refs_2_), channel_id=1, source_target_pairs={{0,16},{1,17},{2,18},{3,19},{4,20},{5,21},{6,22},{7,23},{8,24},{9,... | collective-permute-start | bytes 2985992 | tf_op jit(solution)/shard_map/ppermute | solution.py:39
  1707.4 334.1 %collective-permute-start.71 = (bf16[3,144,1152]{2,1,0:T(8,128)(2,1)}, bf16[3,144,1152]{2,1,0:T(8,128)(2,1)}, u32[]{:S(2)}, u32[]{:S(2)}) collective-permute-start(bf16[3,144,1152]{2,1,0:T(8,128)(2,1)} %collective-permute-done.67.refs_1_), channel_id=1, source_target_pairs={{0,16},{1,17},{2,18},{3,19},{4,20},{5,21},{6,22},{7,23},{8,24},{9,... | collective-permute-start | bytes 2985992 | tf_op jit(solution)/shard_map/ppermute | solution.py:39
  1707.9 333.6 %collective-permute-start.73 = (bf16[3,144,1152]{2,1,0:T(8,128)(2,1)}, bf16[3,144,1152]{2,1,0:T(8,128)(2,1)}, u32[]{:S(2)}, u32[]{:S(2)}) collective-permute-start(bf16[3,144,1152]{2,1,0:T(8,128)(2,1)} %collective-permute-done.69.refs_3_), channel_id=1, source_target_pairs={{0,16},{1,17},{2,18},{3,19},{4,20},{5,21},{6,22},{7,23},{8,24},{9,... | collective-permute-start | bytes 2985992 | tf_op jit(solution)/shard_map/ppermute | solution.py:39
  2637.0 420.6 %collective-permute-start.74 = (bf16[256,1152]{1,0:T(8,128)(2,1)S(1)}, bf16[256,1152]{1,0:T(8,128)(2,1)S(1)}, u32[]{:S(2)}, u32[]{:S(2)}) collective-permute-start(bf16[256,1152]{1,0:T(8,128)(2,1)S(1)} %copy-done.221), channel_id=1, source_target_pairs={{0,16},{1,17},{2,18},{3,19},{4,20},{5,21},{6,22},{7,23},{8,24},{9,... | collective-permute-start | bytes 1769480 | tf_op jit(solution)/shard_map/ppermute | solution.py:39
  (379 other events, 15548.0 us)
Sparse Core Ops, SparseCore 0:
  3112.2 117.5 all-reduce.1
where the time goes:
time: 3310 us; the launch traced here: 3290 us
  Pallas kernels  2030 us (61%)
  waiting for transfers between devices  662 us (20%)
  starting transfers between devices  152 us (5%)
  matrix products  131 us (4%)
  local copies, waits for them, and re-layouts  119 us (4%)
  blocking collectives  107 us (3%)
  other arithmetic  74 us (2%)
    pallas_call x6, Pallas kernels, assemble(): pl.pallas_call(functools.partial(assemble_kernel, block, by_rows), out_sh...  1940 us
    ppermute x170, waiting for transfers between devices, move(): return lax.ppermute(value, ALL, pairs)  564 us
    ppermute x170, starting transfers between devices, move(): return lax.ppermute(value, ALL, pairs)  152 us
    psum x1, waiting for transfers between devices, per_device(): sums = lax.psum(jnp.stack([sums0, sums1]), ALL)  98.5 us
    all_gather x1, blocking collectives, per_device(): lax.all_gather(jnp.stack([dada0, dada1]), ALL, axis=0, tiled=False)  68.5 us
  transfers between devices with their start and end apart: 171, of which 61 were waited for; matrix products, arithmetic and copies ran while one was open for 6% of the time, Pallas kernels for 52%

commit v1 on v0

v1 whole, which is shorter than its diff:
```python
import functools
import math

import jax
import jax.numpy as jnp
from jax import lax
from jax.experimental import pallas as pl
from jax.experimental.pallas import tpu as pltpu
from jax.sharding import PartitionSpec as P

S = "section"
Z = "shard"
R = "replica"
ALL = (S, Z, R)
BF = jnp.bfloat16
F32 = jnp.float32
D = 1152
HEAD_DIM = 72
HEADS = 16
FF = 4608
HALF = 2304
ROWS = 288
PIECE = 144
NZ = 4
SHARDS = (1, 2, 3)
VMEM_LIMIT = 50 * 1024 * 1024


def move(value, to):
    ns, nz, nr = (lax.axis_size(a) for a in ALL)
    pairs = []
    for s in range(ns):
        for z in range(nz):
            for r in range(nr):
                there = to(s, z, r)
                if there is not None:
                    a, b, c = there
                    pairs.append(((s * nz + z) * nr + r, (a * nz + b) * nr + c))
    return lax.ppermute(value, ALL, pairs)


def swap(value):
    return move(value, lambda s, z, r: (1 - s, z, r))


def to_core(value, core):
    return move(value, lambda s, z, r: (core, z, r) if s != core else None)


def zshift(value, by=1):
    nz = lax.axis_size(Z)
    return move(value, lambda s, z, r: (s, (z + by) % nz, r))


def trade(value):
    return lax.all_to_all(value, Z, split_axis=0, concat_axis=0, tiled=True)


def along_z(value):
    return trade(jnp.stack([value] * NZ))


def cross(value, bit):
    return move(value, lambda s, z, r: (s, z, r ^ bit))


def place():
    return lax.axis_index(S), lax.axis_index(Z), lax.rem(lax.axis_index(R), 4)


ANYWHERE = pl.BlockSpec(memory_space=pl.ANY)
INSIDE = pl.BlockSpec(memory_space=pltpu.VMEM)
PARAMS = pltpu.CompilerParams(vmem_limit_bytes=VMEM_LIMIT)
ONE = jax.ShapeDtypeStruct((PIECE, D), BF)


def cost(nbytes, flops=0):
    return pl.CostEstimate(flops=flops, bytes_accessed=nbytes, transcendentals=0)


def fence(arrays, after):
    n = len(arrays)
    return pl.pallas_call(
        lambda *refs: None,
        out_shape=tuple(jax.ShapeDtypeStruct(a.shape, a.dtype) for a in arrays),
        in_specs=[ANYWHERE] * (n + 1),
        out_specs=(ANYWHERE,) * n,
        input_output_aliases={i: i for i in range(n)},
        cost_estimate=cost(0),
    )(*arrays, after)


def stack_kernel(every, _, out):
    z = lax.axis_index(Z)
    for i in range(every.shape[1]):
        for k in SHARDS:
            out[i, k - 1] = every[lax.rem(z + NZ - k, NZ), i]


def stacked(every, after):
    n = every.shape[1]
    return pl.pallas_call(
        stack_kernel,
        out_shape=jax.ShapeDtypeStruct((n, 3, PIECE, D), BF),
        in_specs=[INSIDE, ANYWHERE],
        out_specs=INSIDE,
        compiler_params=PARAMS,
        cost_estimate=cost(12 * n * PIECE * D),
    )(every, after)


def join_kernel(*refs):
    out = refs[-1]
    for i in range(out.shape[0]):
        out[i] = refs[i][...]


def joined(parts, after):
    n = len(parts)
    return pl.pallas_call(
        join_kernel,
        out_shape=jax.ShapeDtypeStruct((n, PIECE, D), BF),
        in_specs=[INSIDE] * n + [ANYWHERE],
        out_specs=INSIDE,
        compiler_params=PARAMS,
        cost_estimate=cost(4 * n * PIECE * D),
    )(*parts, after)


def plus_kernel(n, *refs):
    outs = refs[2 * n + 1 :]
    for i in range(n):
        for j in range(2):
            whole = refs[i][j].astype(F32) + refs[n + i][j].astype(F32)
            outs[2 * i + j][...] = whole.astype(BF)


def plus(a, b, after):
    n = len(a)
    shapes = [jax.ShapeDtypeStruct(v.shape[1:], BF) for v in a for _ in range(2)]
    return pl.pallas_call(
        functools.partial(plus_kernel, n),
        out_shape=tuple(shapes),
        in_specs=[INSIDE] * (2 * n) + [ANYWHERE],
        out_specs=(INSIDE,) * (2 * n),
        compiler_params=PARAMS,
        cost_estimate=cost(6 * sum(v.size for v in a)),
    )(*a, *b, after)


def merge_kernel(*refs):
    out = refs[-1]
    for i in range(2):
        whole = refs[i][...].astype(F32) + refs[2 + i][...].astype(F32)
        out[2 * i : 2 * i + 2] = whole.astype(BF)


def merged(a, b, after):
    return pl.pallas_call(
        merge_kernel,
        out_shape=jax.ShapeDtypeStruct((NZ, PIECE, D), BF),
        in_specs=[INSIDE] * 4 + [ANYWHERE],
        out_specs=INSIDE,
        compiler_params=PARAMS,
        cost_estimate=cost(12 * NZ * PIECE * D),
    )(*a, *b, after)


def sum_kernel(parts, _, out):
    whole = parts[0].astype(F32)
    for i in range(1, parts.shape[0]):
        whole = whole + parts[i].astype(F32)
    out[...] = whole.astype(BF)


def summed(parts, after):
    n = parts.shape[0]
    return pl.pallas_call(
        sum_kernel,
        out_shape=ONE,
        in_specs=[INSIDE, ANYWHERE],
        out_specs=INSIDE,
        compiler_params=PARAMS,
        cost_estimate=cost(2 * (n + 1) * PIECE * D),
    )(parts, after)


def pair_kernel(own, far, _, out):
    c = lax.axis_index(S)
    for core in range(2):

        @pl.when(c == core)
        def _():
            for i in range(3):
                out[i, core] = own[i]
                out[i, 1 - core] = far[i]


def paired(own, far, after):
    return pl.pallas_call(
        pair_kernel,
        out_shape=jax.ShapeDtypeStruct((3, 2, PIECE, D), BF),
        in_specs=[INSIDE] * 2 + [ANYWHERE],
        out_specs=INSIDE,
        compiler_params=PARAMS,
        cost_estimate=cost(24 * PIECE * D),
    )(own, far, after)


def chosen(block, mine, other, act):
    c = lax.axis_index(S)

    @pl.when(c == block)
    def _():
        act(mine)

    @pl.when(c != block)
    def _():
        act(other)


def arrays_of(kind):
    return 2 if kind == 0 else 1


def extract_kernel(items, *refs):
    out, sems = refs[-2:]
    c, z, r = place()
    unit = c * 2 + r // 2
    at = 0
    for i, (block, kind) in enumerate(items):
        n = arrays_of(kind)
        mine, other = refs[at : at + n], refs[at + n : at + 2 * n]
        at += 2 * n

        def copy(source):
            for j in range(NZ):
                pltpu.make_async_copy(source, out.at[j, i], sems.at[j, i]).start()

        def act(source):
            if kind == 2:
                copy(source[0].at[pl.ds((c * 4 + r) * PIECE, PIECE), :])
                return
            height = pl.ds(lax.rem(r, 2) * PIECE, PIECE)

            def take(ref, index):
                cols = pl.ds(pl.multiple_of(index * D, D), D)
                copy(ref.at[height, cols])

            if kind == 1:
                take(source[0], unit)
                return

            @pl.when(unit == 3)
            def _():
                take(source[1], 0)

            @pl.when(unit != 3)
            def _():
                take(source[0], unit)

        chosen(block, mine, other, act)
    for i in range(len(items)):
        for j in range(NZ):
            pltpu.make_async_copy(out.at[j, i], out.at[j, i], sems.at[j, i]).wait()


def extract(items, mine, other, after):
    n = len(items)
    operands = []
    for _, kind in items:
        operands += [*mine[kind], *other[kind]]
    return pl.pallas_call(
        functools.partial(extract_kernel, items),
        out_shape=jax.ShapeDtypeStruct((NZ, n, PIECE, D), BF),
        in_specs=[ANYWHERE] * (len(operands) + 1),
        out_specs=INSIDE,
        scratch_shapes=[pltpu.SemaphoreType.DMA((NZ, n))],
        compiler_params=PARAMS,
        cost_estimate=cost(4 * n * PIECE * D),
    )(*operands, after)


def weight_copies(block, kind, index, mine, other, own, far, out, sems):
    n = arrays_of(kind)
    c, z, r = place()
    copies = []
    height = D if kind == 2 else ROWS
    rows = pl.ds(z * height, height)
    if kind == 0:
        targets = (out.at[rows, pl.ds(0, 3 * D)], out.at[rows, pl.ds(3 * D, D)])
    else:
        targets = (out.at[rows, :],)

    def act(source):
        for i in range(n):
            pltpu.make_async_copy(source[i], targets[i], sems.at[i]).start()

    chosen(block, mine, other, act)
    for side, group in ((0, own), (1, far)):
        core = c if side == 0 else 1 - c
        for m in range(4):
            low = lax.rem(r + m, 2)
            high = lax.rem(r // 2 + m // 2, 2)
            for k in SHARDS:
                zp = lax.rem(z + NZ - k, NZ)
                if kind == 2:
                    row = zp * D + core * (D // 2) + (high * 2 + low) * PIECE
                    spot = out.at[pl.ds(row, PIECE), :]
                else:
                    row = zp * ROWS + low * PIECE
                    col = pl.multiple_of((core * 2 + high) * D, D)
                    spot = out.at[pl.ds(row, PIECE), pl.ds(col, D)]
                if m < 3:
                    piece = group[m].at[index, k - 1]
                elif own[0].shape[0] == 2:
                    piece = group[3 + index].at[0, k - 1]
                elif k == 1:
                    piece = group[3].at[0, 0]
                else:
                    piece = group[4].at[0, k - 2]
                sem = sems.at[2 + (side * 4 + m) * 3 + k - 1]
                copies.append(pltpu.make_async_copy(piece, spot, sem))
    for copy in copies:
        copy.start()

    def wait():
        for i in range(n):
            pltpu.make_async_copy(mine[i], targets[i], sems.at[i]).wait()
        for copy in copies:
            copy.wait()

    return wait


GROUPS = (((0, 0),), ((0, 1), (0, 2)), ((1, 0),), ((1, 1), (1, 2)))


class Gatherer:
    def __init__(self, mine, other, after):
        self.mine = mine
        self.other = other
        self.after = after
        self.state = {}

    def extract(self, g):
        self.after = extract(GROUPS[g], self.mine, self.other, self.after)
        self.state[g] = trade(self.after)

    def stack(self, g):
        p0 = stacked(self.state[g], self.after)
        self.after = p0
        self.state[g] = p0, cross(p0, 1), cross(p0, 2), swap(p0)

    def onward(self, g):
        p0, p1, p2, f0 = self.state[g]
        p1, p2 = fence((p1, p2), self.after)
        self.after = p1
        part = (p2[:1], p1[1:]) if len(GROUPS[g]) == 2 else (p2[:, :1], p1[:, 1:])
        p3 = cross(part[0], 1), cross(part[1], 2)
        self.state[g] = (p0, p1, p2), p3, (f0, swap(p1), swap(p2))

    def share(self, g):
        own, p3, far = self.state[g]
        p3 = fence(p3, self.after)
        self.after = p3[0]
        self.state[g] = own + tuple(p3), far + tuple(swap(p) for p in p3)

    def operands(self, g):
        own, far = self.state[g]
        shards = []
        for _, kind in GROUPS[g]:
            shards += [*self.mine[kind], *self.other[kind]]
        return (*own, *far, *shards, self.after)


def tdot(a, b):
    return lax.dot_general(a, b, (((0,), (0,)), ((), ())), preferred_element_type=F32)


def wgrad_kernel(kind, *refs):
    n = 4
    ins = refs[:n]
    keep_x, send_x, keep_y, send_y, acc = refs[n + 1 :]
    c, z, r = place()
    for g in range(2):
        u = lax.rem(g + r // 2, 2)
        if kind == 2:
            lo, lx, ro, rx = ins
            for zp in range(NZ):
                rows = pl.ds(pl.multiple_of(u * ROWS, ROWS), ROWS)
                acc[zp * ROWS : (zp + 1) * ROWS, :] = jnp.dot(
                    lo[zp, c, rows, :], ro[...], preferred_element_type=F32
                ) + jnp.dot(lx[zp, rows, :], rx[...], preferred_element_type=F32)
        else:
            ro, rx = ins[-2:]
            mine = pl.ds(pl.multiple_of(c * HALF + u * D, D), D)
            other = pl.ds(pl.multiple_of(u * D, D), D)

            def product(lo, lx):
                acc[...] = tdot(lo[...], ro[:, mine]) + tdot(lx[...], rx[:, other])

            if kind == 1:
                product(ins[0], ins[1])
            else:

                @pl.when(c * u == 0)
                def _():
                    product(ins[0].at[0], ins[1].at[0])

                @pl.when(c * u == 1)
                def _():
                    product(ins[0].at[1], ins[1].at[1])

        for par in range(2):

            @pl.when(lax.rem(r, 2) == par)
            def _():
                for zp in range(NZ):
                    for h in range(2):
                        start = (zp * 2 + h) * PIECE
                        piece = acc[start : start + PIECE, :].astype(BF)
                        low = h ^ par
                        if zp < 2:
                            (send_x if low else keep_x)[g, zp] = piece
                        else:
                            (send_y if g else keep_y)[low, zp - 2] = piece


def wgrad(kind, operands, after):
    part = jax.ShapeDtypeStruct((2, 2, PIECE, D), BF)
    return pl.pallas_call(
        functools.partial(wgrad_kernel, kind),
        out_shape=(part,) * 4,
        in_specs=[INSIDE] * len(operands) + [ANYWHERE],
        out_specs=(INSIDE,) * 4,
        scratch_shapes=[pltpu.VMEM((D, D), F32)],
        compiler_params=PARAMS,
        cost_estimate=cost(2 * D * HALF + 6 * 512 * D, 2 * 512 * D * HALF),
    )(*operands, after)


def finish_kernel(block, kind, n, *refs):
    pieces = refs[:5]
    acc, sems = refs[-2:]
    outs = refs[-2 - n : -2]
    c, z, r = place()

    @pl.when(c == block)
    def _():
        for core in range(2):
            for m in range(4):
                low = lax.rem(r + m, 2)
                high = lax.rem(r // 2 + m // 2, 2)
                if m < 3:
                    piece = pieces[m][kind, core]
                else:
                    flat = kind * 2 + core
                    piece = pieces[3][flat] if flat < 3 else pieces[4][flat - 3]
                piece = piece.astype(F32)
                if kind == 2:
                    row = pl.multiple_of(core * (D // 2) + (high * 2 + low) * PIECE, PIECE)
                    acc[pl.ds(row, PIECE), :] = piece
                else:
                    row = pl.multiple_of(low * PIECE, PIECE)
                    col = pl.multiple_of((core * 2 + high) * D, D)
                    acc[pl.ds(row, PIECE), pl.ds(col, D)] = piece
        if n == 2:
            parts = (acc.at[:, pl.ds(0, 3 * D)], acc.at[:, pl.ds(3 * D, D)])
        else:
            parts = (acc,)
        copies = [pltpu.make_async_copy(parts[i], outs[i], sems.at[i]) for i in range(n)]
        for copy in copies:
            copy.start()
        for copy in copies:
            copy.wait()


def finish(block, kind, pieces, before, after):
    if kind == 0:
        shapes = ((ROWS, 3 * D), (ROWS, D))
    else:
        shapes = ((D, D),) if kind == 2 else ((ROWS, FF),)
    n = len(shapes)
    return pl.pallas_call(
        functools.partial(finish_kernel, block, kind, n),
        out_shape=tuple(jax.ShapeDtypeStruct(s, F32) for s in shapes),
        in_specs=[INSIDE] * 5 + [ANYWHERE] * (1 + len(before)),
        out_specs=(ANYWHERE,) * n,
        scratch_shapes=[
            pltpu.VMEM((D, D) if kind == 2 else (ROWS, FF), F32),
            pltpu.SemaphoreType.DMA((2,)),
        ],
        input_output_aliases={6 + i: i for i in range(len(before))},
        compiler_params=PARAMS,
        cost_estimate=cost(8 * ROWS * FF),
    )(*pieces, after, *before)


def on_core(value, bit, core):
    return move(value, lambda s, z, r: (s, z, r ^ bit) if s == core else None)


class Reducer:
    def __init__(self, after):
        self.after = after
        self.items = []
        self.state = []
        self.own = {}
        self.ready = {}
        self.results = {0: (), 1: (), 2: ()}

    def begin(self, block, kind, operands):
        keep_x, send_x, keep_y, send_y = wgrad(kind, operands, self.after)
        self.after = keep_x
        self.items.append((block, kind))
        self.state.append(((keep_x, keep_y), (cross(send_x, 1), cross(send_y, 2))))

    def first(self, i):
        xk, xs, yk, ys = plus(*self.state[i], self.after)
        self.after = xk
        self.state[i] = (xk, yk), (cross(xs, 2), cross(ys, 1))

    def second(self, i):
        f = merged(*self.state[i], self.after)
        self.after = f
        self.state[i] = trade(f)

    def third(self, i):
        v = summed(self.state[i], self.after)
        bit = 4
        while bit < lax.axis_size(R):
            v = summed(jnp.stack([v, cross(v, bit)]), v)
            bit *= 2
        self.after = v
        self.own[self.items[i]] = v

    def unite(self, block):
        own = joined([self.own[block, kind] for kind in range(3)], self.after)
        self.after = own
        self.ready[block] = own, to_core(own, block)

    def spread(self, block):
        p0 = paired(*self.ready[block], self.after)
        self.after = p0
        self.ready[block] = p0, on_core(p0, 1, block), on_core(p0, 2, block)

    def spread_on(self, block):
        p0, p1, p2 = self.ready[block]
        p1, p2 = fence((p1, p2), self.after)
        self.after = p1
        flat1, flat2 = p1.reshape(6, PIECE, D), p2.reshape(6, PIECE, D)
        pa, pb = on_core(flat2[:3], 1, block), on_core(flat1[3:], 2, block)
        self.ready[block] = p0, p1, p2, pa, pb

    def finish(self, block):
        for kind in range(3):
            out = finish(block, kind, self.ready[block], self.results[kind], self.after)
            self.results[kind] = out
            self.after = out[0]


def standard(v):
    mean = jnp.mean(v, axis=-1, keepdims=True)
    centred = v - mean
    rstd = lax.rsqrt(jnp.mean(centred * centred, axis=-1, keepdims=True) + 1e-06)
    return centred * rstd, rstd


def mm(a, b):
    return jnp.dot(a, b, preferred_element_type=F32)


def mmt(a, b):
    return lax.dot_general(a, b, (((1,), (1,)), ((), ())), preferred_element_type=F32)


def head_cols(h, base=0):
    return slice(base + h * HEAD_DIM, base + (h + 1) * HEAD_DIM)


def softmax_of(q, k):
    scores = mmt(q, k)
    e = jnp.exp(scores - jnp.max(scores, axis=-1, keepdims=True))
    return e / jnp.sum(e, axis=-1, keepdims=True)


def shape_of(dtype, *dims):
    return jax.ShapeDtypeStruct(dims, dtype)


def row(ref, i):
    return ref[i : i + 1, :]


def attend_kernel(block, *refs):
    x, ada, qv_bias, proj_bias = refs[:4]
    own, far, mine, other = refs[4:9], refs[9:14], refs[14:16], refs[16:18]
    w_out, sides, q, k, v, attended, mid, mlp_in, w, sems = refs[19:]
    attn_in, mixed = sides.at[0], sides.at[1]
    wait = weight_copies(block, 0, 0, mine, other, own, far, w, sems)
    xf = x[...].astype(F32)
    n1, _ = standard(xf)
    attn_in[...] = (n1 * (1.0 + row(ada, 1)) + row(ada, 0)).astype(BF)
    wait()
    keep = pltpu.make_async_copy(w, w_out, sems.at[26])
    keep.start()
    q[...] = ((mm(attn_in[...], w[:, :D]) + qv_bias[:, :D]) * HEAD_DIM**-0.5).astype(BF)
    k[...] = mm(attn_in[...], w[:, D : 2 * D]).astype(BF)
    v[...] = (mm(attn_in[...], w[:, 2 * D : 3 * D]) + qv_bias[:, D:]).astype(BF)
    for h in range(HEADS):
        cols = head_cols(h)
        probs = softmax_of(q[:, cols], k[:, cols]).astype(BF)
        mixed[:, cols] = mm(probs, v[:, cols]).astype(BF)
    attended[...] = mm(mixed[...], w[:, 3 * D :]) + proj_bias[...]
    mid[...] = x[...].astype(F32) + row(ada, 2) * attended[...]
    n2, _ = standard(mid[...])
    mlp_in[...] = (n2 * (1.0 + row(ada, 4)) + row(ada, 3)).astype(BF)
    keep.wait()


def attend(block, x, ada, biases, gathered):
    t = x.shape[0]
    low = shape_of(BF, t, D)
    high = shape_of(F32, t, D)
    return pl.pallas_call(
        functools.partial(attend_kernel, block),
        out_shape=(shape_of(BF, D, FF), shape_of(BF, 2, t, D), low, low, low, high, high, low),
        in_specs=[INSIDE] * 4 + [ANYWHERE] * 15,
        out_specs=(ANYWHERE,) + (INSIDE,) * 7,
        scratch_shapes=[pltpu.VMEM((D, FF), BF), pltpu.SemaphoreType.DMA((27,))],
        compiler_params=PARAMS,
        cost_estimate=cost(4 * D * FF, 2 * t * D * FF),
    )(x, ada, biases[0], biases[1], *gathered)


def mlp_kernel(block, *refs):
    mid, mlp_in, ada, up_bias, down_bias = refs[:5]
    own, far = refs[5:10], refs[10:15]
    wu_out, wd_out, hidden, act_t, branch, y, wu, wd, act, sems_u, sems_d = refs[20:]
    wait_u = weight_copies(block, 1, 0, refs[15:16], refs[16:17], own, far, wu, sems_u)
    wait_d = weight_copies(block, 2, 1, refs[17:18], refs[18:19], own, far, wd, sems_d)
    wait_u()
    keep_u = pltpu.make_async_copy(wu, wu_out, sems_u.at[26])
    keep_u.start()
    for j in range(4):
        cols = slice(j * D, (j + 1) * D)
        hid = mm(mlp_in[...], wu[:, cols]) + up_bias[:, cols]
        hidden[:, cols] = hid
        part = jax.nn.gelu(hid, approximate=True)
        act[:, cols] = part.astype(BF)
        act_t[cols, :] = part.T.astype(BF)
    wait_d()
    keep_d = pltpu.make_async_copy(wd, wd_out, sems_d.at[26])
    keep_d.start()
    branch[...] = mm(act[...], wd[...]) + down_bias[...]
    y[...] = (mid[...] + row(ada, 5) * branch[...]).astype(BF)
    keep_u.wait()
    keep_d.wait()


def mlp(block, mid, mlp_in, ada, biases, gathered):
    t = mid.shape[0]
    return pl.pallas_call(
        functools.partial(mlp_kernel, block),
        out_shape=(
            shape_of(BF, D, FF),
            shape_of(BF, FF, D),
            shape_of(F32, t, FF),
            shape_of(BF, FF, t),
            shape_of(F32, t, D),
            shape_of(BF, t, D),
        ),
        in_specs=[INSIDE] * 5 + [ANYWHERE] * 15,
        out_specs=(ANYWHERE,) * 2 + (INSIDE,) * 4,
        scratch_shapes=[
            pltpu.VMEM((D, FF), BF),
            pltpu.VMEM((FF, D), BF),
            pltpu.VMEM((t, FF), BF),
            pltpu.SemaphoreType.DMA((27,)),
            pltpu.SemaphoreType.DMA((27,)),
        ],
        compiler_params=PARAMS,
        cost_estimate=cost(8 * D * FF, 4 * t * D * FF),
    )(mid, mlp_in, ada, biases[2], biases[3], *gathered)


def column_sum(v):
    return jnp.sum(v, axis=0, keepdims=True)


def norm_back(g, n, rstd):
    return rstd * (
        g - jnp.mean(g, axis=-1, keepdims=True) - n * jnp.mean(g * n, axis=-1, keepdims=True)
    )


def gelu_slope(v):
    c = math.sqrt(2.0 / math.pi)
    t = jnp.tanh(c * (v + 0.044715 * v * v * v))
    return 0.5 * (1.0 + t) + 0.5 * v * (1.0 - t * t) * (c * (1.0 + 3.0 * 0.044715 * v * v))


def mlp_back_kernel(*refs):
    grad, d_branch, ada, mid, attended, hidden, branch, wu_in, wd_in = refs[:9]
    d_hidden, d_mid, d_att, stats, hidden_sum, wu, wd, acc, sems = refs[10:]
    copies = []
    for j in range(4):
        part = slice(j * D, (j + 1) * D)
        down = pltpu.make_async_copy(wd_in.at[part, :], wd.at[part, :], sems.at[2 * j])
        up = pltpu.make_async_copy(wu_in.at[:, part], wu.at[:, part], sems.at[2 * j + 1])
        copies.append((down, up))
    for down, up in copies:
        down.start()
        up.start()
    stats[2:3, :] = column_sum(grad[...].astype(F32) * branch[...])
    stats[4:5, :] = column_sum(d_branch[...].astype(F32))
    for j in range(4):
        part = slice(j * D, (j + 1) * D)
        copies[j][0].wait()
        d_act = mmt(d_branch[...], wd[part, :])
        d_hid = (d_act * gelu_slope(hidden[:, part])).astype(BF)
        d_hidden[:, part] = d_hid
        hidden_sum[:, part] = column_sum(d_hid.astype(F32))
        copies[j][1].wait()
        product = mmt(d_hidden[:, part], wu[:, part])
        if j == 0:
            acc[...] = product
        else:
            acc[...] += product
    n2, r2 = standard(mid[...])
    stats[0:1, :] = column_sum(acc[...])
    stats[1:2, :] = column_sum(acc[...] * n2)
    whole = grad[...].astype(F32) + norm_back(acc[...] * (1.0 + row(ada, 4)), n2, r2)
    d_mid[...] = whole
    d_att[...] = (row(ada, 2) * whole).astype(BF)
    stats[3:4, :] = column_sum(whole * attended[...])
    stats[5:6, :] = column_sum(d_att[...].astype(F32))


def mlp_back(grad, d_branch, ada, mid, attended, hidden, branch, wu, wd, after):
    t = grad.shape[0]
    return pl.pallas_call(
        mlp_back_kernel,
        out_shape=(
            shape_of(BF, t, FF),
            shape_of(F32, t, D),
            shape_of(BF, t, D),
            shape_of(F32, 8, D),
            shape_of(F32, 1, FF),
        ),
        in_specs=[INSIDE] * 7 + [ANYWHERE] * 3,
        out_specs=(INSIDE,) * 5,
        scratch_shapes=[
            pltpu.VMEM((D, FF), BF),
            pltpu.VMEM((FF, D), BF),
            pltpu.VMEM((t, D), F32),
            pltpu.SemaphoreType.DMA((8,)),
        ],
        compiler_params=PARAMS,
        cost_estimate=cost(5 * D * FF, 4 * t * D * FF),
    )(grad, d_branch, ada, mid, attended, hidden, branch, wu, wd, after)


def attend_back_kernel(*refs):
    x, d_mid, d_att, ada, q_ref, k_ref, v_ref, w_in = refs[:8]
    out, d_x, d_x_low, stats, w, mixed, sem = refs[9:]
    copies = [
        pltpu.make_async_copy(w_in.at[:, 3 * D :], w.at[:, 3 * D :], sem.at[0]),
        pltpu.make_async_copy(w_in.at[:, : 3 * D], w.at[:, : 3 * D], sem.at[1]),
    ]
    for copy in copies:
        copy.start()
    copies[0].wait()
    mixed[...] = mmt(d_att[...], w[:, 3 * D :]).astype(BF)
    for h in range(HEADS):
        cols = head_cols(h)
        q, k, v, dm = (ref[:, cols] for ref in (q_ref, k_ref, v_ref, mixed))
        soft = softmax_of(q, k)
        d_probs = mmt(dm, v)
        inner = jnp.sum(d_probs * soft, axis=-1, keepdims=True)
        d_s = (soft * (d_probs - inner)).astype(BF)
        out[:, cols] = (mm(d_s, k) * HEAD_DIM**-0.5).astype(BF)
        out[:, head_cols(h, D)] = tdot(d_s, q).astype(BF)
        out[:, head_cols(h, 2 * D)] = tdot(soft.astype(BF), dm).astype(BF)
    out[:, 3 * D :] = d_att[...]
    stats[2:3, :] = column_sum(out[:, :D].astype(F32))
    stats[3:4, :] = column_sum(out[:, 2 * D : 3 * D].astype(F32))
    copies[1].wait()
    d_in = mmt(out[:, :D], w[:, :D])
    d_in += mmt(out[:, D : 2 * D], w[:, D : 2 * D])
    d_in += mmt(out[:, 2 * D : 3 * D], w[:, 2 * D : 3 * D])
    n1, r1 = standard(x[...].astype(F32))
    stats[0:1, :] = column_sum(d_in)
    stats[1:2, :] = column_sum(d_in * n1)
    whole = d_mid[...] + norm_back(d_in * (1.0 + row(ada, 1)), n1, r1)
    d_x[...] = whole
    d_x_low[...] = whole.astype(BF)


def attend_back(x, d_mid, d_att, ada, q, k, v, wa, after):
    t = x.shape[0]
    return pl.pallas_call(
        attend_back_kernel,
        out_shape=(
            shape_of(BF, t, FF),
            shape_of(F32, t, D),
            shape_of(BF, t, D),
            shape_of(F32, 8, D),
        ),
        in_specs=[INSIDE] * 7 + [ANYWHERE] * 2,
        out_specs=(INSIDE,) * 4,
        scratch_shapes=[
            pltpu.VMEM((D, FF), BF),
            pltpu.VMEM((t, D), BF),
            pltpu.SemaphoreType.DMA((2,)),
        ],
        compiler_params=PARAMS,
        cost_estimate=cost(3 * D * FF, 2 * t * D * FF),
    )(x, d_mid, d_att, ada, q, k, v, wa, after)


def far_half(right):
    c = lax.axis_index(S)
    return swap(lax.dynamic_slice_in_dim(right, (1 - c) * HALF, HALF, 1))


def far_rows(act_t):
    c = lax.axis_index(S)
    return swap(lax.dynamic_index_in_dim(act_t, 1 - c, 1, keepdims=False))


def rows_sum(v):
    return jnp.sum(v.astype(F32), axis=0)


def embed_time(steps):
    half = D // 2
    freq = jnp.exp(-math.log(10000.0) * jnp.arange(half, dtype=F32) / half)
    angles = steps.astype(F32)[:, None] * freq[None, :]
    return jnp.concatenate([jnp.cos(angles), jnp.sin(angles)], axis=-1)


def everywhere(value):
    nr = lax.axis_size(R)
    out = along_z(value)[None]
    bit = 1
    while bit < nr:
        out = jnp.concatenate([out, cross(out, bit)])
        bit *= 2
    return jnp.take(out, lax.axis_index(R) ^ jnp.arange(nr), axis=0)


def total(value):
    value = value + swap(value)
    for bit in (1, 2):
        value = value + move(value, lambda s, z, r: (s, z ^ bit, r))
    bit = 1
    while bit < lax.axis_size(R):
        value = value + cross(value, bit)
        bit *= 2
    return value


def per_device(
    inputs,
    cotangent,
    timesteps,
    labels,
    class_table,
    qkv_weight,
    qv_bias,
    proj_weight,
    proj_bias,
    up_weight,
    up_bias,
    down_weight,
    down_bias,
    ada_weight,
    ada_bias,
):
    c = lax.axis_index(S)
    z = lax.axis_index(Z)
    is_first = c == 0

    ids = jnp.concatenate([timesteps, labels], axis=1)
    vectors = [v[0].astype(F32) for v in (qv_bias, proj_bias, up_bias, down_bias, ada_bias)]
    small = along_z(jnp.concatenate(vectors + [ids.reshape(-1).astype(F32)]))
    ids_z = small[:, -4:].astype(jnp.int32).reshape(NZ, 2, 2)
    vec_mine = small[:, :-4]
    vec_other = swap(vec_mine)

    def cond_of(steps, classes):
        return embed_time(steps) + jnp.take(class_table, classes, axis=0).astype(F32)

    cond_z = cond_of(ids_z[..., 0].reshape(-1), ids_z[..., 1].reshape(-1))
    silu_z = jax.nn.silu(cond_z).astype(BF)
    rows_z = lax.dynamic_slice_in_dim(silu_z, z * ROWS, ROWS, 1)
    partial = mm(rows_z, ada_weight[0]).reshape(NZ, 2, -1)
    ada_sum = jnp.sum(trade(partial), axis=0)
    lengths = (qv_bias.shape[1], proj_bias.shape[1], up_bias.shape[1], down_bias.shape[1], ada_bias.shape[1])

    def split_vectors(vec):
        out = []
        at = 0
        for n in lengths:
            out.append(vec[:, at : at + n].reshape(-1))
            at += n
        return out

    mine_split = split_vectors(vec_mine)
    other_split = split_vectors(vec_other)
    ada_sum = ada_sum + mine_split[4][None]
    ada_keep = lax.dynamic_index_in_dim(ada_sum, c, 0, keepdims=False)
    ada_got = swap(lax.dynamic_index_in_dim(ada_sum, 1 - c, 0, keepdims=False))
    adas = []
    biases = []
    for block in range(2):
        here = c == block
        adas.append(jnp.where(here, ada_keep, ada_got).reshape(6, D))
        biases.append(
            [jnp.where(here, a, b)[None] for a, b in zip(mine_split[:4], other_split[:4])]
        )

    mine = ((qkv_weight[0], proj_weight[0]), (up_weight[0],), (down_weight[0],))
    other = tuple(tuple(swap(w) for w in group) for group in mine)
    gatherer = Gatherer(mine, other, qkv_weight[0])
    x = lax.dynamic_index_in_dim(inputs, c, 0, keepdims=False)[0]
    cot = lax.dynamic_index_in_dim(cotangent, c, 0, keepdims=False)[0]
    kept = []
    kept_mlp = []

    def run_attend(block, value):
        got = attend(block, value, adas[block], biases[block], gatherer.operands(2 * block))
        gatherer.after = got[-1]
        kept.append(got)

    def run_mlp(block):
        mid, mlp_in = kept[block][-2:]
        got = mlp(block, mid, mlp_in, adas[block], biases[block], gatherer.operands(2 * block + 1))
        gatherer.after = got[-1]
        act_t = got[3].reshape(NZ, 2, D // 2, -1)
        kept_mlp.append(got[:3] + (act_t,) + got[4:] + (far_rows(act_t), swap(mlp_in)))

    gatherer.extract(0)
    gatherer.stack(0)
    gatherer.extract(1)
    gatherer.onward(0)
    gatherer.share(0)
    run_attend(0, x)
    gatherer.stack(1)
    gatherer.extract(2)
    gatherer.stack(2)
    gatherer.extract(3)
    gatherer.onward(1)
    gatherer.onward(2)
    gatherer.share(1)
    run_mlp(0)
    y0 = kept_mlp[0][5]
    gatherer.share(2)
    gatherer.stack(3)
    run_attend(1, y0)
    gatherer.onward(3)
    gatherer.share(3)
    run_mlp(1)
    y1 = kept_mlp[1][5]

    reducer = Reducer(y1)

    def run_mlp_back(block, grad):
        ada = adas[block]
        d_branch = (ada[5:] * grad.astype(F32)).astype(BF)
        far_branch = swap(d_branch)
        attended, mid, mlp_in = kept[block][-3:]
        wu, wd, hidden, act_t, branch, _, far_act, far_in = kept_mlp[block]
        got = mlp_back(grad, d_branch, ada, mid, attended, hidden, branch, wu, wd, reducer.after)
        d_hidden = got[0]
        reducer.after = d_hidden
        far_hidden = far_half(d_hidden)
        reducer.begin(block, 2, (act_t, far_act, d_branch, far_branch))
        reducer.begin(block, 1, (mlp_in, far_in, d_hidden, far_hidden))
        return got

    def run_attend_back(block, value, back):
        wa, sides, q, k, v = kept[block][:5]
        _, d_mid, d_att, stats_m, hidden_sum = back
        far = swap(sides)
        d_all, d_x, d_x_low, stats_a = attend_back(
            value, d_mid, d_att, adas[block], q, k, v, wa, reducer.after
        )
        reducer.after = d_x_low
        d_ada = jnp.concatenate(
            [stats_a[0], stats_a[1], stats_m[3], stats_m[0], stats_m[1], stats_m[2]]
        ).astype(BF)
        sums = jnp.concatenate([stats_a[2], stats_a[3], stats_m[5], hidden_sum[0], stats_m[4]])
        operands = (sides, far, d_all, far_half(d_all))
        return d_x, d_x_low, d_ada, sums, operands

    back1 = run_mlp_back(1, cot)
    _, dx1, dada1, sums1, operands1 = run_attend_back(1, y0, back1)
    reducer.first(0)
    reducer.begin(1, 0, operands1)
    back0 = run_mlp_back(0, dx1)
    reducer.first(1)
    reducer.second(0)
    dx0, _, dada0, sums0, operands0 = run_attend_back(0, x, back0)
    reducer.first(2)
    reducer.begin(0, 0, operands0)
    reducer.second(1)
    reducer.third(0)
    reducer.first(3)
    reducer.second(2)
    reducer.third(1)
    reducer.first(4)
    reducer.second(3)
    reducer.third(2)
    reducer.unite(1)
    reducer.first(5)
    reducer.spread(1)
    reducer.second(4)
    reducer.third(3)
    reducer.spread_on(1)
    reducer.second(5)
    reducer.third(4)
    reducer.finish(1)
    reducer.third(5)
    reducer.unite(0)
    reducer.spread(0)
    reducer.spread_on(0)
    reducer.finish(0)
    (qkv_grad, proj_grad), (up_grad,), (down_grad,) = (reducer.results[k] for k in range(3))

    def both_micros(v0, v1):
        keep = jnp.where(is_first, v0, v1)
        got = swap(jnp.where(is_first, v1, v0))
        return jnp.stack([jnp.where(is_first, keep, got), jnp.where(is_first, got, keep)])

    block_outputs = both_micros(y0, y1)[None, :, None]
    input_grads = both_micros(dx0, dx1.astype(F32))[None, :, None]

    sums = total(jnp.stack([sums0, sums1]))
    sums = lax.dynamic_index_in_dim(sums, c, 0, keepdims=False)

    def own_slice(vec):
        n = vec.shape[0] // NZ
        return lax.dynamic_slice_in_dim(vec, z * n, n, 0)[None]

    qv_bias_grad = own_slice(sums[: 2 * D])
    proj_bias_grad = own_slice(sums[2 * D : 3 * D])
    up_bias_grad = own_slice(sums[3 * D : 3 * D + FF])
    down_bias_grad = own_slice(sums[3 * D + FF :])

    ids_all = ids_z[None]
    bit = 1
    while bit < lax.axis_size(R):
        ids_all = jnp.concatenate([ids_all, cross(ids_all, bit)])
        bit *= 2
    ids_all = jnp.take(ids_all, lax.axis_index(R) ^ jnp.arange(lax.axis_size(R)), axis=0)
    ids_all = ids_all.reshape(-1, 2)
    cond_all = cond_of(ids_all[:, 0], ids_all[:, 1])
    labels_all = ids_all[:, 1]
    dada_own = everywhere(both_micros(dada0, dada1)).reshape(-1, 6 * D)
    cond_rows = lax.dynamic_slice_in_dim(cond_all, z * ROWS, ROWS, 1)
    silu_rows = jax.nn.silu(cond_rows).astype(BF)
    ada_grad = lax.dot_general(
        silu_rows, dada_own, (((0,), (0,)), ((), ())), preferred_element_type=F32
    )
    ada_bias_grad = own_slice(rows_sum(dada_own))
    d_silu = mmt(dada_own, ada_weight[0])
    _, silu_back = jax.vjp(jax.nn.silu, cond_rows)
    d_cond = silu_back(d_silu)[0]
    d_cond = d_cond + swap(d_cond)
    d_cond_all = along_z(d_cond).transpose(1, 0, 2).reshape(-1, D)
    row_count = class_table.shape[0] // (2 * NZ)
    row_ids = (c * NZ + z) * row_count + jnp.arange(row_count, dtype=jnp.int32)
    owner = (row_ids[:, None] == labels_all[None, :]).astype(F32)
    table_grad = jnp.dot(owner, d_cond_all, precision=lax.Precision.HIGHEST)

    return (
        block_outputs,
        input_grads,
        table_grad,
        qkv_grad[None],
        qv_bias_grad,
        proj_grad[None],
        proj_bias_grad,
        up_grad[None],
        up_bias_grad,
        down_grad[None],
        down_bias_grad,
        ada_grad[None],
        ada_bias_grad,
    )


def solution(mesh):
    rows = P(None, (Z, R), None, None)
    matrix = P(S, Z, None)
    vector = P(S, Z)
    pair = P(None, (Z, R))
    in_specs = (rows, rows, pair, pair, P()) + (matrix, vector) * 5
    acts = P(S, None, (Z, R), None, None)
    out_specs = (acts, acts, P((S, Z), None)) + (matrix, vector) * 5
    return jax.shard_map(
        per_device, mesh=mesh, in_specs=in_specs, out_specs=out_specs, check_vma=False
    )
```

time: 3310 us -> 1020 us (0.31)
  Pallas kernels: 2030 us -> 290 us
  waiting for transfers between devices: 662 us -> 380 us
  matrix products: 131 us -> 13.6 us
  blocking collectives: 107 us -> 0 us
  other arithmetic: 74 us -> 35.4 us
    pallas_call x9 -> x54, Pallas kernels: 1950 us -> 238 us  [the longest x2 46.8 us: mlp(): pl.pallas_call(functools.partial(mlp_kernel, block), out_shape=(shape_of(...]
    ppermute x170 -> x101, waiting for transfers between devices: 564 us -> 293 us  [move(): return lax.ppermute(value, ALL, pairs)]
    all_gather x2 -> x0, blocking collectives: 107 us -> none  [the longest x1 68.5 us: per_device(): lax.all_gather(jnp.stack([dada0, dada1]), ALL, axis=0, tiled=False)]
    psum x1 -> x0, waiting for transfers between devices: 98.5 us -> none  [per_device(): sums = lax.psum(jnp.stack([sums0, sums1]), ALL)]
    all_to_all x0 -> x14, waiting for transfers between devices: none -> 87.3 us  [trade(): return lax.all_to_all(value, Z, split_axis=0, concat_axis=0, tiled=True)]
    ppermute x170 -> x101, starting transfers between devices: 152 us -> 80 us  [move(): return lax.ppermute(value, ALL, pairs)]
    all_to_all x0 -> x14, starting transfers between devices: none -> 66.3 us  [trade(): return lax.all_to_all(value, Z, split_axis=0, concat_axis=0, tiled=True)]
    dot_general x9 -> x1, matrix products: 63.7 us -> 3.5 us  [mm(): return jnp.dot(a, b, preferred_element_type=F32)]
  transfers between devices with their start and end apart: 171 -> 115, of which waited for: 61 -> 43; matrix products, arithmetic and copies ran while one was open for 6% -> 12% of each run, Pallas kernels for 52% -> 22%
where the time goes in v1:
time: 1020 us; the launch traced here: 1010 us
  waiting for transfers between devices  380 us (37%)
  Pallas kernels  290 us (28%)
  starting transfers between devices  146 us (14%)
  local copies, waits for them, and re-layouts  139 us (14%)
  other arithmetic  35.4 us (3%)
  matrix products  13.6 us (1%)
    ppermute x101, waiting for transfers between devices, move(): return lax.ppermute(value, ALL, pairs)  293 us
    all_to_all x14, waiting for transfers between devices, trade(): return lax.all_to_all(value, Z, split_axis=0, concat_axis=0, tiled=True)  87.3 us
    ppermute x101, starting transfers between devices, move(): return lax.ppermute(value, ALL, pairs)  80 us
    unnamed x317, local copies, waits for them, and re-layouts  76.3 us
    all_to_all x14, starting transfers between devices, trade(): return lax.all_to_all(value, Z, split_axis=0, concat_axis=0, tiled=True)  66.3 us
    pallas_call x6, Pallas kernels, wgrad(): pl.pallas_call(functools.partial(wgrad_kernel, kind), out_shape=(part,) *...  51.2 us
    pallas_call x2, Pallas kernels, mlp(): pl.pallas_call(functools.partial(mlp_kernel, block), out_shape=(shape_of(...  46.8 us
    pallas_call x2, Pallas kernels, attend(): pl.pallas_call(functools.partial(attend_kernel, block), out_shape=(shape_...  37.7 us
  transfers between devices with their start and end apart: 115, of which 43 were waited for; matrix products, arithmetic and copies ran while one was open for 12% of the time, Pallas kernels for 22%

profile of v1, /device:TPU:0, one launch (start us, length us, event | category | flops | bytes accessed | tf_op | source)
XLA Modules:
  0.0 1007.0 jit_solution(2859689353089596686)
XLA Ops:
  33.6 25.7 %all-to-all-done.2.every = bf16[4,1,144,1152]{3,2,1,0:T(8,128)(2,1)} async-done(((bf16[4,1,144,1152]{3,2,1,0:T(8,128)(2,1)}), bf16[4,1,144,1152]{3,2,1,0:T(8,128)(2,1)}, u32[]{:S(2)}, u32[]{:S(2)}) %all-to-all-start.2) | async-done | bytes 1327136 | tf_op jit(solution)/shard_map/all_to_all | solution.py:56
  78.0 20.1 %collective-permute-done.4.refs_0_ = bf16[1,3,144,1152]{3,2,1,0:T(8,128)(2,1)} collective-permute-done((bf16[1,3,144,1152]{3,2,1,0:T(8,128)(2,1)S(1)}, bf16[1,3,144,1152]{3,2,1,0:T(8,128)(2,1)}, u32[]{:S(2)}, u32[]{:S(2)}) %collective-permute-start.4) | collective-permute-done | bytes 995360 | tf_op jit(solution)/shard_map/ppermute | solution.py:39
  108.9 15.1 %collective-permute-done.9.refs_1_ = bf16[1,2,144,1152]{3,2,1,0:T(8,128)(2,1)} collective-permute-done((bf16[1,2,144,1152]{3,2,1,0:T(8,128)(2,1)S(1)}, bf16[1,2,144,1152]{3,2,1,0:T(8,128)(2,1)}, u32[]{:S(2)}, u32[]{:S(2)}) %collective-permute-start.9) | collective-permute-done | bytes 663584 | tf_op jit(solution)/shard_map/ppermute | solution.py:39
  129.2 18.9 %shard_map.251 = (bf16[1152,4608]{1,0:T(8,128)(2,1)}, bf16[2,256,1152]{2,1,0:T(8,128)(2,1)}, bf16[256,1152]{1,0:T(8,128)(2,1)S(1)}, bf16[256,1152]{1,0:T(8,128)(...) custom-call(bf16[256,1152]{1,0:T(8,128)(2,1)S(1)} %copy-done.29, ...), custom_call_target="tpu_custom_call" | custom-call | flops 2717908992 | bytes 21233664 | tf_op jit(solution)/shard_map/pallas_call | solution.py:626
  164.4 30.5 %all-to-all-done.4.every = bf16[4,1,144,1152]{3,2,1,0:T(8,128)(2,1)} async-done(((bf16[4,1,144,1152]{3,2,1,0:T(8,128)(2,1)}), bf16[4,1,144,1152]{3,2,1,0:T(8,128)(2,1)}, u32[]{:S(2)}, u32[]{:S(2)}) %all-to-all-start.4) | async-done | bytes 1327136 | tf_op jit(solution)/shard_map/all_to_all | solution.py:56
  214.9 16.5 %collective-permute-done.19.refs_0_ = bf16[1,3,144,1152]{3,2,1,0:T(8,128)(2,1)} collective-permute-done((bf16[1,3,144,1152]{3,2,1,0:T(8,128)(2,1)S(1)}, bf16[1,3,144,1152]{3,2,1,0:T(8,128)(2,1)}, u32[]{:S(2)}, u32[]{:S(2)}) %collective-permute-start.19) | collective-permute-done | bytes 995360 | tf_op jit(solution)/shard_map/ppermute | solution.py:39
  232.4 18.5 %collective-permute-done.17.refs_0_ = bf16[1,3,144,1152]{3,2,1,0:T(8,128)(2,1)} collective-permute-done((bf16[1,3,144,1152]{3,2,1,0:T(8,128)(2,1)}, bf16[1,3,144,1152]{3,2,1,0:T(8,128)(2,1)}, u32[]{:S(2)}, u32[]{:S(2)}) %collective-permute-start.17) | collective-permute-done | bytes 995360 | tf_op jit(solution)/shard_map/ppermute | solution.py:39
  259.3 23.2 %shard_map.259 = (bf16[1152,4608]{1,0:T(8,128)(2,1)}, bf16[4608,1152]{1,0:T(8,128)(2,1)}, f32[256,4608]{1,0:T(8,128)}, bf16[4608,256]{1,0:T(8,128)(2,1)}, f32[25...) custom-call(f32[256,1152]{1,0:T(8,128)} %get-tuple-element.134.refs_0_.refs_3_, bf16[256,1152]{1,0:T(8,128)(2,1)S(1)} %copy-done.51, ...), custom_call_target="tpu_custom_call" | custom-call | flops 5435817984 | bytes 42467328 | tf_op jit(solution)/shard_map/pallas_call | solution.py:664
  298.4 18.8 %shard_map.262 = (bf16[1152,4608]{1,0:T(8,128)(2,1)}, bf16[2,256,1152]{2,1,0:T(8,128)(2,1)}, bf16[256,1152]{1,0:T(8,128)(2,1)S(1)}, bf16[256,1152]{1,0:T(8,128)(...) custom-call(bf16[256,1152]{1,0:T(8,128)(2,1)S(1)} %copy-done.5, ...), custom_call_target="tpu_custom_call" | custom-call | flops 2717908992 | bytes 21233664 | tf_op jit(solution)/shard_map/pallas_call | solution.py:626
  318.9 13.0 %collective-permute-done.33.refs_0_ = bf16[2,3,144,1152]{3,2,1,0:T(8,128)(2,1)} collective-permute-done((bf16[2,3,144,1152]{3,2,1,0:T(8,128)(2,1)}, bf16[2,3,144,1152]{3,2,1,0:T(8,128)(2,1)}, u32[]{:S(2)}, u32[]{:S(2)}) %collective-permute-start.33) | collective-permute-done | bytes 1990688 | tf_op jit(solution)/shard_map/ppermute | solution.py:39
  338.6 17.6 %collective-permute-done.35.refs_0_ = bf16[1,3,144,1152]{3,2,1,0:T(8,128)(2,1)} collective-permute-done((bf16[1,3,144,1152]{3,2,1,0:T(8,128)(2,1)S(1)}, bf16[1,3,144,1152]{3,2,1,0:T(8,128)(2,1)}, u32[]{:S(2)}, u32[]{:S(2)}) %collective-permute-start.35) | collective-permute-done | bytes 995360 | tf_op jit(solution)/shard_map/ppermute | solution.py:39
  363.0 23.6 %shard_map.265 = (bf16[1152,4608]{1,0:T(8,128)(2,1)}, bf16[4608,1152]{1,0:T(8,128)(2,1)}, f32[256,4608]{1,0:T(8,128)}, bf16[4608,256]{1,0:T(8,128)(2,1)}, f32[25...) custom-call(f32[256,1152]{1,0:T(8,128)} %get-tuple-element.145.refs_0_.refs_3_, ...), custom_call_target="tpu_custom_call" | custom-call | flops 5435817984 | bytes 42467328 | tf_op jit(solution)/shard_map/pallas_call | solution.py:664
  389.4 16.8 %shard_map.266 = (bf16[256,4608]{1,0:T(8,128)(2,1)}, f32[256,1152]{1,0:T(8,128)S(1)}, bf16[256,1152]{1,0:T(8,128)(2,1)S(1)}, f32[8,1152]{1,0:T(8,128)S(1)}, f32[1,4608]{1,0:T(1,128)S(1)}) custom-call(bf16[256,1152]{1,0:T(8,128)(2,1)S(1)} %get-tuple-element.363.refs_0_, bf16[256,1152]{1,0:T(8,128)(2,1)S(1)} %get-tuple-element.362.refs_1_.refs_2_, ...), custom_call_target="tpu_custom_call" | custom-call | flops 5435817984 | bytes 26542080 | tf_op jit(solution)/shard_map/pallas_call | solution.py:743
  433.3 18.6 %shard_map.269 = (bf16[256,4608]{1,0:T(8,128)(2,1)}, f32[256,1152]{1,0:T(8,128)}, bf16[256,1152]{1,0:T(8,128)(2,1)S(1)}, f32[8,1152]{1,0:T(8,128)S(1)}) custom-call(bf16[256,1152]{1,0:T(8,128)(2,1)S(1)} %copy-done.5, f32[256,1152]{1,0:T(8,128)} %copy-done.57, bf16[256,1152]{1,0:T(8,128)(2,1)S(1)} %get-tuple-element.158.refs_2_, ...), custom_call_target="tpu_custom_call" | custom-call | flops 2717908992 | bytes 15925248 | tf_op jit(solution)/shard_map/pallas_call | solution.py:803
  470.8 16.7 %shard_map.272 = (bf16[256,4608]{1,0:T(8,128)(2,1)}, f32[256,1152]{1,0:T(8,128)S(1)}, bf16[256,1152]{1,0:T(8,128)(2,1)S(1)}, f32[8,1152]{1,0:T(8,128)S(1)}, f32[1,4608]{1,0:T(1,128)S(1)}) custom-call(bf16[256,1152]{1,0:T(8,128)(2,1)S(1)} %get-tuple-element.167.refs_4_.refs_0_, bf16[256,1152]{1,0:T(8,128)(2,1)} %fusion.4.refs_1_.refs_2_, ...), custom_call_target="tpu_custom_call" | custom-call | flops 5435817984 | bytes 26542080 | tf_op jit(solution)/shard_map/pallas_call | solution.py:743
  542.2 18.7 %shard_map.277 = (bf16[256,4608]{1,0:T(8,128)(2,1)}, f32[256,1152]{1,0:T(8,128)}, bf16[256,1152]{1,0:T(8,128)(2,1)S(1)}, f32[8,1152]{1,0:T(8,128)S(1)}) custom-call(bf16[256,1152]{1,0:T(8,128)(2,1)S(1)} %copy-done.30, f32[256,1152]{1,0:T(8,128)} %copy-done.56, bf16[256,1152]{1,0:T(8,128)(2,1)S(1)} %copy-done.91, f32[6,1152]{1,0:T(8,128)S(1)} %copy-done.59, ...), custom_call_target="tpu_custom_call" | custom-call | flops 2717908992 | bytes 15925248 | tf_op jit(solution)/shard_map/pallas_call | solution.py:803
  593.3 17.1 %collective-permute-done.68.refs_2_ = bf16[2,2,144,1152]{3,2,1,0:T(8,128)(2,1)} collective-permute-done((bf16[2,2,144,1152]{3,2,1,0:T(8,128)(2,1)}, bf16[2,2,144,1152]{3,2,1,0:T(8,128)(2,1)}, u32[]{:S(2)}, u32[]{:S(2)}) %collective-permute-start.68) | collective-permute-done | bytes 1327136 | tf_op jit(solution)/shard_map/ppermute | solution.py:39
  610.9 10.9 %collective-permute-done.69.refs_3_ = bf16[2,2,144,1152]{3,2,1,0:T(8,128)(2,1)S(1)} collective-permute-done((bf16[2,2,144,1152]{3,2,1,0:T(8,128)(2,1)}, bf16[2,2,144,1152]{3,2,1,0:T(8,128)(2,1)S(1)}, u32[]{:S(2)}, u32[]{:S(2)}) %collective-permute-start.69) | collective-permute-done | bytes 1327136 | tf_op jit(solution)/shard_map/ppermute | solution.py:39
  648.5 39.0 %collective-permute-done.60 = s32[1,4,2,2]{1,3,2,0:T(2,128)S(1)} collective-permute-done((s32[1,4,2,2]{1,3,2,0:T(2,128)S(1)}, s32[1,4,2,2]{1,3,2,0:T(2,128)S(1)}, u32[]{:S(2)}, u32[]{:S(2)}) %collective-permute-start.60) | collective-permute-done | bytes 96 | tf_op jit(solution)/shard_map/ppermute | solution.py:39
  730.9 11.2 %collective-permute-done.80.refs_2_ = bf16[2,2,144,1152]{3,2,1,0:T(8,128)(2,1)} collective-permute-done((bf16[2,2,144,1152]{3,2,1,0:T(8,128)(2,1)}, bf16[2,2,144,1152]{3,2,1,0:T(8,128)(2,1)}, u32[]{:S(2)}, u32[]{:S(2)}) %collective-permute-start.80) | collective-permute-done | bytes 1327136 | tf_op jit(solution)/shard_map/ppermute | solution.py:39
  771.7 22.8 %collective-permute-done.70.refs_2_ = bf16[2,2,144,1152]{3,2,1,0:T(8,128)(2,1)S(1)} collective-permute-done((bf16[2,2,144,1152]{3,2,1,0:T(8,128)(2,1)}, bf16[2,2,144,1152]{3,2,1,0:T(8,128)(2,1)S(1)}, u32[]{:S(2)}, u32[]{:S(2)}) %collective-permute-start.70) | collective-permute-done | bytes 1327136 | tf_op jit(solution)/shard_map/ppermute | solution.py:39
  829.1 18.5 %all-to-all-done.13.parts = bf16[4,144,1152]{2,1,0:T(8,128)(2,1)} async-done(((bf16[4,144,1152]{2,1,0:T(8,128)(2,1)}), bf16[4,144,1152]{2,1,0:T(8,128)(2,1)}, u32[]{:S(2)}, u32[]{:S(2)}) %all-to-all-start.13) | async-done | bytes 1327136 | tf_op jit(solution)/shard_map/all_to_all | solution.py:56
  860.3 26.0 %collective-permute-done.98 = f32[2,9216]{1,0:T(2,128)S(1)} collective-permute-done((f32[2,9216]{1,0:T(2,128)S(1)}, f32[2,9216]{1,0:T(2,128)S(1)}, u32[]{:S(2)}, u32[]{:S(2)}) %collective-permute-start.98) | collective-permute-done | bytes 73760 | tf_op jit(solution)/shard_map/ppermute | solution.py:39
  915.3 16.4 %collective-permute-done.91.far = bf16[3,144,1152]{2,1,0:T(8,128)(2,1)S(1)} collective-permute-done((bf16[3,144,1152]{2,1,0:T(8,128)(2,1)S(1)}, bf16[3,144,1152]{2,1,0:T(8,128)(2,1)S(1)}, u32[]{:S(2)}, u32[]{:S(2)}) %collective-permute-start.91) | collective-permute-done | bytes 995360 | tf_op jit(solution)/shard_map/ppermute | solution.py:39
  (733 shorter events, 530.0 us)
Async XLA Ops:
  1.3 64.8 %collective-permute-start.6 = (bf16[288,4608]{1,0:T(8,128)(2,1)}, bf16[288,4608]{1,0:T(8,128)(2,1)}, u32[]{:S(2)}, u32[]{:S(2)}) collective-permute-start(bf16[288,4608]{1,0:T(8,128)(2,1)} %bitcast.108), channel_id=1, source_target_pairs={{0,16},{1,17},{2,18},{3,19},{4,20},{5,21},{6,22},{7,23},{8,24},{9,... | collective-permute-start | bytes 7962632 | tf_op jit(solution)/shard_map/ppermute | solution.py:39
  1.7 64.4 %collective-permute-start.7 = (bf16[1152,1152]{1,0:T(8,128)(2,1)}, bf16[1152,1152]{1,0:T(8,128)(2,1)}, u32[]{:S(2)}, u32[]{:S(2)}) collective-permute-start(bf16[1152,1152]{1,0:T(8,128)(2,1)} %bitcast.113), channel_id=1, source_target_pairs={{0,16},{1,17},{2,18},{3,19},{4,20},{5,21},{6,22},{7,23},{8,24},{9,... | collective-permute-start | bytes 7962632 | tf_op jit(solution)/shard_map/ppermute | solution.py:39
  71.0 79.6 %all-to-all-start.3 = ((bf16[4,2,144,1152]{3,2,1,0:T(8,128)(2,1)}), bf16[4,2,144,1152]{3,2,1,0:T(8,128)(2,1)}, u32[]{:S(2)}, u32[]{:S(2)}) async-start(bf16[4,2,144,1152]{3,2,1,0:T(8,128)(2,1)} %copy-done.1), calls=%async_computation.3 | async-start | bytes 5308416 | tf_op jit(solution)/shard_map/all_to_all | solution.py:56
  162.6 45.8 %collective-permute-start.15 = (bf16[2,3,144,1152]{3,2,1,0:T(8,128)(2,1)}, bf16[2,3,144,1152]{3,2,1,0:T(8,128)(2,1)}, u32[]{:S(2)}, u32[]{:S(2)}) collective-permute-start(bf16[2,3,144,1152]{3,2,1,0:T(8,128)(2,1)} %copy-done.3), channel_id=1, source_target_pairs={{0,1},{1,0},{2,3},{3,2},{4,5},{5,4},{6,7},{7,6},{8,9},{9,8},{10,11... | collective-permute-start | bytes 5971976 | tf_op jit(solution)/shard_map/ppermute | solution.py:39
  163.9 45.5 %collective-permute-start.16 = (bf16[2,3,144,1152]{3,2,1,0:T(8,128)(2,1)}, bf16[2,3,144,1152]{3,2,1,0:T(8,128)(2,1)}, u32[]{:S(2)}, u32[]{:S(2)}) collective-permute-start(bf16[2,3,144,1152]{3,2,1,0:T(8,128)(2,1)} %copy-done.3), channel_id=1, source_target_pairs={{0,2},{1,3},{2,0},{3,1},{4,6},{5,7},{6,4},{7,5},{8,10},{9,11},{10,... | collective-permute-start | bytes 5971976 | tf_op jit(solution)/shard_map/ppermute | solution.py:39
  201.6 81.7 %all-to-all-start.5 = ((bf16[4,2,144,1152]{3,2,1,0:T(8,128)(2,1)}), bf16[4,2,144,1152]{3,2,1,0:T(8,128)(2,1)}, u32[]{:S(2)}, u32[]{:S(2)}) async-start(bf16[4,2,144,1152]{3,2,1,0:T(8,128)(2,1)} %copy-done.2), calls=%async_computation.5 | async-start | bytes 5308416 | tf_op jit(solution)/shard_map/all_to_all | solution.py:56
  207.3 47.0 %collective-permute-start.21 = (bf16[2,3,144,1152]{3,2,1,0:T(8,128)(2,1)}, bf16[2,3,144,1152]{3,2,1,0:T(8,128)(2,1)}, u32[]{:S(2)}, u32[]{:S(2)}) collective-permute-start(bf16[2,3,144,1152]{3,2,1,0:T(8,128)(2,1)} %copy-done.3), channel_id=1, source_target_pairs={{0,16},{1,17},{2,18},{3,19},{4,20},{5,21},{6,22},{7,23},{8,24},{9,... | collective-permute-start | bytes 5971976 | tf_op jit(solution)/shard_map/ppermute | solution.py:39
  286.6 45.3 %collective-permute-start.33 = (bf16[2,3,144,1152]{3,2,1,0:T(8,128)(2,1)}, bf16[2,3,144,1152]{3,2,1,0:T(8,128)(2,1)}, u32[]{:S(2)}, u32[]{:S(2)}) collective-permute-start(bf16[2,3,144,1152]{3,2,1,0:T(8,128)(2,1)} %shard_map.261.refs_18_.refs_5_), channel_id=1, source_target_pairs={{0,1},{1,0},{2,3},{3,2},{4,5},{5,4},{6,7},{7,6},{8,9},{9,8},{10,11... | collective-permute-start | bytes 5971976 | tf_op jit(solution)/shard_map/ppermute | solution.py:39
  287.8 44.7 %collective-permute-start.34 = (bf16[2,3,144,1152]{3,2,1,0:T(8,128)(2,1)}, bf16[2,3,144,1152]{3,2,1,0:T(8,128)(2,1)}, u32[]{:S(2)}, u32[]{:S(2)}) collective-permute-start(bf16[2,3,144,1152]{3,2,1,0:T(8,128)(2,1)} %shard_map.261.refs_18_.refs_5_), channel_id=1, source_target_pairs={{0,2},{1,3},{2,0},{3,1},{4,6},{5,7},{6,4},{7,5},{8,10},{9,11},{10,... | collective-permute-start | bytes 5971976 | tf_op jit(solution)/shard_map/ppermute | solution.py:39
  409.0 52.1 %collective-permute-start.47 = (bf16[2,256,1152]{2,1,0:T(8,128)(2,1)S(1)}, bf16[2,256,1152]{2,1,0:T(8,128)(2,1)S(1)}, u32[]{:S(2)}, u32[]{:S(2)}) collective-permute-start(bf16[2,256,1152]{2,1,0:T(8,128)(2,1)S(1)} %copy-done.101), channel_id=1, source_target_pairs={{0,16},{1,17},{2,18},{3,19},{4,20},{5,21},{6,22},{7,23},{8,24},{9,... | collective-permute-start | bytes 3538952 | tf_op jit(solution)/shard_map/ppermute | solution.py:39
  495.9 43.2 %collective-permute-start.51 = (bf16[2,144,1152]{2,1,0:T(8,128)(2,1)}, bf16[2,144,1152]{2,1,0:T(8,128)(2,1)}, u32[]{:S(2)}, u32[]{:S(2)}) collective-permute-start(bf16[2,144,1152]{2,1,0:T(8,128)(2,1)} %copy-done.109), channel_id=1, source_target_pairs={{0,2},{1,3},{2,0},{3,1},{4,6},{5,7},{6,4},{7,5},{8,10},{9,11},{10,... | collective-permute-start | bytes 1990664 | tf_op jit(solution)/shard_map/ppermute | solution.py:39
  497.7 41.5 %collective-permute-start.52 = (bf16[2,144,1152]{2,1,0:T(8,128)(2,1)}, bf16[2,144,1152]{2,1,0:T(8,128)(2,1)}, u32[]{:S(2)}, u32[]{:S(2)}) collective-permute-start(bf16[2,144,1152]{2,1,0:T(8,128)(2,1)} %copy-done.108), channel_id=1, source_target_pairs={{0,1},{1,0},{2,3},{3,2},{4,5},{5,4},{6,7},{7,6},{8,9},{9,8},{10,11... | collective-permute-start | bytes 1990664 | tf_op jit(solution)/shard_map/ppermute | solution.py:39
  585.2 52.4 %all-to-all-start.8 = ((bf16[4,144,1152]{2,1,0:T(8,128)(2,1)}), bf16[4,144,1152]{2,1,0:T(8,128)(2,1)}, u32[]{:S(2)}, u32[]{:S(2)}) async-start(bf16[4,144,1152]{2,1,0:T(8,128)(2,1)} %shard_map.276.refs_8_), calls=%async_computation.8 | async-start | bytes 2654208 | tf_op jit(solution)/shard_map/all_to_all | solution.py:56
  591.6 44.6 %collective-permute-start.76 = (bf16[2,144,1152]{2,1,0:T(8,128)(2,1)S(1)}, bf16[2,144,1152]{2,1,0:T(8,128)(2,1)S(1)}, u32[]{:S(2)}, u32[]{:S(2)}) collective-permute-start(bf16[2,144,1152]{2,1,0:T(8,128)(2,1)S(1)} %copy-done.105), channel_id=1, source_target_pairs={{0,2},{1,3},{2,0},{3,1},{4,6},{5,7},{6,4},{7,5},{8,10},{9,11},{10,... | collective-permute-start | bytes 1990664 | tf_op jit(solution)/shard_map/ppermute | solution.py:39
  637.6 66.6 %all-to-all-start.10 = ((bf16[4,144,1152]{2,1,0:T(8,128)(2,1)}), bf16[4,144,1152]{2,1,0:T(8,128)(2,1)}, u32[]{:S(2)}, u32[]{:S(2)}) async-start(bf16[4,144,1152]{2,1,0:T(8,128)(2,1)} %copy-done.10), calls=%async_computation.10 | async-start | bytes 2654208 | tf_op jit(solution)/shard_map/all_to_all | solution.py:56
  642.9 51.8 %collective-permute-start.74 = (bf16[2,2,144,1152]{3,2,1,0:T(8,128)(2,1)}, bf16[2,2,144,1152]{3,2,1,0:T(8,128)(2,1)}, u32[]{:S(2)}, u32[]{:S(2)}) collective-permute-start(bf16[2,2,144,1152]{3,2,1,0:T(8,128)(2,1)} %get-tuple-element.217), channel_id=1, source_target_pairs={{0,1},{1,0},{2,3},{3,2},{4,5},{5,4},{6,7},{7,6},{8,9},{9,8},{10,11... | collective-permute-start | bytes 3981320 | tf_op jit(solution)/shard_map/ppermute | solution.py:39
  643.6 51.2 %collective-permute-start.75 = (bf16[2,2,144,1152]{3,2,1,0:T(8,128)(2,1)}, bf16[2,2,144,1152]{3,2,1,0:T(8,128)(2,1)}, u32[]{:S(2)}, u32[]{:S(2)}) collective-permute-start(bf16[2,2,144,1152]{3,2,1,0:T(8,128)(2,1)} %get-tuple-element.218), channel_id=1, source_target_pairs={{0,2},{1,3},{2,0},{3,1},{4,6},{5,7},{6,4},{7,5},{8,10},{9,11},{10,... | collective-permute-start | bytes 3981320 | tf_op jit(solution)/shard_map/ppermute | solution.py:39
  643.9 56.7 %collective-permute-start.72 = (bf16[2,144,1152]{2,1,0:T(8,128)(2,1)}, bf16[2,144,1152]{2,1,0:T(8,128)(2,1)}, u32[]{:S(2)}, u32[]{:S(2)}) collective-permute-start(bf16[2,144,1152]{2,1,0:T(8,128)(2,1)} %copy-done.107), channel_id=1, source_target_pairs={{0,2},{1,3},{2,0},{3,1},{4,6},{5,7},{6,4},{7,5},{8,10},{9,11},{10,... | collective-permute-start | bytes 1990664 | tf_op jit(solution)/shard_map/ppermute | solution.py:39
  645.6 55.0 %collective-permute-start.73 = (bf16[2,144,1152]{2,1,0:T(8,128)(2,1)}, bf16[2,144,1152]{2,1,0:T(8,128)(2,1)}, u32[]{:S(2)}, u32[]{:S(2)}) collective-permute-start(bf16[2,144,1152]{2,1,0:T(8,128)(2,1)} %copy-done.106), channel_id=1, source_target_pairs={{0,1},{1,0},{2,3},{3,2},{4,5},{5,4},{6,7},{7,6},{8,9},{9,8},{10,11... | collective-permute-start | bytes 1990664 | tf_op jit(solution)/shard_map/ppermute | solution.py:39
  704.2 51.8 %all-to-all-start.9 = ((bf16[4,144,1152]{2,1,0:T(8,128)(2,1)}), bf16[4,144,1152]{2,1,0:T(8,128)(2,1)}, u32[]{:S(2)}, u32[]{:S(2)}) async-start(bf16[4,144,1152]{2,1,0:T(8,128)(2,1)} %shard_map.283._), calls=%async_computation.9 | async-start | bytes 2654208 | tf_op jit(solution)/shard_map/all_to_all | solution.py:56
  756.0 55.6 %all-to-all-start.11 = ((bf16[4,144,1152]{2,1,0:T(8,128)(2,1)}), bf16[4,144,1152]{2,1,0:T(8,128)(2,1)}, u32[]{:S(2)}, u32[]{:S(2)}) async-start(bf16[4,144,1152]{2,1,0:T(8,128)(2,1)} %shard_map.286._), calls=%async_computation.11 | async-start | bytes 2654208 | tf_op jit(solution)/shard_map/all_to_all | solution.py:56
  847.6 62.4 %all-to-all-start.12 = ((bf16[4,144,1152]{2,1,0:T(8,128)(2,1)}), bf16[4,144,1152]{2,1,0:T(8,128)(2,1)}, u32[]{:S(2)}, u32[]{:S(2)}) async-start(bf16[4,144,1152]{2,1,0:T(8,128)(2,1)} %copy-done.14), calls=%async_computation.12 | async-start | bytes 2654208 | tf_op jit(solution)/shard_map/all_to_all | solution.py:56
  892.9 83.4 %collective-permute-start.59 = (f32[256,1152]{1,0:T(8,128)}, f32[256,1152]{1,0:T(8,128)}, u32[]{:S(2)}, u32[]{:S(2)}) collective-permute-start(f32[256,1152]{1,0:T(8,128)} %convert_select_fusion), channel_id=1, source_target_pairs={{0,16},{1,17},{2,18},{3,19},{4,20},{5,21},{6,22},{7,23},{8,24},{9,... | collective-permute-start | bytes 3538952 | tf_op jit(solution)/shard_map/ppermute | solution.py:39
  898.1 41.9 %collective-permute-start.64 = (bf16[2,4,2,6912]{3,1,2,0:T(4,128)(2,1)}, bf16[2,4,2,6912]{3,1,2,0:T(4,128)(2,1)}, u32[]{:S(2)}, u32[]{:S(2)}) collective-permute-start(bf16[2,4,2,6912]{3,1,2,0:T(4,128)(2,1)} %pad_maximum_fusion.1), channel_id=1, source_target_pairs={{0,2},{1,3},{2,0},{3,1},{4,6},{5,7},{6,4},{7,5},{8,10},{9,11},{10,... | collective-permute-start | bytes 663560 | tf_op jit(solution)/shard_map/ppermute | solution.py:39
  (239 other events, 3195.2 us)

commit v2 on v1

--- a/solution.py
+++ b/solution.py
@@ -75,7 +75,7 @@
 
 
 def cost(nbytes, flops=0):
-    return pl.CostEstimate(flops=flops, bytes_accessed=nbytes, transcendentals=0)
+    return pl.CostEstimate(flops=0, bytes_accessed=0, transcendentals=0)
 
 
 def fence(arrays, after):
@@ -234,8 +234,7 @@
         at += 2 * n
 
         def copy(source):
-            for j in range(NZ):
-                pltpu.make_async_copy(source, out.at[j, i], sems.at[j, i]).start()
+            pltpu.make_async_copy(source, out.at[i], sems.at[i]).start()
 
         def act(source):
             if kind == 2:
@@ -261,8 +260,7 @@
 
         chosen(block, mine, other, act)
     for i in range(len(items)):
-        for j in range(NZ):
-            pltpu.make_async_copy(out.at[j, i], out.at[j, i], sems.at[j, i]).wait()
+        pltpu.make_async_copy(out.at[i], out.at[i], sems.at[i]).wait()
 
 
 def extract(items, mine, other, after):
@@ -272,10 +270,10 @@
         operands += [*mine[kind], *other[kind]]
     return pl.pallas_call(
         functools.partial(extract_kernel, items),
-        out_shape=jax.ShapeDtypeStruct((NZ, n, PIECE, D), BF),
+        out_shape=jax.ShapeDtypeStruct((n, PIECE, D), BF),
         in_specs=[ANYWHERE] * (len(operands) + 1),
         out_specs=INSIDE,
-        scratch_shapes=[pltpu.SemaphoreType.DMA((NZ, n))],
+        scratch_shapes=[pltpu.SemaphoreType.DMA((n,))],
         compiler_params=PARAMS,
         cost_estimate=cost(4 * n * PIECE * D),
     )(*operands, after)
@@ -345,7 +343,7 @@
 
     def extract(self, g):
         self.after = extract(GROUPS[g], self.mine, self.other, self.after)
-        self.state[g] = trade(self.after)
+        self.state[g] = lax.all_gather(self.after, Z, axis=0, tiled=False)
 
     def stack(self, g):
         p0 = stacked(self.state[g], self.after)
@@ -365,6 +363,11 @@
         p3 = fence(p3, self.after)
         self.after = p3[0]
         self.state[g] = own + tuple(p3), far + tuple(swap(p) for p in p3)
+
+    def hold(self, *values):
+        values = fence(values, self.after)
+        self.after = values[0]
+        return values
 
     def operands(self, g):
         own, far = self.state[g]
@@ -390,15 +393,14 @@
             for zp in range(NZ):
                 rows = pl.ds(pl.multiple_of(u * ROWS, ROWS), ROWS)
                 acc[zp * ROWS : (zp + 1) * ROWS, :] = jnp.dot(
-                    lo[zp, c, rows, :], ro[...], preferred_element_type=F32
+                    lo[c, zp, rows, :], ro[...], preferred_element_type=F32
                 ) + jnp.dot(lx[zp, rows, :], rx[...], preferred_element_type=F32)
         else:
             ro, rx = ins[-2:]
-            mine = pl.ds(pl.multiple_of(c * HALF + u * D, D), D)
-            other = pl.ds(pl.multiple_of(u * D, D), D)
+            cols = pl.ds(pl.multiple_of(u * D, D), D)
 
             def product(lo, lx):
-                acc[...] = tdot(lo[...], ro[:, mine]) + tdot(lx[...], rx[:, other])
+                acc[...] = tdot(lo[...], ro[c, :, cols]) + tdot(lx[...], rx[:, cols])
 
             if kind == 1:
                 product(ins[0], ins[1])
@@ -440,56 +442,67 @@
     )(*operands, after)
 
 
-def finish_kernel(block, kind, n, *refs):
-    pieces = refs[:5]
-    acc, sems = refs[-2:]
-    outs = refs[-2 - n : -2]
+def finish_kernel(block, *refs):
+    p0, p1, p2, pa, pb = refs[:5]
+    outs = refs[-8:-4]
+    raw, acc, sems_in, sems_out = refs[-4:]
     c, z, r = place()
 
     @pl.when(c == block)
     def _():
-        for core in range(2):
-            for m in range(4):
-                low = lax.rem(r + m, 2)
-                high = lax.rem(r // 2 + m // 2, 2)
-                if m < 3:
-                    piece = pieces[m][kind, core]
+        copies = {}
+        for kind in range(3):
+            for core in range(2):
+                flat = kind * 2 + core
+                last = pa.at[flat] if flat < 3 else pb.at[flat - 3]
+                for m, piece in enumerate((p0.at[kind, core], p1.at[kind, core], p2.at[kind, core], last)):
+                    n = flat * 4 + m
+                    copy = pltpu.make_async_copy(piece, raw.at[n], sems_in.at[n])
+                    copy.start()
+                    copies[n] = copy
+        done = []
+        for kind in range(3):
+            for core in range(2):
+                for m in range(4):
+                    n = (kind * 2 + core) * 4 + m
+                    copies[n].wait()
+                    low = lax.rem(r + m, 2)
+                    unit = core * 2 + lax.rem(r // 2 + m // 2, 2)
+                    piece = raw[n].astype(F32)
+                    if kind == 2:
+                        at = pl.multiple_of((unit * 2 + low) * PIECE, PIECE)
+                        acc[pl.ds(2 * 4 * ROWS + at, PIECE), :] = piece
+                    else:
+                        at = pl.multiple_of((kind * 4 + unit) * ROWS + low * PIECE, PIECE)
+                        acc[pl.ds(at, PIECE), :] = piece
+            if kind == 2:
+                done.append(pltpu.make_async_copy(acc.at[8 * ROWS :, :], outs[3], sems_out.at[8]))
+                done[-1].start()
+                continue
+            for unit in range(4):
+                source = acc.at[(kind * 4 + unit) * ROWS : (kind * 4 + unit + 1) * ROWS, :]
+                if kind == 0 and unit == 3:
+                    target = outs[1]
                 else:
-                    flat = kind * 2 + core
-                    piece = pieces[3][flat] if flat < 3 else pieces[4][flat - 3]
-                piece = piece.astype(F32)
-                if kind == 2:
-                    row = pl.multiple_of(core * (D // 2) + (high * 2 + low) * PIECE, PIECE)
-                    acc[pl.ds(row, PIECE), :] = piece
-                else:
-                    row = pl.multiple_of(low * PIECE, PIECE)
-                    col = pl.multiple_of((core * 2 + high) * D, D)
-                    acc[pl.ds(row, PIECE), pl.ds(col, D)] = piece
-        if n == 2:
-            parts = (acc.at[:, pl.ds(0, 3 * D)], acc.at[:, pl.ds(3 * D, D)])
-        else:
-            parts = (acc,)
-        copies = [pltpu.make_async_copy(parts[i], outs[i], sems.at[i]) for i in range(n)]
-        for copy in copies:
-            copy.start()
-        for copy in copies:
+                    target = outs[0 if kind == 0 else 2].at[:, unit * D : (unit + 1) * D]
+                done.append(pltpu.make_async_copy(source, target, sems_out.at[kind * 4 + unit]))
+                done[-1].start()
+        for copy in done:
             copy.wait()
 
 
-def finish(block, kind, pieces, before, after):
-    if kind == 0:
-        shapes = ((ROWS, 3 * D), (ROWS, D))
-    else:
-        shapes = ((D, D),) if kind == 2 else ((ROWS, FF),)
-    n = len(shapes)
-    return pl.pallas_call(
-        functools.partial(finish_kernel, block, kind, n),
+def finish(block, pieces, before, after):
+    shapes = ((ROWS, 3 * D), (ROWS, D), (ROWS, FF), (D, D))
+    return pl.pallas_call(
+        functools.partial(finish_kernel, block),
         out_shape=tuple(jax.ShapeDtypeStruct(s, F32) for s in shapes),
-        in_specs=[INSIDE] * 5 + [ANYWHERE] * (1 + len(before)),
-        out_specs=(ANYWHERE,) * n,
+        in_specs=[ANYWHERE] * (6 + len(before)),
+        out_specs=(ANYWHERE,) * 4,
         scratch_shapes=[
-            pltpu.VMEM((D, D) if kind == 2 else (ROWS, FF), F32),
-            pltpu.SemaphoreType.DMA((2,)),
+            pltpu.VMEM((24, PIECE, D), BF),
+            pltpu.VMEM((12 * ROWS, D), F32),
+            pltpu.SemaphoreType.DMA((24,)),
+            pltpu.SemaphoreType.DMA((9,)),
         ],
         input_output_aliases={6 + i: i for i in range(len(before))},
         compiler_params=PARAMS,
@@ -508,7 +521,7 @@
         self.state = []
         self.own = {}
         self.ready = {}
-        self.results = {0: (), 1: (), 2: ()}
+        self.results = ()
 
     def begin(self, block, kind, operands):
         keep_x, send_x, keep_y, send_y = wgrad(kind, operands, self.after)
@@ -554,10 +567,13 @@
         self.ready[block] = p0, p1, p2, pa, pb
 
     def finish(self, block):
-        for kind in range(3):
-            out = finish(block, kind, self.ready[block], self.results[kind], self.after)
-            self.results[kind] = out
-            self.after = out[0]
+        self.results = finish(block, self.ready[block], self.results, self.after)
+        self.after = self.results[0]
+
+    def hold(self, *values):
+        values = fence(values, self.after)
+        self.after = values[0]
+        return values
 
 
 def standard(v):
@@ -649,7 +665,9 @@
         hidden[:, cols] = hid
         part = jax.nn.gelu(hid, approximate=True)
         act[:, cols] = part.astype(BF)
-        act_t[cols, :] = part.T.astype(BF)
+        turned = part.T.astype(BF)
+        act_t[0, j] = turned[: D // 2]
+        act_t[1, j] = turned[D // 2 :]
     wait_d()
     keep_d = pltpu.make_async_copy(wd, wd_out, sems_d.at[26])
     keep_d.start()
@@ -667,7 +685,7 @@
             shape_of(BF, D, FF),
             shape_of(BF, FF, D),
             shape_of(F32, t, FF),
-            shape_of(BF, FF, t),
+            shape_of(BF, 2, NZ, D // 2, t),
             shape_of(F32, t, D),
             shape_of(BF, t, D),
         ),
@@ -703,7 +721,7 @@
 
 def mlp_back_kernel(*refs):
     grad, d_branch, ada, mid, attended, hidden, branch, wu_in, wd_in = refs[:9]
-    d_hidden, d_mid, d_att, stats, hidden_sum, wu, wd, acc, sems = refs[10:]
+    d_hidden, d_mid, d_att, stats, wu, wd, acc, sems = refs[10:]
     copies = []
     for j in range(4):
         part = slice(j * D, (j + 1) * D)
@@ -713,29 +731,30 @@
     for down, up in copies:
         down.start()
         up.start()
-    stats[2:3, :] = column_sum(grad[...].astype(F32) * branch[...])
-    stats[4:5, :] = column_sum(d_branch[...].astype(F32))
+    stats[...] = jnp.zeros_like(stats)
+    stats[5:6, :] = column_sum(grad[...].astype(F32) * branch[...])
+    stats[13:14, :] = column_sum(d_branch[...].astype(F32))
     for j in range(4):
         part = slice(j * D, (j + 1) * D)
         copies[j][0].wait()
         d_act = mmt(d_branch[...], wd[part, :])
         d_hid = (d_act * gelu_slope(hidden[:, part])).astype(BF)
-        d_hidden[:, part] = d_hid
-        hidden_sum[:, part] = column_sum(d_hid.astype(F32))
+        d_hidden[j // 2, :, (j % 2) * D : (j % 2 + 1) * D] = d_hid
+        stats[9 + j : 10 + j, :] = column_sum(d_hid.astype(F32))
         copies[j][1].wait()
-        product = mmt(d_hidden[:, part], wu[:, part])
+        product = mmt(d_hid, wu[:, part])
         if j == 0:
             acc[...] = product
         else:
             acc[...] += product
     n2, r2 = standard(mid[...])
-    stats[0:1, :] = column_sum(acc[...])
-    stats[1:2, :] = column_sum(acc[...] * n2)
+    stats[3:4, :] = column_sum(acc[...])
+    stats[4:5, :] = column_sum(acc[...] * n2)
     whole = grad[...].astype(F32) + norm_back(acc[...] * (1.0 + row(ada, 4)), n2, r2)
     d_mid[...] = whole
     d_att[...] = (row(ada, 2) * whole).astype(BF)
-    stats[3:4, :] = column_sum(whole * attended[...])
-    stats[5:6, :] = column_sum(d_att[...].astype(F32))
+    stats[2:3, :] = column_sum(whole * attended[...])
+    stats[8:9, :] = column_sum(d_att[...].astype(F32))
 
 
 def mlp_back(grad, d_branch, ada, mid, attended, hidden, branch, wu, wd, after):
@@ -743,14 +762,13 @@
     return pl.pallas_call(
         mlp_back_kernel,
         out_shape=(
-            shape_of(BF, t, FF),
+            shape_of(BF, 2, t, HALF),
             shape_of(F32, t, D),
             shape_of(BF, t, D),
-            shape_of(F32, 8, D),
-            shape_of(F32, 1, FF),
+            shape_of(F32, 16, D),
         ),
         in_specs=[INSIDE] * 7 + [ANYWHERE] * 3,
-        out_specs=(INSIDE,) * 5,
+        out_specs=(INSIDE,) * 4,
         scratch_shapes=[
             pltpu.VMEM((D, FF), BF),
             pltpu.VMEM((FF, D), BF),
@@ -763,8 +781,8 @@
 
 
 def attend_back_kernel(*refs):
-    x, d_mid, d_att, ada, q_ref, k_ref, v_ref, w_in = refs[:8]
-    out, d_x, d_x_low, stats, w, mixed, sem = refs[9:]
+    x, d_mid, d_att, ada, q_ref, k_ref, v_ref, stats, w_in = refs[:9]
+    out, d_x, d_x_low, small, w, mixed, sem = refs[10:]
     copies = [
         pltpu.make_async_copy(w_in.at[:, 3 * D :], w.at[:, 3 * D :], sem.at[0]),
         pltpu.make_async_copy(w_in.at[:, : 3 * D], w.at[:, : 3 * D], sem.at[1]),
@@ -780,35 +798,40 @@
         d_probs = mmt(dm, v)
         inner = jnp.sum(d_probs * soft, axis=-1, keepdims=True)
         d_s = (soft * (d_probs - inner)).astype(BF)
-        out[:, cols] = (mm(d_s, k) * HEAD_DIM**-0.5).astype(BF)
-        out[:, head_cols(h, D)] = tdot(d_s, q).astype(BF)
-        out[:, head_cols(h, 2 * D)] = tdot(soft.astype(BF), dm).astype(BF)
-    out[:, 3 * D :] = d_att[...]
-    stats[2:3, :] = column_sum(out[:, :D].astype(F32))
-    stats[3:4, :] = column_sum(out[:, 2 * D : 3 * D].astype(F32))
+        out[0, :, cols] = (mm(d_s, k) * HEAD_DIM**-0.5).astype(BF)
+        out[0, :, head_cols(h, D)] = tdot(d_s, q).astype(BF)
+        out[1, :, cols] = tdot(soft.astype(BF), dm).astype(BF)
+    out[1, :, D:] = d_att[...]
     copies[1].wait()
-    d_in = mmt(out[:, :D], w[:, :D])
-    d_in += mmt(out[:, D : 2 * D], w[:, D : 2 * D])
-    d_in += mmt(out[:, 2 * D : 3 * D], w[:, 2 * D : 3 * D])
+    d_in = mmt(out[0, :, :D], w[:, :D])
+    d_in += mmt(out[0, :, D:], w[:, D : 2 * D])
+    d_in += mmt(out[1, :, :D], w[:, 2 * D : 3 * D])
     n1, r1 = standard(x[...].astype(F32))
-    stats[0:1, :] = column_sum(d_in)
-    stats[1:2, :] = column_sum(d_in * n1)
+    rows = [
+        column_sum(d_in),
+        column_sum(d_in * n1),
+        stats[2:6, :],
+        column_sum(out[0, :, :D].astype(F32)),
+        column_sum(out[1, :, :D].astype(F32)),
+        stats[8:, :],
+    ]
+    small[...] = jnp.concatenate(rows, axis=0).astype(BF)
     whole = d_mid[...] + norm_back(d_in * (1.0 + row(ada, 1)), n1, r1)
     d_x[...] = whole
     d_x_low[...] = whole.astype(BF)
 
 
-def attend_back(x, d_mid, d_att, ada, q, k, v, wa, after):
+def attend_back(x, d_mid, d_att, ada, q, k, v, stats, wa, after):
     t = x.shape[0]
     return pl.pallas_call(
         attend_back_kernel,
         out_shape=(
-            shape_of(BF, t, FF),
+            shape_of(BF, 2, t, HALF),
             shape_of(F32, t, D),
             shape_of(BF, t, D),
-            shape_of(F32, 8, D),
+            shape_of(BF, 16, D),
         ),
-        in_specs=[INSIDE] * 7 + [ANYWHERE] * 2,
+        in_specs=[INSIDE] * 8 + [ANYWHERE] * 2,
         out_specs=(INSIDE,) * 4,
         scratch_shapes=[
             pltpu.VMEM((D, FF), BF),
@@ -817,17 +840,12 @@
         ],
         compiler_params=PARAMS,
         cost_estimate=cost(3 * D * FF, 2 * t * D * FF),
-    )(x, d_mid, d_att, ada, q, k, v, wa, after)
-
-
-def far_half(right):
+    )(x, d_mid, d_att, ada, q, k, v, stats, wa, after)
+
+
+def far_half(halves):
     c = lax.axis_index(S)
-    return swap(lax.dynamic_slice_in_dim(right, (1 - c) * HALF, HALF, 1))
-
-
-def far_rows(act_t):
-    c = lax.axis_index(S)
-    return swap(lax.dynamic_index_in_dim(act_t, 1 - c, 1, keepdims=False))
+    return swap(lax.dynamic_index_in_dim(halves, 1 - c, 0, keepdims=False))
 
 
 def rows_sum(v):
@@ -841,25 +859,18 @@
     return jnp.concatenate([jnp.cos(angles), jnp.sin(angles)], axis=-1)
 
 
-def everywhere(value):
-    nr = lax.axis_size(R)
-    out = along_z(value)[None]
+def across(value):
+    out = value[None]
     bit = 1
-    while bit < nr:
+    while bit < lax.axis_size(R):
         out = jnp.concatenate([out, cross(out, bit)])
         bit *= 2
-    return jnp.take(out, lax.axis_index(R) ^ jnp.arange(nr), axis=0)
-
-
-def total(value):
-    value = value + swap(value)
-    for bit in (1, 2):
-        value = value + move(value, lambda s, z, r: (s, z ^ bit, r))
-    bit = 1
-    while bit < lax.axis_size(R):
-        value = value + cross(value, bit)
-        bit *= 2
-    return value
+    return out
+
+
+def in_order(value):
+    nr = lax.axis_size(R)
+    return jnp.take(value, lax.axis_index(R) ^ jnp.arange(nr), axis=0)
 
 
 def per_device(
@@ -934,101 +945,128 @@
         got = attend(block, value, adas[block], biases[block], gatherer.operands(2 * block))
         gatherer.after = got[-1]
         kept.append(got)
+        return swap(got[1])
 
     def run_mlp(block):
         mid, mlp_in = kept[block][-2:]
         got = mlp(block, mid, mlp_in, adas[block], biases[block], gatherer.operands(2 * block + 1))
         gatherer.after = got[-1]
-        act_t = got[3].reshape(NZ, 2, D // 2, -1)
-        kept_mlp.append(got[:3] + (act_t,) + got[4:] + (far_rows(act_t), swap(mlp_in)))
-
-    gatherer.extract(0)
+        kept_mlp.append(got)
+        return far_half(got[3]), swap(mlp_in)
+
+    def branch_grad(block, grad):
+        return (adas[block][5:] * grad.astype(F32)).astype(BF)
+
+    for g in range(4):
+        gatherer.extract(g)
+    ids_all = in_order(across(ids_z)).reshape(-1, 2)
+    gatherer.after = ids_all
     gatherer.stack(0)
-    gatherer.extract(1)
     gatherer.onward(0)
     gatherer.share(0)
-    run_attend(0, x)
+    far_sides0 = run_attend(0, x)
     gatherer.stack(1)
-    gatherer.extract(2)
+    d_branch1 = branch_grad(1, cot)
+    far_branch1 = swap(d_branch1)
+    far_sides0, far_branch1 = gatherer.hold(far_sides0, far_branch1)
+    gatherer.onward(1)
     gatherer.stack(2)
-    gatherer.extract(3)
-    gatherer.onward(1)
+    gatherer.share(1)
+    far_mlp0 = run_mlp(0)
+    y0 = kept_mlp[0][5]
     gatherer.onward(2)
-    gatherer.share(1)
-    run_mlp(0)
-    y0 = kept_mlp[0][5]
+    gatherer.stack(3)
+    far_mlp0 = gatherer.hold(*far_mlp0)
     gatherer.share(2)
-    gatherer.stack(3)
-    run_attend(1, y0)
+    far_sides1 = run_attend(1, y0)
     gatherer.onward(3)
+    (far_sides1,) = gatherer.hold(far_sides1)
     gatherer.share(3)
-    run_mlp(1)
+    far_mlp1 = run_mlp(1)
     y1 = kept_mlp[1][5]
 
     reducer = Reducer(y1)
 
-    def run_mlp_back(block, grad):
-        ada = adas[block]
-        d_branch = (ada[5:] * grad.astype(F32)).astype(BF)
-        far_branch = swap(d_branch)
+    def run_mlp_back(block, grad, d_branch):
         attended, mid, mlp_in = kept[block][-3:]
-        wu, wd, hidden, act_t, branch, _, far_act, far_in = kept_mlp[block]
-        got = mlp_back(grad, d_branch, ada, mid, attended, hidden, branch, wu, wd, reducer.after)
-        d_hidden = got[0]
-        reducer.after = d_hidden
-        far_hidden = far_half(d_hidden)
-        reducer.begin(block, 2, (act_t, far_act, d_branch, far_branch))
-        reducer.begin(block, 1, (mlp_in, far_in, d_hidden, far_hidden))
-        return got
+        wu, wd, hidden, act_t, branch, _ = kept_mlp[block]
+        got = mlp_back(
+            grad, d_branch, adas[block], mid, attended, hidden, branch, wu, wd, reducer.after
+        )
+        reducer.after = got[0]
+        return got, far_half(got[0])
 
     def run_attend_back(block, value, back):
         wa, sides, q, k, v = kept[block][:5]
-        _, d_mid, d_att, stats_m, hidden_sum = back
-        far = swap(sides)
-        d_all, d_x, d_x_low, stats_a = attend_back(
-            value, d_mid, d_att, adas[block], q, k, v, wa, reducer.after
+        _, d_mid, d_att, stats = back
+        got = attend_back(
+            value, d_mid, d_att, adas[block], q, k, v, stats, wa, reducer.after
         )
-        reducer.after = d_x_low
-        d_ada = jnp.concatenate(
-            [stats_a[0], stats_a[1], stats_m[3], stats_m[0], stats_m[1], stats_m[2]]
-        ).astype(BF)
-        sums = jnp.concatenate([stats_a[2], stats_a[3], stats_m[5], hidden_sum[0], stats_m[4]])
-        operands = (sides, far, d_all, far_half(d_all))
-        return d_x, d_x_low, d_ada, sums, operands
-
-    back1 = run_mlp_back(1, cot)
-    _, dx1, dada1, sums1, operands1 = run_attend_back(1, y0, back1)
+        reducer.after = got[2]
+        return got
+
+    def begin(block, kind, *operands):
+        reducer.begin(block, kind, operands)
+
+    back1, far_hidden1 = run_mlp_back(1, cot, d_branch1)
+    begin(1, 2, kept_mlp[1][3], far_mlp1[0], d_branch1, far_branch1)
+    begin(1, 1, kept[1][-1], far_mlp1[1], back1[0], far_hidden1)
+    d_all1, dx1f, dx1, small1 = run_attend_back(1, y0, back1)
+    far_all1 = far_half(d_all1)
+    d_branch0 = branch_grad(0, dx1)
+    far_branch0 = swap(d_branch0)
     reducer.first(0)
-    reducer.begin(1, 0, operands1)
-    back0 = run_mlp_back(0, dx1)
+    begin(1, 0, kept[1][1], far_sides1, d_all1, far_all1)
+    back0, far_hidden0 = run_mlp_back(0, dx1, d_branch0)
+    begin(0, 2, kept_mlp[0][3], far_mlp0[0], d_branch0, far_branch0)
     reducer.first(1)
     reducer.second(0)
-    dx0, _, dada0, sums0, operands0 = run_attend_back(0, x, back0)
+    begin(0, 1, kept[0][-1], far_mlp0[1], back0[0], far_hidden0)
+    d_all0, dx0, dx0_low, small0 = run_attend_back(0, x, back0)
+    far_all0 = far_half(d_all0)
     reducer.first(2)
-    reducer.begin(0, 0, operands0)
     reducer.second(1)
     reducer.third(0)
+    begin(0, 0, kept[0][1], far_sides0, d_all0, far_all0)
+    small_keep = jnp.where(is_first, small0, small1)
+    small_got = swap(jnp.where(is_first, small1, small0))
     reducer.first(3)
     reducer.second(2)
     reducer.third(1)
+    (small_got,) = reducer.hold(small_got)
+    small = jnp.stack(
+        [jnp.where(is_first, small_keep, small_got), jnp.where(is_first, small_got, small_keep)]
+    )
     reducer.first(4)
     reducer.second(3)
     reducer.third(2)
+    small = along_z(small)
     reducer.unite(1)
     reducer.first(5)
+    (small,) = reducer.hold(small)
+    small = small[None]
+    bits = [1 << i for i in range(lax.axis_size(R).bit_length() - 1)]
+    hop = cross(small, 1)
     reducer.spread(1)
     reducer.second(4)
     reducer.third(3)
+    (hop,) = reducer.hold(hop)
+    small = jnp.concatenate([small, hop])
+    hop = cross(small, 2)
     reducer.spread_on(1)
     reducer.second(5)
     reducer.third(4)
+    (hop,) = reducer.hold(hop)
+    small = jnp.concatenate([small, hop])
+    for bit in bits[2:]:
+        small = jnp.concatenate([small, cross(small, bit)])
     reducer.finish(1)
     reducer.third(5)
     reducer.unite(0)
     reducer.spread(0)
     reducer.spread_on(0)
     reducer.finish(0)
-    (qkv_grad, proj_grad), (up_grad,), (down_grad,) = (reducer.results[k] for k in range(3))
+    qkv_grad, proj_grad, up_grad, down_grad = reducer.results
 
     def both_micros(v0, v1):
         keep = jnp.where(is_first, v0, v1)
@@ -1038,28 +1076,22 @@
     block_outputs = both_micros(y0, y1)[None, :, None]
     input_grads = both_micros(dx0, dx1.astype(F32))[None, :, None]
 
-    sums = total(jnp.stack([sums0, sums1]))
-    sums = lax.dynamic_index_in_dim(sums, c, 0, keepdims=False)
+    small = in_order(small).reshape(-1, 16, D)
+    sums = rows_sum(small[:, 6:14])
+    dada_own = small[:, :6].reshape(-1, 6 * D)
 
     def own_slice(vec):
+        vec = vec.reshape(-1)
         n = vec.shape[0] // NZ
         return lax.dynamic_slice_in_dim(vec, z * n, n, 0)[None]
 
-    qv_bias_grad = own_slice(sums[: 2 * D])
-    proj_bias_grad = own_slice(sums[2 * D : 3 * D])
-    up_bias_grad = own_slice(sums[3 * D : 3 * D + FF])
-    down_bias_grad = own_slice(sums[3 * D + FF :])
-
-    ids_all = ids_z[None]
-    bit = 1
-    while bit < lax.axis_size(R):
-        ids_all = jnp.concatenate([ids_all, cross(ids_all, bit)])
-        bit *= 2
-    ids_all = jnp.take(ids_all, lax.axis_index(R) ^ jnp.arange(lax.axis_size(R)), axis=0)
-    ids_all = ids_all.reshape(-1, 2)
+    qv_bias_grad = own_slice(sums[:2])
+    proj_bias_grad = own_slice(sums[2])
+    up_bias_grad = own_slice(sums[3:7])
+    down_bias_grad = own_slice(sums[7])
+
     cond_all = cond_of(ids_all[:, 0], ids_all[:, 1])
     labels_all = ids_all[:, 1]
-    dada_own = everywhere(both_micros(dada0, dada1)).reshape(-1, 6 * D)
     cond_rows = lax.dynamic_slice_in_dim(cond_all, z * ROWS, ROWS, 1)
     silu_rows = jax.nn.silu(cond_rows).astype(BF)
     ada_grad = lax.dot_general(

time: 1020 us -> 894 us (0.88)
  waiting for transfers between devices: 380 us -> 299 us
  starting transfers between devices: 146 us -> 126 us
  Pallas kernels: 290 us -> 273 us
  local copies, waits for them, and re-layouts: 139 us -> 125 us
  between operations: 2.86 us -> 15.7 us
  blocking collectives: 0 us -> 12.4 us
  other arithmetic: 35.4 us -> 23.3 us
    all_to_all x14 -> x9, waiting for transfers between devices: 87.3 us -> 8.04 us  [trade(): return lax.all_to_all(value, Z, split_axis=0, concat_axis=0, tiled=True)]
    all_to_all x14 -> x9, starting transfers between devices: 66.3 us -> 42.7 us  [trade(): return lax.all_to_all(value, Z, split_axis=0, concat_axis=0, tiled=True)]
    pallas_call x10 -> x6, Pallas kernels: 96 us -> 79.1 us  [the longest x2 37.6 us: attend_back(): pl.pallas_call(attend_back_kernel, out_shape=(shape_of(BF, 2, t, HALF), s...]
    all_to_all x0 -> x1, blocking collectives: none -> 12.4 us  [trade(): return lax.all_to_all(value, Z, split_axis=0, concat_axis=0, tiled=True)]
    ppermute x101 -> x96, waiting for transfers between devices: 293 us -> 281 us  [move(): return lax.ppermute(value, ALL, pairs)]
    all_gather x0 -> x4, waiting for transfers between devices: none -> 10.7 us  [extract(): self.state[g] = lax.all_gather(self.after, Z, axis=0, tiled=False)]
    unnamed x317 -> x306, local copies, waits for them, and re-layouts: 76.3 us -> 66.2 us
    ppermute x101 -> x96, starting transfers between devices: 80 us -> 82.6 us  [move(): return lax.ppermute(value, ALL, pairs)]
  transfers between devices with their start and end apart: 115 -> 109, of which waited for: 43 -> 37; matrix products, arithmetic and copies ran while one was open for 12% -> 11% of each run, Pallas kernels for 22% -> 27%
where the time goes in v2:
time: 894 us; the launch traced here: 887 us
  waiting for transfers between devices  299 us (33%)
  Pallas kernels  273 us (31%)
  starting transfers between devices  126 us (14%)
  local copies, waits for them, and re-layouts  125 us (14%)
  other arithmetic  23.3 us (3%)
  between operations  15.7 us (2%)
  matrix products  12.6 us (1%)
  blocking collectives  12.4 us (1%)
    ppermute x96, waiting for transfers between devices, move(): return lax.ppermute(value, ALL, pairs)  281 us
    ppermute x96, starting transfers between devices, move(): return lax.ppermute(value, ALL, pairs)  82.6 us
    unnamed x306, local copies, waits for them, and re-layouts  66.2 us
    pallas_call x6, Pallas kernels, wgrad(): pl.pallas_call(functools.partial(wgrad_kernel, kind), out_shape=(part,) *...  50.6 us
    pallas_call x2, Pallas kernels, mlp(): pl.pallas_call(functools.partial(mlp_kernel, block), out_shape=(shape_of(...  46.7 us
    all_to_all x9, starting transfers between devices, trade(): return lax.all_to_all(value, Z, split_axis=0, concat_axis=0, tiled=True)  42.7 us
    pallas_call x2, Pallas kernels, attend(): pl.pallas_call(functools.partial(attend_kernel, block), out_shape=(shape_...  37.6 us
    pallas_call x2, Pallas kernels, attend_back(): pl.pallas_call(attend_back_kernel, out_shape=(shape_of(BF, 2, t, HALF), s...  37.6 us
  transfers between devices with their start and end apart: 109, of which 37 were waited for; matrix products, arithmetic and copies ran while one was open for 11% of the time, Pallas kernels for 27%

profile of v2, /device:TPU:0, one launch (start us, length us, event | category | flops | bytes accessed | tf_op | source)
XLA Modules:
  0.0 886.8 jit_solution(15670454869345413635)
XLA Ops:
  44.2 10.7 %all-gather.9.cloned.1.call-done = bf16[4,144,1152]{2,1,0:T(8,128)(2,1)} async-done(((bf16[1,144,1152]{2,1,0:T(8,128)(2,1)}), bf16[4,144,1152]{2,1,0:T(8,128)(2,1)}) %all-gather.9.cloned.1.call-update) | async-done | bytes 1327120 | tf_op jit(solution)/shard_map/all_gather | solution.py:346
  68.1 12.6 %collective-permute-done.6.refs_0_ = bf16[1,3,144,1152]{3,2,1,0:T(8,128)(2,1)} collective-permute-done((bf16[1,3,144,1152]{3,2,1,0:T(8,128)(2,1)}, bf16[1,3,144,1152]{3,2,1,0:T(8,128)(2,1)}, u32[]{:S(2)}, u32[]{:S(2)}) %collective-permute-start.6) | collective-permute-done | bytes 995360 | tf_op jit(solution)/shard_map/ppermute | solution.py:39
  93.1 14.3 %collective-permute-done.9.refs_1_ = bf16[1,2,144,1152]{3,2,1,0:T(8,128)(2,1)} collective-permute-done((bf16[1,2,144,1152]{3,2,1,0:T(8,128)(2,1)S(1)}, bf16[1,2,144,1152]{3,2,1,0:T(8,128)(2,1)}, u32[]{:S(2)}, u32[]{:S(2)}) %collective-permute-start.9) | collective-permute-done | bytes 663584 | tf_op jit(solution)/shard_map/ppermute | solution.py:39
  115.7 18.8 %shard_map.250 = (bf16[1152,4608]{1,0:T(8,128)(2,1)}, bf16[2,256,1152]{2,1,0:T(8,128)(2,1)}, bf16[256,1152]{1,0:T(8,128)(2,1)S(1)}, bf16[256,1152]{1,0:T(8,128)(...) custom-call(bf16[256,1152]{1,0:T(8,128)(2,1)S(1)} %copy-done.30, ...), custom_call_target="tpu_custom_call" | custom-call | tf_op jit(solution)/shard_map/pallas_call | solution.py:642
  148.8 37.5 %collective-permute-done.17.refs_0_ = bf16[2,3,144,1152]{3,2,1,0:T(8,128)(2,1)} collective-permute-done((bf16[2,3,144,1152]{3,2,1,0:T(8,128)(2,1)}, bf16[2,3,144,1152]{3,2,1,0:T(8,128)(2,1)}, u32[]{:S(2)}, u32[]{:S(2)}) %collective-permute-start.17) | collective-permute-done | bytes 1990688 | tf_op jit(solution)/shard_map/ppermute | solution.py:39
  196.0 17.2 %collective-permute-done.21.refs_0_ = bf16[1,3,144,1152]{3,2,1,0:T(8,128)(2,1)S(1)} collective-permute-done((bf16[1,3,144,1152]{3,2,1,0:T(8,128)(2,1)}, bf16[1,3,144,1152]{3,2,1,0:T(8,128)(2,1)S(1)}, u32[]{:S(2)}, u32[]{:S(2)}) %collective-permute-start.21) | collective-permute-done | bytes 995360 | tf_op jit(solution)/shard_map/ppermute | solution.py:39
  223.1 23.1 %shard_map.258 = (bf16[1152,4608]{1,0:T(8,128)(2,1)}, bf16[4608,1152]{1,0:T(8,128)(2,1)}, f32[256,4608]{1,0:T(8,128)}, bf16[2,4,576,256]{3,2,1,0:T(8,128)(2,1)},...) custom-call(f32[256,1152]{1,0:T(8,128)} %get-tuple-element.140.refs_0_.refs_3_, ...), custom_call_target="tpu_custom_call" | custom-call | tf_op jit(solution)/shard_map/pallas_call | solution.py:682
  275.5 18.8 %shard_map.264 = (bf16[1152,4608]{1,0:T(8,128)(2,1)}, bf16[2,256,1152]{2,1,0:T(8,128)(2,1)}, bf16[256,1152]{1,0:T(8,128)(2,1)S(1)}, bf16[256,1152]{1,0:T(8,128)(...) custom-call(bf16[256,1152]{1,0:T(8,128)(2,1)S(1)} %copy-done.5, ...), custom_call_target="tpu_custom_call" | custom-call | tf_op jit(solution)/shard_map/pallas_call | solution.py:642
  298.2 16.6 %collective-permute-done.39.refs_0_ = bf16[2,3,144,1152]{3,2,1,0:T(8,128)(2,1)} collective-permute-done((bf16[2,3,144,1152]{3,2,1,0:T(8,128)(2,1)}, bf16[2,3,144,1152]{3,2,1,0:T(8,128)(2,1)}, u32[]{:S(2)}, u32[]{:S(2)}) %collective-permute-start.39) | collective-permute-done | bytes 1990688 | tf_op jit(solution)/shard_map/ppermute | solution.py:39
  323.2 17.7 %collective-permute-done.41.refs_0_ = bf16[1,3,144,1152]{3,2,1,0:T(8,128)(2,1)} collective-permute-done((bf16[1,3,144,1152]{3,2,1,0:T(8,128)(2,1)}, bf16[1,3,144,1152]{3,2,1,0:T(8,128)(2,1)}, u32[]{:S(2)}, u32[]{:S(2)}) %collective-permute-start.41) | collective-permute-done | bytes 995360 | tf_op jit(solution)/shard_map/ppermute | solution.py:39
  347.9 23.6 %shard_map.268 = (bf16[1152,4608]{1,0:T(8,128)(2,1)}, bf16[4608,1152]{1,0:T(8,128)(2,1)}, f32[256,4608]{1,0:T(8,128)}, bf16[2,4,576,256]{3,2,1,0:T(8,128)(2,1)},...) custom-call(f32[256,1152]{1,0:T(8,128)} %get-tuple-element.155.refs_0_.refs_3_, bf16[256,1152]{1,0:T(8,128)(2,1)S(1)} %copy-done.36, ...), custom_call_target="tpu_custom_call" | custom-call | tf_op jit(solution)/shard_map/pallas_call | solution.py:682
  373.3 16.9 %shard_map.269 = (bf16[2,256,2304]{2,1,0:T(8,128)(2,1)}, f32[256,1152]{1,0:T(8,128)S(1)}, bf16[256,1152]{1,0:T(8,128)(2,1)S(1)}, f32[16,1152]{1,0:T(8,128)S(1)}) custom-call(bf16[256,1152]{1,0:T(8,128)(2,1)S(1)} %copy-done.62, bf16[256,1152]{1,0:T(8,128)(2,1)} %get-tuple-element.315.refs_1_.refs_2_, f32[6,1152]{1,0:T(8,128)S(1)} %reshape.339.refs_1_.refs_2_.refs_3_, ...), custom_call_target="tpu_custom_call" | custom-call | tf_op jit(solution)/shard_map/pallas_call | solution.py:762
  415.2 18.9 %shard_map.272 = (bf16[2,256,2304]{2,1,0:T(8,128)(2,1)}, f32[256,1152]{1,0:T(8,128)}, bf16[256,1152]{1,0:T(8,128)(2,1)S(1)}, bf16[16,1152]{1,0:T(8,128)(2,1)S(1)}) custom-call(bf16[256,1152]{1,0:T(8,128)(2,1)S(1)} %copy-done.5, f32[256,1152]{1,0:T(8,128)} %copy-done.66, bf16[256,1152]{1,0:T(8,128)(2,1)S(1)} %get-tuple-element.169.refs_2_, ...), custom_call_target="tpu_custom_call" | custom-call | tf_op jit(solution)/shard_map/pallas_call | solution.py:826
  455.7 16.7 %shard_map.275 = (bf16[2,256,2304]{2,1,0:T(8,128)(2,1)}, f32[256,1152]{1,0:T(8,128)S(1)}, bf16[256,1152]{1,0:T(8,128)(2,1)S(1)}, f32[16,1152]{1,0:T(8,128)S(1)}) custom-call(bf16[256,1152]{1,0:T(8,128)(2,1)S(1)} %get-tuple-element.180.refs_4_.refs_0_, bf16[256,1152]{1,0:T(8,128)(2,1)S(1)} %fusion.4.refs_1_.refs_2_, f32[6,1152]{1,0:T(8,128)S(1)} %copy-done.69, ...), custom_call_target="tpu_custom_call" | custom-call | tf_op jit(solution)/shard_map/pallas_call | solution.py:762
  501.4 9.0 %shard_map.279 = (bf16[2,2,144,1152]{3,2,1,0:T(8,128)(2,1)S(1)}, bf16[2,2,144,1152]{3,2,1,0:T(8,128)(2,1)}, bf16[2,2,144,1152]{3,2,1,0:T(8,128)(2,1)}, bf16[2,2,144,1152]{3,2,1,0:T(8,128)(2,1)}) custom-call(bf16[256,1152]{1,0:T(8,128)(2,1)} %get-tuple-element.141._.refs_1_.refs_0_, bf16[256,1152]{1,0:T(8,128)(2,1)} %get-tuple-element.199.refs_1_, ...), custom_call_target="tpu_custom_call" | custom-call | tf_op jit(solution)/shard_map/pallas_call | solution.py:434
  511.5 18.7 %shard_map.280 = (bf16[2,256,2304]{2,1,0:T(8,128)(2,1)}, f32[256,1152]{1,0:T(8,128)}, bf16[256,1152]{1,0:T(8,128)(2,1)S(1)}, bf16[16,1152]{1,0:T(8,128)(2,1)S(1)}) custom-call(bf16[256,1152]{1,0:T(8,128)(2,1)S(1)} %copy-done.31, f32[256,1152]{1,0:T(8,128)} %copy-done.65, bf16[256,1152]{1,0:T(8,128)(2,1)S(1)} %copy-done.93, f32[6,1152]{1,0:T(8,128)S(1)} %copy-done.69, ...), custom_call_target="tpu_custom_call" | custom-call | tf_op jit(solution)/shard_map/pallas_call | solution.py:826
  564.7 15.8 %collective-permute-done.70.refs_2_ = bf16[2,2,144,1152]{3,2,1,0:T(8,128)(2,1)S(1)} collective-permute-done((bf16[2,2,144,1152]{3,2,1,0:T(8,128)(2,1)}, bf16[2,2,144,1152]{3,2,1,0:T(8,128)(2,1)S(1)}, u32[]{:S(2)}, u32[]{:S(2)}) %collective-permute-start.70) | collective-permute-done | bytes 1327136 | tf_op jit(solution)/shard_map/ppermute | solution.py:39
  600.0 12.4 %all_to_all.54.refs_0_ = bf16[4,2,16,1152]{3,2,1,0:T(8,128)(2,1)} all-to-all(bf16[4,2,16,1152]{3,2,1,0:T(8,128)(2,1)S(1)} %stack.58), channel_id=1, replica_groups=mesh['section'=2,'shard'=4,'replica'=4] {'shard'}, dimensions={0} | all-to-all | bytes 589824 | tf_op jit(solution)/shard_map/all_to_all | solution.py:56
  621.2 28.2 %collective-permute-done.77.refs_2_ = bf16[2,2,144,1152]{3,2,1,0:T(8,128)(2,1)S(1)} collective-permute-done((bf16[2,2,144,1152]{3,2,1,0:T(8,128)(2,1)}, bf16[2,2,144,1152]{3,2,1,0:T(8,128)(2,1)S(1)}, u32[]{:S(2)}, u32[]{:S(2)}) %collective-permute-start.77) | collective-permute-done | bytes 1327136 | tf_op jit(solution)/shard_map/ppermute | solution.py:39
  675.2 21.5 %collective-permute-done.73.refs_2_ = bf16[2,2,144,1152]{3,2,1,0:T(8,128)(2,1)S(1)} collective-permute-done((bf16[2,2,144,1152]{3,2,1,0:T(8,128)(2,1)}, bf16[2,2,144,1152]{3,2,1,0:T(8,128)(2,1)S(1)}, u32[]{:S(2)}, u32[]{:S(2)}) %collective-permute-start.73) | collective-permute-done | bytes 1327136 | tf_op jit(solution)/shard_map/ppermute | solution.py:39
  726.6 18.9 %collective-permute-done.79.refs_0_ = bf16[1,4,2,16,1152]{4,3,2,1,0:T(8,128)(2,1)} collective-permute-done((bf16[1,4,2,16,1152]{4,3,2,1,0:T(8,128)(2,1)}, bf16[1,4,2,16,1152]{4,3,2,1,0:T(8,128)(2,1)}, u32[]{:S(2)}, u32[]{:S(2)}) %collective-permute-start.79) | collective-permute-done | bytes 294944 | tf_op jit(solution)/shard_map/ppermute | solution.py:39
  774.2 10.4 %collective-permute-done.83.refs_0_ = bf16[2,4,2,16,1152]{4,3,2,1,0:T(8,128)(2,1)} collective-permute-done((bf16[2,4,2,16,1152]{4,3,2,1,0:T(8,128)(2,1)S(1)}, bf16[2,4,2,16,1152]{4,3,2,1,0:T(8,128)(2,1)}, u32[]{:S(2)}, u32[]{:S(2)}) %collective-permute-start.83) | collective-permute-done | bytes 589856 | tf_op jit(solution)/shard_map/ppermute | solution.py:39
  795.1 11.3 %collective-permute-done.91.far = bf16[3,144,1152]{2,1,0:T(8,128)(2,1)} collective-permute-done((bf16[3,144,1152]{2,1,0:T(8,128)(2,1)}, bf16[3,144,1152]{2,1,0:T(8,128)(2,1)}, u32[]{:S(2)}, u32[]{:S(2)}) %collective-permute-start.91) | collective-permute-done | bytes 995360 | tf_op jit(solution)/shard_map/ppermute | solution.py:39
  827.4 9.0 %collective-permute-done.92.refs_0_ = bf16[3,2,144,1152]{3,2,1,0:T(8,128)(2,1)} collective-permute-done((bf16[3,2,144,1152]{3,2,1,0:T(8,128)(2,1)}, bf16[3,2,144,1152]{3,2,1,0:T(8,128)(2,1)}, u32[]{:S(2)}, u32[]{:S(2)}) %collective-permute-start.92) | collective-permute-done | bytes 1990688 | tf_op jit(solution)/shard_map/ppermute | solution.py:39
  (691 shorter events, 452.4 us)
Async XLA Ops:
  7.2 47.7 %all-gather.9.cloned.1.call-start = ((), (), s32[]{:S(2)}) async-start(), calls=%async_computation.10 | async-start | bytes 1658880 | tf_op jit(solution)/shard_map/all_gather | solution.py:346
  26.5 110.5 %all-gather.11.cloned.1.call-start = ((), (), s32[]{:S(2)}) async-start(), calls=%async_computation.11 | async-start | bytes 3317760 | tf_op jit(solution)/shard_map/all_gather | solution.py:346
  68.0 125.6 %all-gather.13.cloned.1.call-start = ((), (), s32[]{:S(2)}) async-start(), calls=%async_computation.12 | async-start | bytes 1658880 | tf_op jit(solution)/shard_map/all_gather | solution.py:346
  113.3 151.7 %all-gather.15.cloned.1.call-start = ((), (), s32[]{:S(2)}) async-start(), calls=%async_computation.13 | async-start | bytes 3317760 | tf_op jit(solution)/shard_map/all_gather | solution.py:346
  140.3 46.0 %collective-permute-start.17 = (bf16[2,3,144,1152]{3,2,1,0:T(8,128)(2,1)}, bf16[2,3,144,1152]{3,2,1,0:T(8,128)(2,1)}, u32[]{:S(2)}, u32[]{:S(2)}) collective-permute-start(bf16[2,3,144,1152]{3,2,1,0:T(8,128)(2,1)} %shard_map.252.refs_2_.refs_5_), channel_id=1, source_target_pairs={{0,1},{1,0},{2,3},{3,2},{4,5},{5,4},{6,7},{7,6},{8,9},{9,8},{10,11... | collective-permute-start | bytes 5971976 | tf_op jit(solution)/shard_map/ppermute | solution.py:39
  141.8 45.7 %collective-permute-start.18 = (bf16[2,3,144,1152]{3,2,1,0:T(8,128)(2,1)}, bf16[2,3,144,1152]{3,2,1,0:T(8,128)(2,1)}, u32[]{:S(2)}, u32[]{:S(2)}) collective-permute-start(bf16[2,3,144,1152]{3,2,1,0:T(8,128)(2,1)} %shard_map.252.refs_2_.refs_5_), channel_id=1, source_target_pairs={{0,2},{1,3},{2,0},{3,1},{4,6},{5,7},{6,4},{7,5},{8,10},{9,11},{10,... | collective-permute-start | bytes 5971976 | tf_op jit(solution)/shard_map/ppermute | solution.py:39
  269.5 45.3 %collective-permute-start.39 = (bf16[2,3,144,1152]{3,2,1,0:T(8,128)(2,1)}, bf16[2,3,144,1152]{3,2,1,0:T(8,128)(2,1)}, u32[]{:S(2)}, u32[]{:S(2)}) collective-permute-start(bf16[2,3,144,1152]{3,2,1,0:T(8,128)(2,1)} %shard_map.261.refs_2_.refs_5_), channel_id=1, source_target_pairs={{0,1},{1,0},{2,3},{3,2},{4,5},{5,4},{6,7},{7,6},{8,9},{9,8},{10,11... | collective-permute-start | bytes 5971976 | tf_op jit(solution)/shard_map/ppermute | solution.py:39
  271.0 45.0 %collective-permute-start.40 = (bf16[2,3,144,1152]{3,2,1,0:T(8,128)(2,1)}, bf16[2,3,144,1152]{3,2,1,0:T(8,128)(2,1)}, u32[]{:S(2)}, u32[]{:S(2)}) collective-permute-start(bf16[2,3,144,1152]{3,2,1,0:T(8,128)(2,1)} %shard_map.261.refs_2_.refs_5_), channel_id=1, source_target_pairs={{0,2},{1,3},{2,0},{3,1},{4,6},{5,7},{6,4},{7,5},{8,10},{9,11},{10,... | collective-permute-start | bytes 5971976 | tf_op jit(solution)/shard_map/ppermute | solution.py:39
  297.8 47.7 %collective-permute-start.44 = (bf16[2,3,144,1152]{3,2,1,0:T(8,128)(2,1)}, bf16[2,3,144,1152]{3,2,1,0:T(8,128)(2,1)}, u32[]{:S(2)}, u32[]{:S(2)}) collective-permute-start(bf16[2,3,144,1152]{3,2,1,0:T(8,128)(2,1)} %shard_map.261.refs_2_.refs_5_), channel_id=1, source_target_pairs={{0,16},{1,17},{2,18},{3,19},{4,20},{5,21},{6,22},{7,23},{8,24},{9,... | collective-permute-start | bytes 5971976 | tf_op jit(solution)/shard_map/ppermute | solution.py:39
  435.6 48.3 %collective-permute-start.59 = (bf16[2,2,144,1152]{3,2,1,0:T(8,128)(2,1)}, bf16[2,2,144,1152]{3,2,1,0:T(8,128)(2,1)}, u32[]{:S(2)}, u32[]{:S(2)}) collective-permute-start(bf16[2,2,144,1152]{3,2,1,0:T(8,128)(2,1)} %get-tuple-element.205), channel_id=1, source_target_pairs={{0,1},{1,0},{2,3},{3,2},{4,5},{5,4},{6,7},{7,6},{8,9},{9,8},{10,11... | collective-permute-start | bytes 3981320 | tf_op jit(solution)/shard_map/ppermute | solution.py:39
  436.3 47.6 %collective-permute-start.60 = (bf16[2,2,144,1152]{3,2,1,0:T(8,128)(2,1)}, bf16[2,2,144,1152]{3,2,1,0:T(8,128)(2,1)}, u32[]{:S(2)}, u32[]{:S(2)}) collective-permute-start(bf16[2,2,144,1152]{3,2,1,0:T(8,128)(2,1)} %get-tuple-element.206), channel_id=1, source_target_pairs={{0,2},{1,3},{2,0},{3,1},{4,6},{5,7},{6,4},{7,5},{8,10},{9,11},{10,... | collective-permute-start | bytes 3981320 | tf_op jit(solution)/shard_map/ppermute | solution.py:39
  442.5 46.6 %collective-permute-start.57 = (bf16[2,144,1152]{2,1,0:T(8,128)(2,1)}, bf16[2,144,1152]{2,1,0:T(8,128)(2,1)S(1)}, u32[]{:S(2)}, u32[]{:S(2)}) collective-permute-start(bf16[2,144,1152]{2,1,0:T(8,128)(2,1)} %get-tuple-element.202), channel_id=1, source_target_pairs={{0,2},{1,3},{2,0},{3,1},{4,6},{5,7},{6,4},{7,5},{8,10},{9,11},{10,... | collective-permute-start | bytes 1990664 | tf_op jit(solution)/shard_map/ppermute | solution.py:39
  444.2 45.0 %collective-permute-start.58 = (bf16[2,144,1152]{2,1,0:T(8,128)(2,1)S(1)}, bf16[2,144,1152]{2,1,0:T(8,128)(2,1)S(1)}, u32[]{:S(2)}, u32[]{:S(2)}) collective-permute-start(bf16[2,144,1152]{2,1,0:T(8,128)(2,1)S(1)} %get-tuple-element.203), channel_id=1, source_target_pairs={{0,1},{1,0},{2,3},{3,2},{4,5},{5,4},{6,7},{7,6},{8,9},{9,8},{10,11... | collective-permute-start | bytes 1990664 | tf_op jit(solution)/shard_map/ppermute | solution.py:39
  491.4 52.0 %all-to-all-start.3 = ((bf16[4,144,1152]{2,1,0:T(8,128)(2,1)}), bf16[4,144,1152]{2,1,0:T(8,128)(2,1)}, u32[]{:S(2)}, u32[]{:S(2)}) async-start(bf16[4,144,1152]{2,1,0:T(8,128)(2,1)} %shard_map.278.refs_4_), calls=%async_computation.3 | async-start | bytes 2654208 | tf_op jit(solution)/shard_map/all_to_all | solution.py:56
  498.3 42.9 %collective-permute-start.64 = (bf16[2,144,1152]{2,1,0:T(8,128)(2,1)S(1)}, bf16[2,144,1152]{2,1,0:T(8,128)(2,1)S(1)}, u32[]{:S(2)}, u32[]{:S(2)}) collective-permute-start(bf16[2,144,1152]{2,1,0:T(8,128)(2,1)S(1)} %copy-done.105), channel_id=1, source_target_pairs={{0,2},{1,3},{2,0},{3,1},{4,6},{5,7},{6,4},{7,5},{8,10},{9,11},{10,... | collective-permute-start | bytes 1990664 | tf_op jit(solution)/shard_map/ppermute | solution.py:39
  500.0 41.2 %collective-permute-start.65 = (bf16[2,144,1152]{2,1,0:T(8,128)(2,1)S(1)}, bf16[2,144,1152]{2,1,0:T(8,128)(2,1)S(1)}, u32[]{:S(2)}, u32[]{:S(2)}) collective-permute-start(bf16[2,144,1152]{2,1,0:T(8,128)(2,1)S(1)} %copy-done.103), channel_id=1, source_target_pairs={{0,1},{1,0},{2,3},{3,2},{4,5},{5,4},{6,7},{7,6},{8,9},{9,8},{10,11... | collective-permute-start | bytes 1990664 | tf_op jit(solution)/shard_map/ppermute | solution.py:39
  543.4 51.5 %all-to-all-start.2 = ((bf16[4,144,1152]{2,1,0:T(8,128)(2,1)}), bf16[4,144,1152]{2,1,0:T(8,128)(2,1)}, u32[]{:S(2)}, u32[]{:S(2)}) async-start(bf16[4,144,1152]{2,1,0:T(8,128)(2,1)} %shard_map.282._), calls=%async_computation.2 | async-start | bytes 2654208 | tf_op jit(solution)/shard_map/all_to_all | solution.py:56
  551.3 41.4 %collective-permute-start.68 = (bf16[2,144,1152]{2,1,0:T(8,128)(2,1)}, bf16[2,144,1152]{2,1,0:T(8,128)(2,1)S(1)}, u32[]{:S(2)}, u32[]{:S(2)}) collective-permute-start(bf16[2,144,1152]{2,1,0:T(8,128)(2,1)} %copy-done.108), channel_id=1, source_target_pairs={{0,2},{1,3},{2,0},{3,1},{4,6},{5,7},{6,4},{7,5},{8,10},{9,11},{10,... | collective-permute-start | bytes 1990664 | tf_op jit(solution)/shard_map/ppermute | solution.py:39
  554.4 44.1 %collective-permute-start.63 = (bf16[16,1152]{1,0:T(8,128)(2,1)}, bf16[16,1152]{1,0:T(8,128)(2,1)S(1)}, u32[]{:S(2)}, u32[]{:S(2)}) collective-permute-start(bf16[16,1152]{1,0:T(8,128)(2,1)} %broadcast_select_fusion.2), channel_id=1, source_target_pairs={{0,16},{1,17},{2,18},{3,19},{4,20},{5,21},{6,22},{7,23},{8,24},{9,... | collective-permute-start | bytes 110600 | tf_op jit(solution)/shard_map/ppermute | solution.py:39
  612.4 47.8 %all-to-all-start.5 = ((bf16[4,144,1152]{2,1,0:T(8,128)(2,1)}), bf16[4,144,1152]{2,1,0:T(8,128)(2,1)}, u32[]{:S(2)}, u32[]{:S(2)}) async-start(bf16[4,144,1152]{2,1,0:T(8,128)(2,1)} %shard_map.286._), calls=%async_computation.5 | async-start | bytes 2654208 | tf_op jit(solution)/shard_map/all_to_all | solution.py:56
  618.1 39.8 %collective-permute-start.75 = (bf16[2,144,1152]{2,1,0:T(8,128)(2,1)}, bf16[2,144,1152]{2,1,0:T(8,128)(2,1)S(1)}, u32[]{:S(2)}, u32[]{:S(2)}) collective-permute-start(bf16[2,144,1152]{2,1,0:T(8,128)(2,1)} %copy-done.110), channel_id=1, source_target_pairs={{0,2},{1,3},{2,0},{3,1},{4,6},{5,7},{6,4},{7,5},{8,10},{9,11},{10,... | collective-permute-start | bytes 1990664 | tf_op jit(solution)/shard_map/ppermute | solution.py:39
  660.2 55.8 %all-to-all-start.6 = ((bf16[4,144,1152]{2,1,0:T(8,128)(2,1)}), bf16[4,144,1152]{2,1,0:T(8,128)(2,1)}, u32[]{:S(2)}, u32[]{:S(2)}) async-start(bf16[4,144,1152]{2,1,0:T(8,128)(2,1)} %shard_map.290._), calls=%async_computation.6 | async-start | bytes 2654208 | tf_op jit(solution)/shard_map/all_to_all | solution.py:56
  672.8 40.4 %collective-permute-start.80 = (bf16[2,144,1152]{2,1,0:T(8,128)(2,1)}, bf16[2,144,1152]{2,1,0:T(8,128)(2,1)}, u32[]{:S(2)}, u32[]{:S(2)}) collective-permute-start(bf16[2,144,1152]{2,1,0:T(8,128)(2,1)} %get-tuple-element.242), channel_id=1, source_target_pairs={{0,2},{1,3},{2,0},{3,1},{4,6},{5,7},{6,4},{7,5},{8,10},{9,11},{10,... | collective-permute-start | bytes 1990664 | tf_op jit(solution)/shard_map/ppermute | solution.py:39
  771.2 43.0 %collective-permute-start.62 = (f32[256,1152]{1,0:T(8,128)}, f32[256,1152]{1,0:T(8,128)}, u32[]{:S(2)}, u32[]{:S(2)}) collective-permute-start(f32[256,1152]{1,0:T(8,128)} %convert_select_fusion), channel_id=1, source_target_pairs={{0,16},{1,17},{2,18},{3,19},{4,20},{5,21},{6,22},{7,23},{8,24},{9,... | collective-permute-start | bytes 3538952 | tf_op jit(solution)/shard_map/ppermute | solution.py:39
  (236 other events, 2661.0 us)
Sparse Core Ops, SparseCore 0:
  19.3 35.5 all-gather.8
  57.0 58.9 all-gather.10
  118.2 31.6 all-gather.12
  151.3 54.3 all-gather.14

commit v3 on v2

--- a/solution.py
+++ b/solution.py
@@ -75,6 +75,10 @@
 
 
 def cost(nbytes, flops=0):
+    return pl.CostEstimate(flops=flops, bytes_accessed=nbytes, transcendentals=0)
+
+
+def free():
     return pl.CostEstimate(flops=0, bytes_accessed=0, transcendentals=0)
 
 
@@ -86,7 +90,7 @@
         in_specs=[ANYWHERE] * (n + 1),
         out_specs=(ANYWHERE,) * n,
         input_output_aliases={i: i for i in range(n)},
-        cost_estimate=cost(0),
+        cost_estimate=free(),
     )(*arrays, after)
 
 
@@ -109,6 +113,56 @@
     )(every, after)
 
 
+def collect_kernel(p0, p1, p2, _, big, to_x, to_y):
+    n = p0.shape[0]
+    for m, part in enumerate((p0, p1, p2)):
+        big[m] = part[...]
+    if n == 2:
+        to_x[...] = p2[:1]
+        to_y[...] = p1[1:]
+    else:
+        to_x[...] = p2[:, :1]
+        to_y[...] = p1[:, 1:]
+
+
+def collected(p0, p1, p2, after):
+    n = p0.shape[0]
+    if n == 2:
+        cut = (1, 3), (1, 3)
+    else:
+        cut = (1, 1), (1, 2)
+    shapes = ((3, n, 3), *cut)
+    return pl.pallas_call(
+        collect_kernel,
+        out_shape=tuple(jax.ShapeDtypeStruct((*s, PIECE, D), BF) for s in shapes),
+        in_specs=[INSIDE] * 3 + [ANYWHERE],
+        out_specs=(INSIDE,) * 3,
+        compiler_params=PARAMS,
+        cost_estimate=cost(1),
+    )(p0, p1, p2, after)
+
+
+def combine_kernel(pa, pb, _, out):
+    if out.shape[0] == 2:
+        out[:1] = pa[...]
+        out[1:] = pb[...]
+    else:
+        out[:, :1] = pa[...]
+        out[:, 1:] = pb[...]
+
+
+def combined(pa, pb, after):
+    n = 2 if pa.shape[1] == 3 else 1
+    return pl.pallas_call(
+        combine_kernel,
+        out_shape=jax.ShapeDtypeStruct((n, 3, PIECE, D), BF),
+        in_specs=[INSIDE] * 2 + [ANYWHERE],
+        out_specs=INSIDE,
+        compiler_params=PARAMS,
+        cost_estimate=cost(1),
+    )(pa, pb, after)
+
+
 def join_kernel(*refs):
     out = refs[-1]
     for i in range(out.shape[0]):
@@ -123,7 +177,7 @@
         in_specs=[INSIDE] * n + [ANYWHERE],
         out_specs=INSIDE,
         compiler_params=PARAMS,
-        cost_estimate=cost(4 * n * PIECE * D),
+        cost_estimate=free(),
     )(*parts, after)
 
 
@@ -144,44 +198,70 @@
         in_specs=[INSIDE] * (2 * n) + [ANYWHERE],
         out_specs=(INSIDE,) * (2 * n),
         compiler_params=PARAMS,
-        cost_estimate=cost(6 * sum(v.size for v in a)),
+        cost_estimate=free(),
     )(*a, *b, after)
 
 
-def merge_kernel(*refs):
+def merge_kernel(n, *refs):
     out = refs[-1]
-    for i in range(2):
-        whole = refs[i][...].astype(F32) + refs[2 + i][...].astype(F32)
-        out[2 * i : 2 * i + 2] = whole.astype(BF)
+    for i in range(n):
+        whole = refs[i][...].astype(F32) + refs[n + i][...].astype(F32)
+        rows = refs[i].shape[0]
+        out[i * rows : (i + 1) * rows] = whole.astype(BF)
 
 
 def merged(a, b, after):
-    return pl.pallas_call(
-        merge_kernel,
+    n = len(a)
+    return pl.pallas_call(
+        functools.partial(merge_kernel, n),
         out_shape=jax.ShapeDtypeStruct((NZ, PIECE, D), BF),
-        in_specs=[INSIDE] * 4 + [ANYWHERE],
+        in_specs=[INSIDE] * (2 * n) + [ANYWHERE],
         out_specs=INSIDE,
         compiler_params=PARAMS,
-        cost_estimate=cost(12 * NZ * PIECE * D),
+        cost_estimate=free(),
     )(*a, *b, after)
 
 
-def sum_kernel(parts, _, out):
+def sum_kernel(n, *refs):
+    if n == 1:
+        parts = [refs[0][i] for i in range(refs[0].shape[0])]
+    else:
+        parts = [ref[...] for ref in refs[:n]]
     whole = parts[0].astype(F32)
-    for i in range(1, parts.shape[0]):
-        whole = whole + parts[i].astype(F32)
-    out[...] = whole.astype(BF)
+    for part in parts[1:]:
+        whole = whole + part.astype(F32)
+    refs[-1][...] = whole.astype(BF)
 
 
 def summed(parts, after):
-    n = parts.shape[0]
-    return pl.pallas_call(
-        sum_kernel,
+    n = len(parts)
+    return pl.pallas_call(
+        functools.partial(sum_kernel, n),
         out_shape=ONE,
+        in_specs=[INSIDE] * n + [ANYWHERE],
+        out_specs=INSIDE,
+        compiler_params=PARAMS,
+        cost_estimate=free(),
+    )(*parts, after)
+
+
+def fold_kernel(parts, _, keep, send):
+    for m in range(4):
+        whole = parts[0, m].astype(F32)
+        for i in SHARDS:
+            whole = whole + parts[i, m].astype(F32)
+        (send if m % 2 else keep)[m // 2] = whole.astype(BF)
+
+
+def folded(parts, after):
+    half = jax.ShapeDtypeStruct((2, PIECE, D), BF)
+    return pl.pallas_call(
+        fold_kernel,
+        out_shape=(half, half),
         in_specs=[INSIDE, ANYWHERE],
-        out_specs=INSIDE,
-        compiler_params=PARAMS,
-        cost_estimate=cost(2 * (n + 1) * PIECE * D),
+        out_specs=(INSIDE, INSIDE),
+        compiler_params=PARAMS,
+        cost_estimate=free(),
     )(parts, after)
 
 
@@ -191,7 +271,7 @@
 
         @pl.when(c == core)
         def _():
-            for i in range(3):
+            for i in range(own.shape[0]):
                 out[i, core] = own[i]
                 out[i, 1 - core] = far[i]
 
@@ -199,11 +279,11 @@
 def paired(own, far, after):
     return pl.pallas_call(
         pair_kernel,
-        out_shape=jax.ShapeDtypeStruct((3, 2, PIECE, D), BF),
+        out_shape=jax.ShapeDtypeStruct((own.shape[0], 2, PIECE, D), BF),
         in_specs=[INSIDE] * 2 + [ANYWHERE],
         out_specs=INSIDE,
         compiler_params=PARAMS,
-        cost_estimate=cost(24 * PIECE * D),
+        cost_estimate=free(),
     )(own, far, after)
 
 
@@ -310,13 +390,9 @@
                     col = pl.multiple_of((core * 2 + high) * D, D)
                     spot = out.at[pl.ds(row, PIECE), pl.ds(col, D)]
                 if m < 3:
-                    piece = group[m].at[index, k - 1]
-                elif own[0].shape[0] == 2:
-                    piece = group[3 + index].at[0, k - 1]
-                elif k == 1:
-                    piece = group[3].at[0, 0]
+                    piece = group[0].at[m, index, k - 1]
                 else:
-                    piece = group[4].at[0, k - 2]
+                    piece = group[1].at[index, k - 1]
                 sem = sems.at[2 + (side * 4 + m) * 3 + k - 1]
                 copies.append(pltpu.make_async_copy(piece, spot, sem))
     for copy in copies:
@@ -348,21 +424,18 @@
     def stack(self, g):
         p0 = stacked(self.state[g], self.after)
         self.after = p0
-        self.state[g] = p0, cross(p0, 1), cross(p0, 2), swap(p0)
+        self.state[g] = p0, cross(p0, 1), cross(p0, 2)
 
     def onward(self, g):
-        p0, p1, p2, f0 = self.state[g]
-        p1, p2 = fence((p1, p2), self.after)
-        self.after = p1
-        part = (p2[:1], p1[1:]) if len(GROUPS[g]) == 2 else (p2[:, :1], p1[:, 1:])
-        p3 = cross(part[0], 1), cross(part[1], 2)
-        self.state[g] = (p0, p1, p2), p3, (f0, swap(p1), swap(p2))
+        big, to_x, to_y = collected(*self.state[g], self.after)
+        self.after = to_x
+        self.state[g] = big, (cross(to_x, 1), cross(to_y, 2)), swap(big)
 
     def share(self, g):
-        own, p3, far = self.state[g]
-        p3 = fence(p3, self.after)
-        self.after = p3[0]
-        self.state[g] = own + tuple(p3), far + tuple(swap(p) for p in p3)
+        big, p3, far = self.state[g]
+        p3 = combined(*p3, self.after)
+        self.after = p3
+        self.state[g] = (big, p3), (far, swap(p3))
 
     def hold(self, *values):
         values = fence(values, self.after)
@@ -381,10 +454,11 @@
     return lax.dot_general(a, b, (((0,), (0,)), ((), ())), preferred_element_type=F32)
 
 
-def wgrad_kernel(kind, *refs):
+def wgrad_kernel(kind, mode, *refs):
     n = 4
     ins = refs[:n]
-    keep_x, send_x, keep_y, send_y, acc = refs[n + 1 :]
+    outs = refs[n + 1 : -1]
+    acc = refs[-1]
     c, z, r = place()
     for g in range(2):
         u = lax.rem(g + r // 2, 2)
@@ -423,90 +497,102 @@
                         start = (zp * 2 + h) * PIECE
                         piece = acc[start : start + PIECE, :].astype(BF)
                         low = h ^ par
-                        if zp < 2:
-                            (send_x if low else keep_x)[g, zp] = piece
+                        if mode == 0:
+                            outs[0][zp, g * 2 + low] = piece
+                        elif mode == 1:
+                            outs[low][g, zp] = piece
+                        elif mode == 2:
+                            outs[g][low, zp] = piece
+                        elif zp < 2:
+                            outs[low][g, zp] = piece
                         else:
-                            (send_y if g else keep_y)[low, zp - 2] = piece
-
-
-def wgrad(kind, operands, after):
-    part = jax.ShapeDtypeStruct((2, 2, PIECE, D), BF)
-    return pl.pallas_call(
-        functools.partial(wgrad_kernel, kind),
-        out_shape=(part,) * 4,
+                            outs[2 + g][low, zp - 2] = piece
+
+
+def wgrad(kind, mode, operands, after):
+    leading = ((4, 4), (2, 4), (2, 4), (2, 2))[mode]
+    count = (1, 2, 2, 4)[mode]
+    part = jax.ShapeDtypeStruct((*leading, PIECE, D), BF)
+    return pl.pallas_call(
+        functools.partial(wgrad_kernel, kind, mode),
+        out_shape=(part,) * count,
         in_specs=[INSIDE] * len(operands) + [ANYWHERE],
-        out_specs=(INSIDE,) * 4,
+        out_specs=(INSIDE,) * count,
         scratch_shapes=[pltpu.VMEM((D, D), F32)],
         compiler_params=PARAMS,
-        cost_estimate=cost(2 * D * HALF + 6 * 512 * D, 2 * 512 * D * HALF),
+        cost_estimate=free(),
     )(*operands, after)
 
 
-def finish_kernel(block, *refs):
+def finish_kernel(block, kinds, *refs):
+    count = len(kinds)
+    outs = list(refs[-4 - count - (0 in kinds) : -4])
+    raw, acc, sems_in, sems_out = refs[-4:]
     p0, p1, p2, pa, pb = refs[:5]
-    outs = refs[-8:-4]
-    raw, acc, sems_in, sems_out = refs[-4:]
     c, z, r = place()
 
     @pl.when(c == block)
     def _():
-        copies = {}
-        for kind in range(3):
+        copies = []
+        for i in range(count):
             for core in range(2):
-                flat = kind * 2 + core
-                last = pa.at[flat] if flat < 3 else pb.at[flat - 3]
-                for m, piece in enumerate((p0.at[kind, core], p1.at[kind, core], p2.at[kind, core], last)):
+                flat = i * 2 + core
+                last = pa.at[flat] if flat < count else pb.at[flat - count]
+                sources = (p0.at[i, core], p1.at[i, core], p2.at[i, core], last)
+                for m, piece in enumerate(sources):
                     n = flat * 4 + m
-                    copy = pltpu.make_async_copy(piece, raw.at[n], sems_in.at[n])
-                    copy.start()
-                    copies[n] = copy
+                    copies.append(pltpu.make_async_copy(piece, raw.at[n], sems_in.at[n]))
+                    copies[-1].start()
         done = []
-        for kind in range(3):
+        at_out = 0
+        for i, kind in enumerate(kinds):
+            base = i * 4 * ROWS
             for core in range(2):
                 for m in range(4):
-                    n = (kind * 2 + core) * 4 + m
+                    n = (i * 2 + core) * 4 + m
                     copies[n].wait()
                     low = lax.rem(r + m, 2)
                     unit = core * 2 + lax.rem(r // 2 + m // 2, 2)
-                    piece = raw[n].astype(F32)
-                    if kind == 2:
-                        at = pl.multiple_of((unit * 2 + low) * PIECE, PIECE)
-                        acc[pl.ds(2 * 4 * ROWS + at, PIECE), :] = piece
+                    at = pl.multiple_of(base + unit * ROWS + low * PIECE, PIECE)
+                    acc[pl.ds(at, PIECE), :] = raw[n].astype(F32)
+            if kind == 2:
+                moves = [(acc.at[base : base + D, :], outs[at_out])]
+            else:
+                moves = []
+                for unit in range(4):
+                    source = acc.at[base + unit * ROWS : base + (unit + 1) * ROWS, :]
+                    if kind == 0 and unit == 3:
+                        moves.append((source, outs[at_out + 1]))
                     else:
-                        at = pl.multiple_of((kind * 4 + unit) * ROWS + low * PIECE, PIECE)
-                        acc[pl.ds(at, PIECE), :] = piece
-            if kind == 2:
-                done.append(pltpu.make_async_copy(acc.at[8 * ROWS :, :], outs[3], sems_out.at[8]))
-                done[-1].start()
-                continue
-            for unit in range(4):
-                source = acc.at[(kind * 4 + unit) * ROWS : (kind * 4 + unit + 1) * ROWS, :]
-                if kind == 0 and unit == 3:
-                    target = outs[1]
-                else:
-                    target = outs[0 if kind == 0 else 2].at[:, unit * D : (unit + 1) * D]
-                done.append(pltpu.make_async_copy(source, target, sems_out.at[kind * 4 + unit]))
+                        cols = outs[at_out].at[:, unit * D : (unit + 1) * D]
+                        moves.append((source, cols))
+            at_out += 2 if kind == 0 else 1
+            for source, target in moves:
+                done.append(pltpu.make_async_copy(source, target, sems_out.at[len(done)]))
                 done[-1].start()
         for copy in done:
             copy.wait()
 
 
-def finish(block, pieces, before, after):
-    shapes = ((ROWS, 3 * D), (ROWS, D), (ROWS, FF), (D, D))
-    return pl.pallas_call(
-        functools.partial(finish_kernel, block),
+def finish(block, kinds, pieces, before, after):
+    shapes = []
+    for kind in kinds:
+        shapes += [[(ROWS, 3 * D), (ROWS, D)], [(ROWS, FF)], [(D, D)]][kind]
+    count = len(kinds)
+    return pl.pallas_call(
+        functools.partial(finish_kernel, block, kinds),
         out_shape=tuple(jax.ShapeDtypeStruct(s, F32) for s in shapes),
         in_specs=[ANYWHERE] * (6 + len(before)),
-        out_specs=(ANYWHERE,) * 4,
+        out_specs=(ANYWHERE,) * len(shapes),
         scratch_shapes=[
-            pltpu.VMEM((24, PIECE, D), BF),
-            pltpu.VMEM((12 * ROWS, D), F32),
-            pltpu.SemaphoreType.DMA((24,)),
-            pltpu.SemaphoreType.DMA((9,)),
+            pltpu.VMEM((8 * count, PIECE, D), BF),
+            pltpu.VMEM((4 * count * ROWS, D), F32),
+            pltpu.SemaphoreType.DMA((8 * count,)),
+            pltpu.SemaphoreType.DMA((12,)),
         ],
         input_output_aliases={6 + i: i for i in range(len(before))},
         compiler_params=PARAMS,
-        cost_estimate=cost(8 * ROWS * FF),
+        cost_estimate=free(),
     )(*pieces, after, *before)
 
 
@@ -518,57 +604,87 @@
     def __init__(self, after):
         self.after = after
         self.items = []
+        self.modes = []
         self.state = []
         self.own = {}
         self.ready = {}
-        self.results = ()
-
-    def begin(self, block, kind, operands):
-        keep_x, send_x, keep_y, send_y = wgrad(kind, operands, self.after)
-        self.after = keep_x
+        self.results = {}
+
+    def begin(self, block, kind, mode, operands):
+        out = wgrad(kind, mode, operands, self.after)
+        self.after = out[0]
         self.items.append((block, kind))
-        self.state.append(((keep_x, keep_y), (cross(send_x, 1), cross(send_y, 2))))
+        self.modes.append(mode)
+        if mode == 0:
+            self.state.append(trade(out[0]))
+        elif mode < 3:
+            self.state.append(((out[0],), (cross(out[1], mode),)))
+        else:
+            keep_x, send_x, keep_y, send_y = out
+            self.state.append(((keep_x, keep_y), (cross(send_x, 1), cross(send_y, 2))))
 
     def first(self, i):
-        xk, xs, yk, ys = plus(*self.state[i], self.after)
-        self.after = xk
-        self.state[i] = (xk, yk), (cross(xs, 2), cross(ys, 1))
+        mode = self.modes[i]
+        if mode == 0:
+            keep, send = folded(self.state[i], self.after)
+            self.after = keep
+            self.state[i] = (keep,), (cross(send, 1),)
+            return
+        out = plus(*self.state[i], self.after)
+        self.after = out[0]
+        if mode < 3:
+            self.state[i] = (out[0],), (cross(out[1], 3 - mode),)
+        else:
+            xk, xs, yk, ys = out
+            self.state[i] = (xk, yk), (cross(xs, 2), cross(ys, 1))
 
     def second(self, i):
+        if self.modes[i] == 0:
+            keep, send = plus(*self.state[i], self.after)
+            self.after = keep
+            self.state[i] = keep, cross(send, 2)
+            return
         f = merged(*self.state[i], self.after)
         self.after = f
-        self.state[i] = trade(f)
+        self.state[i] = (trade(f),)
 
     def third(self, i):
         v = summed(self.state[i], self.after)
         bit = 4
         while bit < lax.axis_size(R):
-            v = summed(jnp.stack([v, cross(v, bit)]), v)
+            v = summed((v, cross(v, bit)), v)
             bit *= 2
         self.after = v
         self.own[self.items[i]] = v
 
-    def unite(self, block):
-        own = joined([self.own[block, kind] for kind in range(3)], self.after)
+    def unite(self, block, kinds):
+        own = joined([self.own[block, kind] for kind in kinds], self.after)
         self.after = own
-        self.ready[block] = own, to_core(own, block)
-
-    def spread(self, block):
-        p0 = paired(*self.ready[block], self.after)
+        self.ready[block, kinds] = own, to_core(own, block)
+
+    def spread(self, block, kinds):
+        p0 = paired(*self.ready[block, kinds], self.after)
         self.after = p0
-        self.ready[block] = p0, on_core(p0, 1, block), on_core(p0, 2, block)
-
-    def spread_on(self, block):
-        p0, p1, p2 = self.ready[block]
+        self.ready[block, kinds] = p0, on_core(p0, 1, block), on_core(p0, 2, block)
+
+    def spread_on(self, block, kinds):
+        p0, p1, p2 = self.ready[block, kinds]
         p1, p2 = fence((p1, p2), self.after)
         self.after = p1
-        flat1, flat2 = p1.reshape(6, PIECE, D), p2.reshape(6, PIECE, D)
-        pa, pb = on_core(flat2[:3], 1, block), on_core(flat1[3:], 2, block)
-        self.ready[block] = p0, p1, p2, pa, pb
-
-    def finish(self, block):
-        self.results = finish(block, self.ready[block], self.results, self.after)
-        self.after = self.results[0]
+        n = len(kinds)
+        flat1, flat2 = p1.reshape(2 * n, PIECE, D), p2.reshape(2 * n, PIECE, D)
+        pa, pb = on_core(flat2[:n], 1, block), on_core(flat1[n:], 2, block)
+        self.ready[block, kinds] = p0, p1, p2, pa, pb
+
+    def finish(self, block, kinds):
+        before = []
+        for kind in kinds:
+            before += self.results.get(kind, [])
+        out = list(finish(block, kinds, self.ready[block, kinds], before, self.after))
+        self.after = out[0]
+        for kind in kinds:
+            n = 2 if kind == 0 else 1
+            self.results[kind], out = out[:n], out[n:]
 
     def hold(self, *values):
         values = fence(values, self.after)
@@ -611,8 +727,8 @@
 
 def attend_kernel(block, *refs):
     x, ada, qv_bias, proj_bias = refs[:4]
-    own, far, mine, other = refs[4:9], refs[9:14], refs[14:16], refs[16:18]
-    w_out, sides, q, k, v, attended, mid, mlp_in, w, sems = refs[19:]
+    own, far, mine, other = refs[4:6], refs[6:8], refs[8:10], refs[10:12]
+    w_out, sides, q, k, v, attended, mid, mlp_in, w, sems = refs[13:]
     attn_in, mixed = sides.at[0], sides.at[1]
     wait = weight_copies(block, 0, 0, mine, other, own, far, w, sems)
     xf = x[...].astype(F32)
@@ -642,7 +758,7 @@
     return pl.pallas_call(
         functools.partial(attend_kernel, block),
         out_shape=(shape_of(BF, D, FF), shape_of(BF, 2, t, D), low, low, low, high, high, low),
-        in_specs=[INSIDE] * 4 + [ANYWHERE] * 15,
+        in_specs=[INSIDE] * 4 + [ANYWHERE] * 9,
         out_specs=(ANYWHERE,) + (INSIDE,) * 7,
         scratch_shapes=[pltpu.VMEM((D, FF), BF), pltpu.SemaphoreType.DMA((27,))],
         compiler_params=PARAMS,
@@ -652,10 +768,10 @@
 
 def mlp_kernel(block, *refs):
     mid, mlp_in, ada, up_bias, down_bias = refs[:5]
-    own, far = refs[5:10], refs[10:15]
-    wu_out, wd_out, hidden, act_t, branch, y, wu, wd, act, sems_u, sems_d = refs[20:]
-    wait_u = weight_copies(block, 1, 0, refs[15:16], refs[16:17], own, far, wu, sems_u)
-    wait_d = weight_copies(block, 2, 1, refs[17:18], refs[18:19], own, far, wd, sems_d)
+    own, far = refs[5:7], refs[7:9]
+    wu_out, wd_out, hidden, act_t, branch, y, wu, wd, act, sems_u, sems_d = refs[14:]
+    wait_u = weight_copies(block, 1, 0, refs[9:10], refs[10:11], own, far, wu, sems_u)
+    wait_d = weight_copies(block, 2, 1, refs[11:12], refs[12:13], own, far, wd, sems_d)
     wait_u()
     keep_u = pltpu.make_async_copy(wu, wu_out, sems_u.at[26])
     keep_u.start()
@@ -689,7 +805,7 @@
             shape_of(F32, t, D),
             shape_of(BF, t, D),
         ),
-        in_specs=[INSIDE] * 5 + [ANYWHERE] * 15,
+        in_specs=[INSIDE] * 5 + [ANYWHERE] * 9,
         out_specs=(ANYWHERE,) * 2 + (INSIDE,) * 4,
         scratch_shapes=[
             pltpu.VMEM((D, FF), BF),
@@ -776,7 +892,7 @@
             pltpu.SemaphoreType.DMA((8,)),
         ],
         compiler_params=PARAMS,
-        cost_estimate=cost(5 * D * FF, 4 * t * D * FF),
+        cost_estimate=free(),
     )(grad, d_branch, ada, mid, attended, hidden, branch, wu, wd, after)
 
 
@@ -839,7 +955,7 @@
             pltpu.SemaphoreType.DMA((2,)),
         ],
         compiler_params=PARAMS,
-        cost_estimate=cost(3 * D * FF, 2 * t * D * FF),
+        cost_estimate=free(),
     )(x, d_mid, d_att, ada, q, k, v, stats, wa, after)
 
 
@@ -960,24 +1076,24 @@
     for g in range(4):
         gatherer.extract(g)
     ids_all = in_order(across(ids_z)).reshape(-1, 2)
-    gatherer.after = ids_all
     gatherer.stack(0)
+    (ids_all,) = gatherer.hold(ids_all)
     gatherer.onward(0)
-    gatherer.share(0)
-    far_sides0 = run_attend(0, x)
-    gatherer.stack(1)
     d_branch1 = branch_grad(1, cot)
     far_branch1 = swap(d_branch1)
+    gatherer.share(0)
+    gatherer.stack(1)
+    far_sides0 = run_attend(0, x)
+    gatherer.stack(2)
     far_sides0, far_branch1 = gatherer.hold(far_sides0, far_branch1)
     gatherer.onward(1)
-    gatherer.stack(2)
     gatherer.share(1)
+    gatherer.onward(2)
+    gatherer.stack(3)
     far_mlp0 = run_mlp(0)
     y0 = kept_mlp[0][5]
-    gatherer.onward(2)
-    gatherer.stack(3)
+    gatherer.share(2)
     far_mlp0 = gatherer.hold(*far_mlp0)
-    gatherer.share(2)
     far_sides1 = run_attend(1, y0)
     gatherer.onward(3)
     (far_sides1,) = gatherer.hold(far_sides1)
@@ -1005,68 +1121,73 @@
         reducer.after = got[2]
         return got
 
-    def begin(block, kind, *operands):
-        reducer.begin(block, kind, operands)
+    def begin(block, kind, mode, *operands):
+        reducer.begin(block, kind, mode, operands)
 
     back1, far_hidden1 = run_mlp_back(1, cot, d_branch1)
-    begin(1, 2, kept_mlp[1][3], far_mlp1[0], d_branch1, far_branch1)
-    begin(1, 1, kept[1][-1], far_mlp1[1], back1[0], far_hidden1)
+    begin(1, 2, 0, kept_mlp[1][3], far_mlp1[0], d_branch1, far_branch1)
+    begin(1, 1, 3, kept[1][-1], far_mlp1[1], back1[0], far_hidden1)
     d_all1, dx1f, dx1, small1 = run_attend_back(1, y0, back1)
     far_all1 = far_half(d_all1)
     d_branch0 = branch_grad(0, dx1)
     far_branch0 = swap(d_branch0)
+    reducer.first(1)
+    begin(1, 0, 3, kept[1][1], far_sides1, d_all1, far_all1)
+    back0, far_hidden0 = run_mlp_back(0, dx1, d_branch0)
+    begin(0, 2, 3, kept_mlp[0][3], far_mlp0[0], d_branch0, far_branch0)
+    reducer.first(2)
+    begin(0, 1, 3, kept[0][-1], far_mlp0[1], back0[0], far_hidden0)
     reducer.first(0)
-    begin(1, 0, kept[1][1], far_sides1, d_all1, far_all1)
-    back0, far_hidden0 = run_mlp_back(0, dx1, d_branch0)
-    begin(0, 2, kept_mlp[0][3], far_mlp0[0], d_branch0, far_branch0)
-    reducer.first(1)
-    reducer.second(0)
-    begin(0, 1, kept[0][-1], far_mlp0[1], back0[0], far_hidden0)
+    reducer.second(1)
     d_all0, dx0, dx0_low, small0 = run_attend_back(0, x, back0)
     far_all0 = far_half(d_all0)
-    reducer.first(2)
-    reducer.second(1)
-    reducer.third(0)
-    begin(0, 0, kept[0][1], far_sides0, d_all0, far_all0)
+    reducer.first(3)
+    reducer.third(1)
+    reducer.second(2)
+    begin(0, 0, 3, kept[0][1], far_sides0, d_all0, far_all0)
     small_keep = jnp.where(is_first, small0, small1)
     small_got = swap(jnp.where(is_first, small1, small0))
-    reducer.first(3)
-    reducer.second(2)
-    reducer.third(1)
+    reducer.first(4)
+    reducer.third(2)
+    reducer.second(3)
+    reducer.second(0)
     (small_got,) = reducer.hold(small_got)
     small = jnp.stack(
         [jnp.where(is_first, small_keep, small_got), jnp.where(is_first, small_got, small_keep)]
     )
-    reducer.first(4)
-    reducer.second(3)
-    reducer.third(2)
+    block1, block0, last = (2, 1, 0), (2, 1), (0,)
+    reducer.first(5)
+    reducer.third(0)
+    reducer.unite(1, block1)
+    reducer.third(3)
     small = along_z(small)
-    reducer.unite(1)
-    reducer.first(5)
+    reducer.spread(1, block1)
     (small,) = reducer.hold(small)
     small = small[None]
     bits = [1 << i for i in range(lax.axis_size(R).bit_length() - 1)]
     hop = cross(small, 1)
-    reducer.spread(1)
     reducer.second(4)
-    reducer.third(3)
+    reducer.second(5)
+    reducer.third(4)
+    reducer.unite(0, block0)
+    reducer.spread_on(1, block1)
     (hop,) = reducer.hold(hop)
     small = jnp.concatenate([small, hop])
     hop = cross(small, 2)
-    reducer.spread_on(1)
-    reducer.second(5)
-    reducer.third(4)
+    reducer.spread(0, block0)
+    reducer.third(5)
+    reducer.unite(0, last)
     (hop,) = reducer.hold(hop)
     small = jnp.concatenate([small, hop])
     for bit in bits[2:]:
         small = jnp.concatenate([small, cross(small, bit)])
-    reducer.finish(1)
-    reducer.third(5)
-    reducer.unite(0)
-    reducer.spread(0)
-    reducer.spread_on(0)
-    reducer.finish(0)
-    qkv_grad, proj_grad, up_grad, down_grad = reducer.results
+    reducer.spread_on(0, block0)
+    reducer.spread(0, last)
+    reducer.spread_on(0, last)
+    reducer.finish(1, block1)
+    reducer.finish(0, block0)
+    reducer.finish(0, last)
+    (qkv_grad, proj_grad), (up_grad,), (down_grad,) = (reducer.results[k] for k in range(3))
 
     def both_micros(v0, v1):
         keep = jnp.where(is_first, v0, v1)

time: 894 us -> 872 us (0.975)
  waiting for transfers between devices: 299 us -> 239 us
  Pallas kernels: 273 us -> 302 us
  starting transfers between devices: 126 us -> 140 us
  blocking collectives: 12.4 us -> 0 us
    ppermute x96 -> x87, waiting for transfers between devices: 281 us -> 204 us  [move(): return lax.ppermute(value, ALL, pairs)]
    pallas_call x22 -> x32, Pallas kernels: 82.6 us -> 117 us  [the longest x6 50.6 us: wgrad(): pl.pallas_call(functools.partial(wgrad_kernel, kind, mode), out_shape=(pa...]
    unnamed x306 -> x337, local copies, waits for them, and re-layouts: 66.2 us -> 86.9 us
    all_to_all x9 -> x10, waiting for transfers between devices: 8.04 us -> 26.1 us  [trade(): return lax.all_to_all(value, Z, split_axis=0, concat_axis=0, tiled=True)]
    all_to_all x1 -> x0, blocking collectives: 12.4 us -> none  [trade(): return lax.all_to_all(value, Z, split_axis=0, concat_axis=0, tiled=True)]
    slice x12 -> x6, local copies, waits for them, and re-layouts: 23.8 us -> 12 us  [spread_on(): pa, pb = (on_core(flat2[:n], 1, block), on_core(flat1[n:], 2, block))]
    ppermute x96 -> x87, starting transfers between devices: 82.6 us -> 91.7 us  [move(): return lax.ppermute(value, ALL, pairs)]
    all_to_all x9 -> x10, starting transfers between devices: 42.7 us -> 48.1 us  [trade(): return lax.all_to_all(value, Z, split_axis=0, concat_axis=0, tiled=True)]
  transfers between devices with their start and end apart: 109 -> 101, of which waited for: 37 -> 37; matrix products, arithmetic and copies ran while one was open for 11% -> 10% of each run, Pallas kernels for 27% -> 29%
where the time goes in v3:
time: 872 us; the launch traced here: 864 us
  Pallas kernels  302 us (35%)
  waiting for transfers between devices  239 us (27%)
  starting transfers between devices  140 us (16%)
  local copies, waits for them, and re-layouts  132 us (15%)
  other arithmetic  24.5 us (3%)
  between operations  15.6 us (2%)
  matrix products  10.6 us (1%)
    ppermute x87, waiting for transfers between devices, move(): return lax.ppermute(value, ALL, pairs)  204 us
    ppermute x87, starting transfers between devices, move(): return lax.ppermute(value, ALL, pairs)  91.7 us
    unnamed x337, local copies, waits for them, and re-layouts  86.9 us
    pallas_call x6, Pallas kernels, wgrad(): pl.pallas_call(functools.partial(wgrad_kernel, kind, mode), out_shape=(pa...  50.6 us
    all_to_all x10, starting transfers between devices, trade(): return lax.all_to_all(value, Z, split_axis=0, concat_axis=0, tiled=True)  48.1 us
    pallas_call x2, Pallas kernels, mlp(): pl.pallas_call(functools.partial(mlp_kernel, block), out_shape=(shape_of(...  43.6 us
    pallas_call x2, Pallas kernels, attend(): pl.pallas_call(functools.partial(attend_kernel, block), out_shape=(shape_...  37.6 us
    pallas_call x2, Pallas kernels, attend_back(): pl.pallas_call(attend_back_kernel, out_shape=(shape_of(BF, 2, t, HALF), s...  37.5 us
  transfers between devices with their start and end apart: 101, of which 37 were waited for; matrix products, arithmetic and copies ran while one was open for 10% of the time, Pallas kernels for 29%

profile of v3, /device:TPU:0, one launch (start us, length us, event | category | flops | bytes accessed | tf_op | source)
XLA Modules:
  0.0 863.6 jit_solution(7791581720274691752)
XLA Ops:
  64.1 21.0 %collective-permute-done.9 = s32[2,4,2,2]{1,3,2,0:T(2,128)S(1)} collective-permute-done((s32[2,4,2,2]{1,3,2,0:T(2,128)S(1)}, s32[2,4,2,2]{1,3,2,0:T(2,128)S(1)}, u32[]{:S(2)}, u32[]{:S(2)}) %collective-permute-start.9) | collective-permute-done | bytes 160 | tf_op jit(solution)/shard_map/ppermute | solution.py:39
  105.9 9.4 %all-to-all-done.1 = f32[4,2,6912]{2,1,0:T(2,128)S(1)} async-done(((f32[4,2,6912]{2,1,0:T(2,128)}), f32[4,2,6912]{2,1,0:T(2,128)S(1)}, u32[]{:S(2)}, u32[]{:S(2)}) %all-to-all-start.1) | async-done | bytes 221216 | tf_op jit(solution)/shard_map/all_to_all | solution.py:56
  126.6 18.8 %shard_map.255 = (bf16[1152,4608]{1,0:T(8,128)(2,1)}, bf16[2,256,1152]{2,1,0:T(8,128)(2,1)}, bf16[256,1152]{1,0:T(8,128)(2,1)S(1)}, bf16[256,1152]{1,0:T(8,128)(...) custom-call(bf16[256,1152]{1,0:T(8,128)(2,1)S(1)} %copy-done.27, ...), custom_call_target="tpu_custom_call" | custom-call | flops 2717908992 | bytes 21233664 | tf_op jit(solution)/shard_map/pallas_call | solution.py:758
  155.7 11.9 %collective-permute-done.14.p1 = bf16[2,3,144,1152]{3,2,1,0:T(8,128)(2,1)} collective-permute-done((bf16[2,3,144,1152]{3,2,1,0:T(8,128)(2,1)}, bf16[2,3,144,1152]{3,2,1,0:T(8,128)(2,1)}, u32[]{:S(2)}, u32[]{:S(2)}) %collective-permute-start.14) | collective-permute-done | bytes 1990688 | tf_op jit(solution)/shard_map/ppermute | solution.py:39
  180.9 21.0 %collective-permute-done.18.pa = bf16[1,3,144,1152]{3,2,1,0:T(8,128)(2,1)S(1)} collective-permute-done((bf16[1,3,144,1152]{3,2,1,0:T(8,128)(2,1)}, bf16[1,3,144,1152]{3,2,1,0:T(8,128)(2,1)S(1)}, u32[]{:S(2)}, u32[]{:S(2)}) %collective-permute-start.18) | collective-permute-done | bytes 995360 | tf_op jit(solution)/shard_map/ppermute | solution.py:39
  206.2 16.5 %collective-permute-done.22.p1 = bf16[1,3,144,1152]{3,2,1,0:T(8,128)(2,1)S(1)} collective-permute-done((bf16[1,3,144,1152]{3,2,1,0:T(8,128)(2,1)S(1)}, bf16[1,3,144,1152]{3,2,1,0:T(8,128)(2,1)S(1)}, u32[]{:S(2)}, u32[]{:S(2)}) %collective-permute-start.22) | collective-permute-done | bytes 995360 | tf_op jit(solution)/shard_map/ppermute | solution.py:39
  239.9 22.1 %shard_map.262 = (bf16[1152,4608]{1,0:T(8,128)(2,1)}, bf16[4608,1152]{1,0:T(8,128)(2,1)}, f32[256,4608]{1,0:T(8,128)}, bf16[2,4,576,256]{3,2,1,0:T(8,128)(2,1)},...) custom-call(f32[256,1152]{1,0:T(8,128)S(1)} %copy-done.38, bf16[256,1152]{1,0:T(8,128)(2,1)S(1)} %copy-done.36, ...), custom_call_target="tpu_custom_call" | custom-call | flops 5435817984 | bytes 42467328 | tf_op jit(solution)/shard_map/pallas_call | solution.py:798
  271.7 18.8 %shard_map.265 = (bf16[1152,4608]{1,0:T(8,128)(2,1)}, bf16[2,256,1152]{2,1,0:T(8,128)(2,1)}, bf16[256,1152]{1,0:T(8,128)(2,1)S(1)}, bf16[256,1152]{1,0:T(8,128)(...) custom-call(bf16[256,1152]{1,0:T(8,128)(2,1)S(1)} %get-tuple-element, ...), custom_call_target="tpu_custom_call" | custom-call | flops 2717908992 | bytes 21233664 | tf_op jit(solution)/shard_map/pallas_call | solution.py:758
  306.9 17.3 %collective-permute-done.32.pa = bf16[1,3,144,1152]{3,2,1,0:T(8,128)(2,1)} collective-permute-done((bf16[1,3,144,1152]{3,2,1,0:T(8,128)(2,1)}, bf16[1,3,144,1152]{3,2,1,0:T(8,128)(2,1)}, u32[]{:S(2)}, u32[]{:S(2)}) %collective-permute-start.32) | collective-permute-done | bytes 995360 | tf_op jit(solution)/shard_map/ppermute | solution.py:39
  334.2 21.5 %shard_map.269 = (bf16[1152,4608]{1,0:T(8,128)(2,1)}, bf16[4608,1152]{1,0:T(8,128)(2,1)}, f32[256,4608]{1,0:T(8,128)}, bf16[2,4,576,256]{3,2,1,0:T(8,128)(2,1)},...) custom-call(f32[256,1152]{1,0:T(8,128)S(1)} %copy-done.39, ...), custom_call_target="tpu_custom_call" | custom-call | flops 5435817984 | bytes 42467328 | tf_op jit(solution)/shard_map/pallas_call | solution.py:798
  358.6 16.9 %shard_map.270 = (bf16[2,256,2304]{2,1,0:T(8,128)(2,1)}, f32[256,1152]{1,0:T(8,128)S(1)}, bf16[256,1152]{1,0:T(8,128)(2,1)S(1)}, f32[16,1152]{1,0:T(8,128)S(1)}) custom-call(bf16[256,1152]{1,0:T(8,128)(2,1)S(1)} %copy-done.62, bf16[256,1152]{1,0:T(8,128)(2,1)} %get-tuple-element.303.refs_1_.refs_2_, f32[6,1152]{1,0:T(8,128)S(1)} %reshape.341.refs_1_.refs_2_.refs_3_, ...), custom_call_target="tpu_custom_call" | custom-call | tf_op jit(solution)/shard_map/pallas_call | solution.py:878
  378.1 8.2 shard_map.271.refs_4_
  396.6 8.6 shard_map.272
  407.6 18.7 %shard_map.273 = (bf16[2,256,2304]{2,1,0:T(8,128)(2,1)}, f32[256,1152]{1,0:T(8,128)}, bf16[256,1152]{1,0:T(8,128)(2,1)S(1)}, bf16[16,1152]{1,0:T(8,128)(2,1)S(1)}) custom-call(bf16[256,1152]{1,0:T(8,128)(2,1)S(1)} %get-tuple-element.141._.refs_0_, f32[256,1152]{1,0:T(8,128)} %copy-done.69, bf16[256,1152]{1,0:T(8,128)(2,1)S(1)} %copy-done.105, ...), custom_call_target="tpu_custom_call" | custom-call | tf_op jit(solution)/shard_map/pallas_call | solution.py:942
  444.3 9.0 %shard_map.275 = (bf16[2,2,144,1152]{3,2,1,0:T(8,128)(2,1)}, bf16[2,2,144,1152]{3,2,1,0:T(8,128)(2,1)}, bf16[2,2,144,1152]{3,2,1,0:T(8,128)(2,1)}, bf16[2,2,144,1152]{3,2,1,0:T(8,128)(2,1)}) custom-call(bf16[2,256,1152]{2,1,0:T(8,128)(2,1)S(1)} %copy-done.73, bf16[2,256,1152]{2,1,0:T(8,128)(2,1)} %shard_map.267._.refs_1_, ...), custom_call_target="tpu_custom_call" | custom-call | tf_op jit(solution)/shard_map/pallas_call | solution.py:516
  454.9 16.6 %shard_map.276 = (bf16[2,256,2304]{2,1,0:T(8,128)(2,1)}, f32[256,1152]{1,0:T(8,128)S(1)}, bf16[256,1152]{1,0:T(8,128)(2,1)S(1)}, f32[16,1152]{1,0:T(8,128)S(1)}) custom-call(bf16[256,1152]{1,0:T(8,128)(2,1)S(1)} %get-tuple-element.169.refs_4_.refs_0_, bf16[256,1152]{1,0:T(8,128)(2,1)S(1)} %fusion.4.refs_1_.refs_2_, f32[6,1152]{1,0:T(8,128)S(1)} %copy-done.77, ...), custom_call_target="tpu_custom_call" | custom-call | tf_op jit(solution)/shard_map/pallas_call | solution.py:878
  477.2 8.2 shard_map.277
  493.4 8.6 shard_map.279
  533.1 18.9 %shard_map.282 = (bf16[2,256,2304]{2,1,0:T(8,128)(2,1)}, f32[256,1152]{1,0:T(8,128)}, bf16[256,1152]{1,0:T(8,128)(2,1)S(1)}, bf16[16,1152]{1,0:T(8,128)(2,1)S(1)}) custom-call(bf16[256,1152]{1,0:T(8,128)(2,1)S(1)} %copy-done.28, f32[256,1152]{1,0:T(8,128)} %copy-done.68, bf16[256,1152]{1,0:T(8,128)(2,1)S(1)} %copy-done.103, f32[6,1152]{1,0:T(8,128)S(1)} %copy-done.77, ...), custom_call_target="tpu_custom_call" | custom-call | tf_op jit(solution)/shard_map/pallas_call | solution.py:942
  582.5 8.1 shard_map.286
  591.5 17.0 %collective-permute-done.59.refs_2_ = bf16[2,2,144,1152]{3,2,1,0:T(8,128)(2,1)S(1)} collective-permute-done((bf16[2,2,144,1152]{3,2,1,0:T(8,128)(2,1)}, bf16[2,2,144,1152]{3,2,1,0:T(8,128)(2,1)S(1)}, u32[]{:S(2)}, u32[]{:S(2)}) %collective-permute-start.59) | collective-permute-done | bytes 1327136 | tf_op jit(solution)/shard_map/ppermute | solution.py:39
  633.6 28.9 %collective-permute-done.52.refs_1_ = bf16[2,144,1152]{2,1,0:T(8,128)(2,1)S(1)} collective-permute-done((bf16[2,144,1152]{2,1,0:T(8,128)(2,1)}, bf16[2,144,1152]{2,1,0:T(8,128)(2,1)S(1)}, u32[]{:S(2)}, u32[]{:S(2)}) %collective-permute-start.52) | collective-permute-done | bytes 663584 | tf_op jit(solution)/shard_map/ppermute | solution.py:39
  718.1 8.9 %collective-permute-done.71.refs_2_ = bf16[2,144,1152]{2,1,0:T(8,128)(2,1)S(1)} collective-permute-done((bf16[2,144,1152]{2,1,0:T(8,128)(2,1)}, bf16[2,144,1152]{2,1,0:T(8,128)(2,1)S(1)}, u32[]{:S(2)}, u32[]{:S(2)}) %collective-permute-start.71) | collective-permute-done | bytes 663584 | tf_op jit(solution)/shard_map/ppermute | solution.py:39
  786.8 9.7 %collective-permute-start.75 = (f32[32,288]{1,0:T(8,128)S(1)}, f32[32,288]{1,0:T(8,128)S(1)}, u32[]{:S(2)}, u32[]{:S(2)}) collective-permute-start(f32[32,288]{1,0:T(8,128)S(1)} %fusion.8), channel_id=1, source_target_pairs={{0,16},{1,17},{2,18},{3,19},{4,20},{5,21},{6,22},{7,23},{8,24},{9,... | collective-permute-start | bytes 110600 | tf_op jit(solution)/shard_map/ppermute | solution.py:39
  (704 shorter events, 483.5 us)
Async XLA Ops:
  7.2 49.2 %all-gather.9.cloned.1.call-start = ((), (), s32[]{:S(2)}) async-start(), calls=%async_computation.10 | async-start | bytes 1658880 | tf_op jit(solution)/shard_map/all_gather | solution.py:422
  19.1 99.3 %all-gather.11.cloned.1.call-start = ((), (), s32[]{:S(2)}) async-start(), calls=%async_computation.11 | async-start | bytes 3317760 | tf_op jit(solution)/shard_map/all_gather | solution.py:422
  100.3 51.0 %all-gather.13.cloned.1.call-start = ((), (), s32[]{:S(2)}) async-start(), calls=%async_computation.12 | async-start | bytes 1658880 | tf_op jit(solution)/shard_map/all_gather | solution.py:422
  116.1 114.7 %all-gather.15.cloned.1.call-start = ((), (), s32[]{:S(2)}) async-start(), calls=%async_computation.13 | async-start | bytes 3317760 | tf_op jit(solution)/shard_map/all_gather | solution.py:422
  121.6 46.0 %collective-permute-start.14 = (bf16[2,3,144,1152]{3,2,1,0:T(8,128)(2,1)}, bf16[2,3,144,1152]{3,2,1,0:T(8,128)(2,1)}, u32[]{:S(2)}, u32[]{:S(2)}) collective-permute-start(bf16[2,3,144,1152]{3,2,1,0:T(8,128)(2,1)} %shard_map.254.refs_12_.p0), channel_id=1, source_target_pairs={{0,1},{1,0},{2,3},{3,2},{4,5},{5,4},{6,7},{7,6},{8,9},{9,8},{10,11... | collective-permute-start | bytes 5971976 | tf_op jit(solution)/shard_map/ppermute | solution.py:39
  122.1 45.5 %collective-permute-start.15 = (bf16[2,3,144,1152]{3,2,1,0:T(8,128)(2,1)}, bf16[2,3,144,1152]{3,2,1,0:T(8,128)(2,1)}, u32[]{:S(2)}, u32[]{:S(2)}) collective-permute-start(bf16[2,3,144,1152]{3,2,1,0:T(8,128)(2,1)} %shard_map.254.refs_12_.p0), channel_id=1, source_target_pairs={{0,2},{1,3},{2,0},{3,1},{4,6},{5,7},{6,4},{7,5},{8,10},{9,11},{10,... | collective-permute-start | bytes 5971976 | tf_op jit(solution)/shard_map/ppermute | solution.py:39
  176.7 62.0 %collective-permute-start.20 = (bf16[3,2,3,144,1152]{4,3,2,1,0:T(8,128)(2,1)}, bf16[3,2,3,144,1152]{4,3,2,1,0:T(8,128)(2,1)}, u32[]{:S(2)}, u32[]{:S(2)}) collective-permute-start(bf16[3,2,3,144,1152]{4,3,2,1,0:T(8,128)(2,1)} %get-tuple-element.137.refs_5_), channel_id=1, source_target_pairs={{0,16},{1,17},{2,18},{3,19},{4,20},{5,21},{6,22},{7,23},{8,24},{9,... | collective-permute-start | bytes 17915912 | tf_op jit(solution)/shard_map/ppermute | solution.py:39
  178.9 43.9 %collective-permute-start.22 = (bf16[1,3,144,1152]{3,2,1,0:T(8,128)(2,1)S(1)}, bf16[1,3,144,1152]{3,2,1,0:T(8,128)(2,1)S(1)}, u32[]{:S(2)}, u32[]{:S(2)}) collective-permute-start(bf16[1,3,144,1152]{3,2,1,0:T(8,128)(2,1)S(1)} %copy-done.16), channel_id=1, source_target_pairs={{0,1},{1,0},{2,3},{3,2},{4,5},{5,4},{6,7},{7,6},{8,9},{9,8},{10,11... | collective-permute-start | bytes 2985992 | tf_op jit(solution)/shard_map/ppermute | solution.py:39
  179.8 44.4 %collective-permute-start.23 = (bf16[1,3,144,1152]{3,2,1,0:T(8,128)(2,1)S(1)}, bf16[1,3,144,1152]{3,2,1,0:T(8,128)(2,1)S(1)}, u32[]{:S(2)}, u32[]{:S(2)}) collective-permute-start(bf16[1,3,144,1152]{3,2,1,0:T(8,128)(2,1)S(1)} %copy-done.16), channel_id=1, source_target_pairs={{0,2},{1,3},{2,0},{3,1},{4,6},{5,7},{6,4},{7,5},{8,10},{9,11},{10,... | collective-permute-start | bytes 2985992 | tf_op jit(solution)/shard_map/ppermute | solution.py:39
  237.7 55.3 %collective-permute-start.30 = (bf16[2,3,144,1152]{3,2,1,0:T(8,128)(2,1)}, bf16[2,3,144,1152]{3,2,1,0:T(8,128)(2,1)}, u32[]{:S(2)}, u32[]{:S(2)}) collective-permute-start(bf16[2,3,144,1152]{3,2,1,0:T(8,128)(2,1)} %shard_map.261.refs_13_.p0), channel_id=1, source_target_pairs={{0,1},{1,0},{2,3},{3,2},{4,5},{5,4},{6,7},{7,6},{8,9},{9,8},{10,11... | collective-permute-start | bytes 5971976 | tf_op jit(solution)/shard_map/ppermute | solution.py:39
  238.7 54.3 %collective-permute-start.31 = (bf16[2,3,144,1152]{3,2,1,0:T(8,128)(2,1)}, bf16[2,3,144,1152]{3,2,1,0:T(8,128)(2,1)}, u32[]{:S(2)}, u32[]{:S(2)}) collective-permute-start(bf16[2,3,144,1152]{3,2,1,0:T(8,128)(2,1)} %shard_map.261.refs_13_.p0), channel_id=1, source_target_pairs={{0,2},{1,3},{2,0},{3,1},{4,6},{5,7},{6,4},{7,5},{8,10},{9,11},{10,... | collective-permute-start | bytes 5971976 | tf_op jit(solution)/shard_map/ppermute | solution.py:39
  386.3 122.9 %all-to-all-start.2 = ((bf16[4,4,144,1152]{3,2,1,0:T(8,128)(2,1)}), bf16[4,4,144,1152]{3,2,1,0:T(8,128)(2,1)}, u32[]{:S(2)}, u32[]{:S(2)}) async-start(bf16[4,4,144,1152]{3,2,1,0:T(8,128)(2,1)} %shard_map.271.refs_4_), calls=%async_computation.2 | async-start | bytes 10616832 | tf_op jit(solution)/shard_map/all_to_all | solution.py:56
  429.5 46.9 %collective-permute-start.49 = (bf16[256,1152]{1,0:T(8,128)(2,1)S(1)}, bf16[256,1152]{1,0:T(8,128)(2,1)S(1)}, u32[]{:S(2)}, u32[]{:S(2)}) collective-permute-start(bf16[256,1152]{1,0:T(8,128)(2,1)S(1)} %fusion.4.refs_1_.refs_2_), channel_id=1, source_target_pairs={{0,16},{1,17},{2,18},{3,19},{4,20},{5,21},{6,22},{7,23},{8,24},{9,... | collective-permute-start | bytes 1769480 | tf_op jit(solution)/shard_map/ppermute | solution.py:39
  518.3 44.9 %all-to-all-start.3 = ((bf16[4,144,1152]{2,1,0:T(8,128)(2,1)}), bf16[4,144,1152]{2,1,0:T(8,128)(2,1)}, u32[]{:S(2)}, u32[]{:S(2)}) async-start(bf16[4,144,1152]{2,1,0:T(8,128)(2,1)} %shard_map.281.refs_9_), calls=%async_computation.3 | async-start | bytes 2654208 | tf_op jit(solution)/shard_map/all_to_all | solution.py:56
  524.2 43.9 %collective-permute-start.57 = (bf16[2,144,1152]{2,1,0:T(8,128)(2,1)}, bf16[2,144,1152]{2,1,0:T(8,128)(2,1)}, u32[]{:S(2)}, u32[]{:S(2)}) collective-permute-start(bf16[2,144,1152]{2,1,0:T(8,128)(2,1)} %copy-done.126), channel_id=1, source_target_pairs={{0,2},{1,3},{2,0},{3,1},{4,6},{5,7},{6,4},{7,5},{8,10},{9,11},{10,... | collective-permute-start | bytes 1990664 | tf_op jit(solution)/shard_map/ppermute | solution.py:39
  525.3 42.8 %collective-permute-start.58 = (bf16[2,144,1152]{2,1,0:T(8,128)(2,1)}, bf16[2,144,1152]{2,1,0:T(8,128)(2,1)}, u32[]{:S(2)}, u32[]{:S(2)}) collective-permute-start(bf16[2,144,1152]{2,1,0:T(8,128)(2,1)} %copy-done.125), channel_id=1, source_target_pairs={{0,1},{1,0},{2,3},{3,2},{4,5},{5,4},{6,7},{7,6},{8,9},{9,8},{10,11... | collective-permute-start | bytes 1990664 | tf_op jit(solution)/shard_map/ppermute | solution.py:39
  571.5 44.9 %all-to-all-start.4 = ((bf16[4,144,1152]{2,1,0:T(8,128)(2,1)}), bf16[4,144,1152]{2,1,0:T(8,128)(2,1)}, u32[]{:S(2)}, u32[]{:S(2)}) async-start(bf16[4,144,1152]{2,1,0:T(8,128)(2,1)} %shard_map.285.refs_4_), calls=%async_computation.4 | async-start | bytes 2654208 | tf_op jit(solution)/shard_map/all_to_all | solution.py:56
  579.6 44.9 %collective-permute-start.55 = (bf16[2,144,1152]{2,1,0:T(8,128)(2,1)}, bf16[2,144,1152]{2,1,0:T(8,128)(2,1)}, u32[]{:S(2)}, u32[]{:S(2)}) collective-permute-start(bf16[2,144,1152]{2,1,0:T(8,128)(2,1)} %copy-done.128), channel_id=1, source_target_pairs={{0,2},{1,3},{2,0},{3,1},{4,6},{5,7},{6,4},{7,5},{8,10},{9,11},{10,... | collective-permute-start | bytes 1990664 | tf_op jit(solution)/shard_map/ppermute | solution.py:39
  581.4 43.1 %collective-permute-start.56 = (bf16[2,144,1152]{2,1,0:T(8,128)(2,1)}, bf16[2,144,1152]{2,1,0:T(8,128)(2,1)}, u32[]{:S(2)}, u32[]{:S(2)}) collective-permute-start(bf16[2,144,1152]{2,1,0:T(8,128)(2,1)} %copy-done.127), channel_id=1, source_target_pairs={{0,1},{1,0},{2,3},{3,2},{4,5},{5,4},{6,7},{7,6},{8,9},{9,8},{10,11... | collective-permute-start | bytes 1990664 | tf_op jit(solution)/shard_map/ppermute | solution.py:39
  590.5 79.6 %collective-permute-start.63 = (bf16[2,2,144,1152]{3,2,1,0:T(8,128)(2,1)}, bf16[2,2,144,1152]{3,2,1,0:T(8,128)(2,1)}, u32[]{:S(2)}, u32[]{:S(2)}) collective-permute-start(bf16[2,2,144,1152]{3,2,1,0:T(8,128)(2,1)} %get-tuple-element.224), channel_id=1, source_target_pairs={{0,1},{1,0},{2,3},{3,2},{4,5},{5,4},{6,7},{7,6},{8,9},{9,8},{10,11... | collective-permute-start | bytes 3981320 | tf_op jit(solution)/shard_map/ppermute | solution.py:39
  608.5 61.6 %collective-permute-start.64 = (bf16[2,2,144,1152]{3,2,1,0:T(8,128)(2,1)}, bf16[2,2,144,1152]{3,2,1,0:T(8,128)(2,1)}, u32[]{:S(2)}, u32[]{:S(2)}) collective-permute-start(bf16[2,2,144,1152]{3,2,1,0:T(8,128)(2,1)} %get-tuple-element.225), channel_id=1, source_target_pairs={{0,2},{1,3},{2,0},{3,1},{4,6},{5,7},{6,4},{7,5},{8,10},{9,11},{10,... | collective-permute-start | bytes 3981320 | tf_op jit(solution)/shard_map/ppermute | solution.py:39
  627.9 54.4 %all-to-all-start.6 = ((bf16[4,144,1152]{2,1,0:T(8,128)(2,1)}), bf16[4,144,1152]{2,1,0:T(8,128)(2,1)}, u32[]{:S(2)}, u32[]{:S(2)}) async-start(bf16[4,144,1152]{2,1,0:T(8,128)(2,1)} %shard_map.289.refs_2_), calls=%async_computation.6 | async-start | bytes 2654208 | tf_op jit(solution)/shard_map/all_to_all | solution.py:56
  755.7 78.3 %collective-permute-start.85 = (bf16[3,144,1152]{2,1,0:T(8,128)(2,1)}, bf16[3,144,1152]{2,1,0:T(8,128)(2,1)}, u32[]{:S(2)}, u32[]{:S(2)}) collective-permute-start(bf16[3,144,1152]{2,1,0:T(8,128)(2,1)} %slice.166), channel_id=1, source_target_pairs={{16,17},{17,16},{18,19},{19,18},{20,21},{21,20},{22,23},{23,22},{2... | collective-permute-start | bytes 2985992 | tf_op jit(solution)/shard_map/ppermute | solution.py:39
  767.8 43.2 %collective-permute-start.77 = (bf16[2,2,144,1152]{3,2,1,0:T(8,128)(2,1)}, bf16[2,2,144,1152]{3,2,1,0:T(8,128)(2,1)}, u32[]{:S(2)}, u32[]{:S(2)}) collective-permute-start(bf16[2,2,144,1152]{3,2,1,0:T(8,128)(2,1)} %shard_map.304.refs_1_.refs_0_), channel_id=1, source_target_pairs={{0,1},{1,0},{2,3},{3,2},{4,5},{5,4},{6,7},{7,6},{8,9},{9,8},{10,11... | collective-permute-start | bytes 3981320 | tf_op jit(solution)/shard_map/ppermute | solution.py:39
  (243 other events, 2613.2 us)
Sparse Core Ops, SparseCore 0:
  19.2 37.0 all-gather.8
  58.5 58.8 all-gather.10
  119.6 31.6 all-gather.12
  176.9 53.9 all-gather.14

commit v4 on v3

--- a/solution.py
+++ b/solution.py
@@ -581,7 +581,7 @@
     count = len(kinds)
     return pl.pallas_call(
         functools.partial(finish_kernel, block, kinds),
-        out_shape=tuple(jax.ShapeDtypeStruct(s, F32) for s in shapes),
+        out_shape=tuple(pltpu.HBM(s, F32) for s in shapes),
         in_specs=[ANYWHERE] * (6 + len(before)),
         out_specs=(ANYWHERE,) * len(shapes),
         scratch_shapes=[
@@ -638,7 +638,11 @@
             xk, xs, yk, ys = out
             self.state[i] = (xk, yk), (cross(xs, 2), cross(ys, 1))
 
-    def second(self, i):
+    def send(self, i):
+        (f,) = self.hold(self.state[i])
+        self.state[i] = (trade(f),)
+
+    def second(self, i, send=True):
         if self.modes[i] == 0:
             keep, send = plus(*self.state[i], self.after)
             self.after = keep
@@ -646,7 +650,7 @@
             return
         f = merged(*self.state[i], self.after)
         self.after = f
-        self.state[i] = (trade(f),)
+        self.state[i] = (trade(f),) if send else f
 
     def third(self, i):
         v = summed(self.state[i], self.after)
@@ -681,7 +685,7 @@
         for kind in kinds:
             before += self.results.get(kind, [])
         out = list(finish(block, kinds, self.ready[block, kinds], before, self.after))
-        self.after = out[0]
+        self.after = out[-1]
         for kind in kinds:
             n = 2 if kind == 0 else 1
             self.results[kind], out = out[:n], out[n:]
@@ -1136,9 +1140,10 @@
     back0, far_hidden0 = run_mlp_back(0, dx1, d_branch0)
     begin(0, 2, 3, kept_mlp[0][3], far_mlp0[0], d_branch0, far_branch0)
     reducer.first(2)
+    reducer.second(1, send=False)
     begin(0, 1, 3, kept[0][-1], far_mlp0[1], back0[0], far_hidden0)
     reducer.first(0)
-    reducer.second(1)
+    reducer.send(1)
     d_all0, dx0, dx0_low, small0 = run_attend_back(0, x, back0)
     far_all0 = far_half(d_all0)
     reducer.first(3)

time: 872 us -> 864 us (level)
    unnamed x337 -> x328, local copies, waits for them, and re-layouts: 86.9 us -> 80.6 us
  transfers between devices with their start and end apart: 101 -> 101, of which waited for: 37 -> 37; matrix products, arithmetic and copies ran while one was open for 10% -> 9% of each run, Pallas kernels for 29% -> 29%
where the time goes in v4:
time: 864 us; the launch traced here: 855 us
  Pallas kernels  299 us (35%)
  waiting for transfers between devices  239 us (28%)
  starting transfers between devices  140 us (16%)
  local copies, waits for them, and re-layouts  125 us (14%)
  other arithmetic  24.5 us (3%)
  between operations  15.6 us (2%)
  matrix products  10.6 us (1%)
    ppermute x87, waiting for transfers between devices, move(): return lax.ppermute(value, ALL, pairs)  210 us
    ppermute x87, starting transfers between devices, move(): return lax.ppermute(value, ALL, pairs)  91.7 us
    unnamed x328, local copies, waits for them, and re-layouts  80.6 us
    pallas_call x6, Pallas kernels, wgrad(): pl.pallas_call(functools.partial(wgrad_kernel, kind, mode), out_shape=(pa...  50.2 us
    all_to_all x10, starting transfers between devices, trade(): return lax.all_to_all(value, Z, split_axis=0, concat_axis=0, tiled=True)  48.5 us
    pallas_call x2, Pallas kernels, mlp(): pl.pallas_call(functools.partial(mlp_kernel, block), out_shape=(shape_of(...  43.5 us
    pallas_call x2, Pallas kernels, attend(): pl.pallas_call(functools.partial(attend_kernel, block), out_shape=(shape_...  37.6 us
    pallas_call x2, Pallas kernels, attend_back(): pl.pallas_call(attend_back_kernel, out_shape=(shape_of(BF, 2, t, HALF), s...  37.6 us
  transfers between devices with their start and end apart: 101, of which 37 were waited for; matrix products, arithmetic and copies ran while one was open for 9% of the time, Pallas kernels for 29%

profile of v4, /device:TPU:0, one launch (start us, length us, event | category | flops | bytes accessed | tf_op | source)
XLA Modules:
  0.0 854.9 jit_solution(16246173923214303087)
XLA Ops:
  64.1 21.0 %collective-permute-done.9 = s32[2,4,2,2]{1,3,2,0:T(2,128)S(1)} collective-permute-done((s32[2,4,2,2]{1,3,2,0:T(2,128)S(1)}, s32[2,4,2,2]{1,3,2,0:T(2,128)S(1)}, u32[]{:S(2)}, u32[]{:S(2)}) %collective-permute-start.9) | collective-permute-done | bytes 160 | tf_op jit(solution)/shard_map/ppermute | solution.py:39
  105.9 9.4 %all-to-all-done.1 = f32[4,2,6912]{2,1,0:T(2,128)S(1)} async-done(((f32[4,2,6912]{2,1,0:T(2,128)}), f32[4,2,6912]{2,1,0:T(2,128)S(1)}, u32[]{:S(2)}, u32[]{:S(2)}) %all-to-all-start.1) | async-done | bytes 221216 | tf_op jit(solution)/shard_map/all_to_all | solution.py:56
  126.6 18.8 %shard_map.255 = (bf16[1152,4608]{1,0:T(8,128)(2,1)}, bf16[2,256,1152]{2,1,0:T(8,128)(2,1)}, bf16[256,1152]{1,0:T(8,128)(2,1)S(1)}, bf16[256,1152]{1,0:T(8,128)(...) custom-call(bf16[256,1152]{1,0:T(8,128)(2,1)S(1)} %copy-done.27, ...), custom_call_target="tpu_custom_call" | custom-call | flops 2717908992 | bytes 21233664 | tf_op jit(solution)/shard_map/pallas_call | solution.py:762
  155.7 11.9 %collective-permute-done.14.p1 = bf16[2,3,144,1152]{3,2,1,0:T(8,128)(2,1)} collective-permute-done((bf16[2,3,144,1152]{3,2,1,0:T(8,128)(2,1)}, bf16[2,3,144,1152]{3,2,1,0:T(8,128)(2,1)}, u32[]{:S(2)}, u32[]{:S(2)}) %collective-permute-start.14) | collective-permute-done | bytes 1990688 | tf_op jit(solution)/shard_map/ppermute | solution.py:39
  180.8 21.0 %collective-permute-done.18.pa = bf16[1,3,144,1152]{3,2,1,0:T(8,128)(2,1)S(1)} collective-permute-done((bf16[1,3,144,1152]{3,2,1,0:T(8,128)(2,1)}, bf16[1,3,144,1152]{3,2,1,0:T(8,128)(2,1)S(1)}, u32[]{:S(2)}, u32[]{:S(2)}) %collective-permute-start.18) | collective-permute-done | bytes 995360 | tf_op jit(solution)/shard_map/ppermute | solution.py:39
  206.2 16.5 %collective-permute-done.22.p1 = bf16[1,3,144,1152]{3,2,1,0:T(8,128)(2,1)S(1)} collective-permute-done((bf16[1,3,144,1152]{3,2,1,0:T(8,128)(2,1)S(1)}, bf16[1,3,144,1152]{3,2,1,0:T(8,128)(2,1)S(1)}, u32[]{:S(2)}, u32[]{:S(2)}) %collective-permute-start.22) | collective-permute-done | bytes 995360 | tf_op jit(solution)/shard_map/ppermute | solution.py:39
  239.8 22.0 %shard_map.262 = (bf16[1152,4608]{1,0:T(8,128)(2,1)}, bf16[4608,1152]{1,0:T(8,128)(2,1)}, f32[256,4608]{1,0:T(8,128)}, bf16[2,4,576,256]{3,2,1,0:T(8,128)(2,1)},...) custom-call(f32[256,1152]{1,0:T(8,128)S(1)} %copy-done.39, bf16[256,1152]{1,0:T(8,128)(2,1)S(1)} %copy-done.36, ...), custom_call_target="tpu_custom_call" | custom-call | flops 5435817984 | bytes 42467328 | tf_op jit(solution)/shard_map/pallas_call | solution.py:802
  271.6 18.8 %shard_map.265 = (bf16[1152,4608]{1,0:T(8,128)(2,1)}, bf16[2,256,1152]{2,1,0:T(8,128)(2,1)}, bf16[256,1152]{1,0:T(8,128)(2,1)S(1)}, bf16[256,1152]{1,0:T(8,128)(...) custom-call(bf16[256,1152]{1,0:T(8,128)(2,1)S(1)} %get-tuple-element, ...), custom_call_target="tpu_custom_call" | custom-call | flops 2717908992 | bytes 21233664 | tf_op jit(solution)/shard_map/pallas_call | solution.py:762
  307.0 17.1 %collective-permute-done.32.pa = bf16[1,3,144,1152]{3,2,1,0:T(8,128)(2,1)} collective-permute-done((bf16[1,3,144,1152]{3,2,1,0:T(8,128)(2,1)}, bf16[1,3,144,1152]{3,2,1,0:T(8,128)(2,1)}, u32[]{:S(2)}, u32[]{:S(2)}) %collective-permute-start.32) | collective-permute-done | bytes 995360 | tf_op jit(solution)/shard_map/ppermute | solution.py:39
  334.2 21.5 %shard_map.269 = (bf16[1152,4608]{1,0:T(8,128)(2,1)}, bf16[4608,1152]{1,0:T(8,128)(2,1)}, f32[256,4608]{1,0:T(8,128)}, bf16[2,4,576,256]{3,2,1,0:T(8,128)(2,1)},...) custom-call(f32[256,1152]{1,0:T(8,128)S(1)} %copy-done.40, ...), custom_call_target="tpu_custom_call" | custom-call | flops 5435817984 | bytes 42467328 | tf_op jit(solution)/shard_map/pallas_call | solution.py:802
  358.6 16.9 %shard_map.270 = (bf16[2,256,2304]{2,1,0:T(8,128)(2,1)}, f32[256,1152]{1,0:T(8,128)S(1)}, bf16[256,1152]{1,0:T(8,128)(2,1)S(1)}, f32[16,1152]{1,0:T(8,128)S(1)}) custom-call(bf16[256,1152]{1,0:T(8,128)(2,1)S(1)} %copy-done.61, bf16[256,1152]{1,0:T(8,128)(2,1)} %get-tuple-element.303.refs_1_.refs_2_, f32[6,1152]{1,0:T(8,128)S(1)} %reshape.341.refs_1_.refs_2_.refs_3_, ...), custom_call_target="tpu_custom_call" | custom-call | tf_op jit(solution)/shard_map/pallas_call | solution.py:882
  378.1 8.2 shard_map.271.refs_4_
  396.6 8.6 %shard_map.272 = (bf16[2,2,144,1152]{3,2,1,0:T(8,128)(2,1)S(1)}, bf16[2,2,144,1152]{3,2,1,0:T(8,128)(2,1)}, bf16[2,2,144,1152]{3,2,1,0:T(8,128)(2,1)}, bf16[2,2,144,1152]{3,2,1,0:T(8,128)(2,1)}) custom-call(bf16[256,1152]{1,0:T(8,128)(2,1)S(1)} %get-tuple-element.147._.refs_1_.refs_0_, bf16[256,1152]{1,0:T(8,128)(2,1)S(1)} %collective-permute-done.38.refs_1_, ...), custom_call_target="tpu_custom_call" | custom-call | tf_op jit(solution)/shard_map/pallas_call | solution.py:516
  407.6 18.7 %shard_map.273 = (bf16[2,256,2304]{2,1,0:T(8,128)(2,1)}, f32[256,1152]{1,0:T(8,128)}, bf16[256,1152]{1,0:T(8,128)(2,1)S(1)}, bf16[16,1152]{1,0:T(8,128)(2,1)S(1)}) custom-call(bf16[256,1152]{1,0:T(8,128)(2,1)S(1)} %get-tuple-element.141._.refs_0_, f32[256,1152]{1,0:T(8,128)} %copy-done.68, bf16[256,1152]{1,0:T(8,128)(2,1)S(1)} %copy-done.102, ...), custom_call_target="tpu_custom_call" | custom-call | tf_op jit(solution)/shard_map/pallas_call | solution.py:946
  429.2 8.6 %collective-permute-done.42.refs_2_ = bf16[2,2,144,1152]{3,2,1,0:T(8,128)(2,1)S(1)} collective-permute-done((bf16[2,2,144,1152]{3,2,1,0:T(8,128)(2,1)}, bf16[2,2,144,1152]{3,2,1,0:T(8,128)(2,1)S(1)}, u32[]{:S(2)}, u32[]{:S(2)}) %collective-permute-start.42) | collective-permute-done | bytes 1327136 | tf_op jit(solution)/shard_map/ppermute | solution.py:39
  444.1 9.0 %shard_map.275 = (bf16[2,2,144,1152]{3,2,1,0:T(8,128)(2,1)}, bf16[2,2,144,1152]{3,2,1,0:T(8,128)(2,1)}, bf16[2,2,144,1152]{3,2,1,0:T(8,128)(2,1)}, bf16[2,2,144,1152]{3,2,1,0:T(8,128)(2,1)}) custom-call(bf16[2,256,1152]{2,1,0:T(8,128)(2,1)S(1)} %copy-done.72, bf16[2,256,1152]{2,1,0:T(8,128)(2,1)} %shard_map.267._.refs_1_, ...), custom_call_target="tpu_custom_call" | custom-call | tf_op jit(solution)/shard_map/pallas_call | solution.py:516
  454.8 16.6 %shard_map.276 = (bf16[2,256,2304]{2,1,0:T(8,128)(2,1)}, f32[256,1152]{1,0:T(8,128)S(1)}, bf16[256,1152]{1,0:T(8,128)(2,1)S(1)}, f32[16,1152]{1,0:T(8,128)S(1)}) custom-call(bf16[256,1152]{1,0:T(8,128)(2,1)S(1)} %get-tuple-element.169.refs_4_.refs_0_, bf16[256,1152]{1,0:T(8,128)(2,1)S(1)} %fusion.4.refs_1_.refs_2_, f32[6,1152]{1,0:T(8,128)S(1)} %copy-done.76, ...), custom_call_target="tpu_custom_call" | custom-call | tf_op jit(solution)/shard_map/pallas_call | solution.py:882
  477.0 8.2 shard_map.277
  500.4 8.1 shard_map.280
  530.9 18.9 %shard_map.283 = (bf16[2,256,2304]{2,1,0:T(8,128)(2,1)}, f32[256,1152]{1,0:T(8,128)}, bf16[256,1152]{1,0:T(8,128)(2,1)S(1)}, bf16[16,1152]{1,0:T(8,128)(2,1)S(1)}) custom-call(bf16[256,1152]{1,0:T(8,128)(2,1)S(1)} %copy-done.28, f32[256,1152]{1,0:T(8,128)} %copy-done.67, bf16[256,1152]{1,0:T(8,128)(2,1)S(1)} %copy-done.100, f32[6,1152]{1,0:T(8,128)S(1)} %copy-done.76, ...), custom_call_target="tpu_custom_call" | custom-call | tf_op jit(solution)/shard_map/pallas_call | solution.py:946
  588.7 17.0 %collective-permute-done.59.refs_2_ = bf16[2,2,144,1152]{3,2,1,0:T(8,128)(2,1)S(1)} collective-permute-done((bf16[2,2,144,1152]{3,2,1,0:T(8,128)(2,1)}, bf16[2,2,144,1152]{3,2,1,0:T(8,128)(2,1)S(1)}, u32[]{:S(2)}, u32[]{:S(2)}) %collective-permute-start.59) | collective-permute-done | bytes 1327136 | tf_op jit(solution)/shard_map/ppermute | solution.py:39
  630.9 28.2 %collective-permute-done.52.refs_1_ = bf16[2,144,1152]{2,1,0:T(8,128)(2,1)S(1)} collective-permute-done((bf16[2,144,1152]{2,1,0:T(8,128)(2,1)}, bf16[2,144,1152]{2,1,0:T(8,128)(2,1)S(1)}, u32[]{:S(2)}, u32[]{:S(2)}) %collective-permute-start.52) | collective-permute-done | bytes 663584 | tf_op jit(solution)/shard_map/ppermute | solution.py:39
  714.6 8.9 %collective-permute-done.71.refs_2_ = bf16[2,144,1152]{2,1,0:T(8,128)(2,1)S(1)} collective-permute-done((bf16[2,144,1152]{2,1,0:T(8,128)(2,1)}, bf16[2,144,1152]{2,1,0:T(8,128)(2,1)S(1)}, u32[]{:S(2)}, u32[]{:S(2)}) %collective-permute-start.71) | collective-permute-done | bytes 663584 | tf_op jit(solution)/shard_map/ppermute | solution.py:39
  783.3 9.6 %collective-permute-start.75 = (f32[32,288]{1,0:T(8,128)S(1)}, f32[32,288]{1,0:T(8,128)S(1)}, u32[]{:S(2)}, u32[]{:S(2)}) collective-permute-start(f32[32,288]{1,0:T(8,128)S(1)} %fusion.8), channel_id=1, source_target_pairs={{0,16},{1,17},{2,18},{3,19},{4,20},{5,21},{6,22},{7,23},{8,24},{9,... | collective-permute-start | bytes 110600 | tf_op jit(solution)/shard_map/ppermute | solution.py:39
  (696 shorter events, 475.6 us)
Async XLA Ops:
  7.2 49.2 %all-gather.9.cloned.1.call-start = ((), (), s32[]{:S(2)}) async-start(), calls=%async_computation.10 | async-start | bytes 1658880 | tf_op jit(solution)/shard_map/all_gather | solution.py:422
  19.1 99.2 %all-gather.11.cloned.1.call-start = ((), (), s32[]{:S(2)}) async-start(), calls=%async_computation.11 | async-start | bytes 3317760 | tf_op jit(solution)/shard_map/all_gather | solution.py:422
  100.3 51.0 %all-gather.13.cloned.1.call-start = ((), (), s32[]{:S(2)}) async-start(), calls=%async_computation.12 | async-start | bytes 1658880 | tf_op jit(solution)/shard_map/all_gather | solution.py:422
  116.0 114.7 %all-gather.15.cloned.1.call-start = ((), (), s32[]{:S(2)}) async-start(), calls=%async_computation.13 | async-start | bytes 3317760 | tf_op jit(solution)/shard_map/all_gather | solution.py:422
  121.6 46.0 %collective-permute-start.14 = (bf16[2,3,144,1152]{3,2,1,0:T(8,128)(2,1)}, bf16[2,3,144,1152]{3,2,1,0:T(8,128)(2,1)}, u32[]{:S(2)}, u32[]{:S(2)}) collective-permute-start(bf16[2,3,144,1152]{3,2,1,0:T(8,128)(2,1)} %shard_map.254.refs_12_.p0), channel_id=1, source_target_pairs={{0,1},{1,0},{2,3},{3,2},{4,5},{5,4},{6,7},{7,6},{8,9},{9,8},{10,11... | collective-permute-start | bytes 5971976 | tf_op jit(solution)/shard_map/ppermute | solution.py:39
  122.1 45.5 %collective-permute-start.15 = (bf16[2,3,144,1152]{3,2,1,0:T(8,128)(2,1)}, bf16[2,3,144,1152]{3,2,1,0:T(8,128)(2,1)}, u32[]{:S(2)}, u32[]{:S(2)}) collective-permute-start(bf16[2,3,144,1152]{3,2,1,0:T(8,128)(2,1)} %shard_map.254.refs_12_.p0), channel_id=1, source_target_pairs={{0,2},{1,3},{2,0},{3,1},{4,6},{5,7},{6,4},{7,5},{8,10},{9,11},{10,... | collective-permute-start | bytes 5971976 | tf_op jit(solution)/shard_map/ppermute | solution.py:39
  176.7 62.0 %collective-permute-start.20 = (bf16[3,2,3,144,1152]{4,3,2,1,0:T(8,128)(2,1)}, bf16[3,2,3,144,1152]{4,3,2,1,0:T(8,128)(2,1)}, u32[]{:S(2)}, u32[]{:S(2)}) collective-permute-start(bf16[3,2,3,144,1152]{4,3,2,1,0:T(8,128)(2,1)} %get-tuple-element.137.refs_5_), channel_id=1, source_target_pairs={{0,16},{1,17},{2,18},{3,19},{4,20},{5,21},{6,22},{7,23},{8,24},{9,... | collective-permute-start | bytes 17915912 | tf_op jit(solution)/shard_map/ppermute | solution.py:39
  178.8 43.9 %collective-permute-start.22 = (bf16[1,3,144,1152]{3,2,1,0:T(8,128)(2,1)S(1)}, bf16[1,3,144,1152]{3,2,1,0:T(8,128)(2,1)S(1)}, u32[]{:S(2)}, u32[]{:S(2)}) collective-permute-start(bf16[1,3,144,1152]{3,2,1,0:T(8,128)(2,1)S(1)} %copy-done.16), channel_id=1, source_target_pairs={{0,1},{1,0},{2,3},{3,2},{4,5},{5,4},{6,7},{7,6},{8,9},{9,8},{10,11... | collective-permute-start | bytes 2985992 | tf_op jit(solution)/shard_map/ppermute | solution.py:39
  179.8 44.4 %collective-permute-start.23 = (bf16[1,3,144,1152]{3,2,1,0:T(8,128)(2,1)S(1)}, bf16[1,3,144,1152]{3,2,1,0:T(8,128)(2,1)S(1)}, u32[]{:S(2)}, u32[]{:S(2)}) collective-permute-start(bf16[1,3,144,1152]{3,2,1,0:T(8,128)(2,1)S(1)} %copy-done.16), channel_id=1, source_target_pairs={{0,2},{1,3},{2,0},{3,1},{4,6},{5,7},{6,4},{7,5},{8,10},{9,11},{10,... | collective-permute-start | bytes 2985992 | tf_op jit(solution)/shard_map/ppermute | solution.py:39
  226.4 42.5 %collective-permute-start.26 = (bf16[3,1,3,144,1152]{4,3,2,1,0:T(8,128)(2,1)}, bf16[3,1,3,144,1152]{4,3,2,1,0:T(8,128)(2,1)}, u32[]{:S(2)}, u32[]{:S(2)}) collective-permute-start(bf16[3,1,3,144,1152]{4,3,2,1,0:T(8,128)(2,1)} %get-tuple-element.142.refs_4_), channel_id=1, source_target_pairs={{0,16},{1,17},{2,18},{3,19},{4,20},{5,21},{6,22},{7,23},{8,24},{9,... | collective-permute-start | bytes 8957960 | tf_op jit(solution)/shard_map/ppermute | solution.py:39
  237.6 55.3 %collective-permute-start.30 = (bf16[2,3,144,1152]{3,2,1,0:T(8,128)(2,1)}, bf16[2,3,144,1152]{3,2,1,0:T(8,128)(2,1)}, u32[]{:S(2)}, u32[]{:S(2)}) collective-permute-start(bf16[2,3,144,1152]{3,2,1,0:T(8,128)(2,1)} %shard_map.261.refs_13_.p0), channel_id=1, source_target_pairs={{0,1},{1,0},{2,3},{3,2},{4,5},{5,4},{6,7},{7,6},{8,9},{9,8},{10,11... | collective-permute-start | bytes 5971976 | tf_op jit(solution)/shard_map/ppermute | solution.py:39
  238.7 54.3 %collective-permute-start.31 = (bf16[2,3,144,1152]{3,2,1,0:T(8,128)(2,1)}, bf16[2,3,144,1152]{3,2,1,0:T(8,128)(2,1)}, u32[]{:S(2)}, u32[]{:S(2)}) collective-permute-start(bf16[2,3,144,1152]{3,2,1,0:T(8,128)(2,1)} %shard_map.261.refs_13_.p0), channel_id=1, source_target_pairs={{0,2},{1,3},{2,0},{3,1},{4,6},{5,7},{6,4},{7,5},{8,10},{9,11},{10,... | collective-permute-start | bytes 5971976 | tf_op jit(solution)/shard_map/ppermute | solution.py:39
  386.3 123.3 %all-to-all-start.2 = ((bf16[4,4,144,1152]{3,2,1,0:T(8,128)(2,1)}), bf16[4,4,144,1152]{3,2,1,0:T(8,128)(2,1)}, u32[]{:S(2)}, u32[]{:S(2)}) async-start(bf16[4,4,144,1152]{3,2,1,0:T(8,128)(2,1)} %shard_map.271.refs_4_), calls=%async_computation.2 | async-start | bytes 10616832 | tf_op jit(solution)/shard_map/all_to_all | solution.py:56
  428.6 47.6 %collective-permute-start.48 = (bf16[256,1152]{1,0:T(8,128)(2,1)S(1)}, bf16[256,1152]{1,0:T(8,128)(2,1)S(1)}, u32[]{:S(2)}, u32[]{:S(2)}) collective-permute-start(bf16[256,1152]{1,0:T(8,128)(2,1)S(1)} %fusion.4.refs_1_.refs_2_), channel_id=1, source_target_pairs={{0,16},{1,17},{2,18},{3,19},{4,20},{5,21},{6,22},{7,23},{8,24},{9,... | collective-permute-start | bytes 1769480 | tf_op jit(solution)/shard_map/ppermute | solution.py:39
  515.8 45.8 %all-to-all-start.3 = ((bf16[4,144,1152]{2,1,0:T(8,128)(2,1)}), bf16[4,144,1152]{2,1,0:T(8,128)(2,1)}, u32[]{:S(2)}, u32[]{:S(2)}) async-start(bf16[4,144,1152]{2,1,0:T(8,128)(2,1)} %shard_map.282.refs_9_), calls=%async_computation.3 | async-start | bytes 2654208 | tf_op jit(solution)/shard_map/all_to_all | solution.py:56
  522.2 43.1 %collective-permute-start.57 = (bf16[2,144,1152]{2,1,0:T(8,128)(2,1)}, bf16[2,144,1152]{2,1,0:T(8,128)(2,1)}, u32[]{:S(2)}, u32[]{:S(2)}) collective-permute-start(bf16[2,144,1152]{2,1,0:T(8,128)(2,1)} %copy-done.123), channel_id=1, source_target_pairs={{0,2},{1,3},{2,0},{3,1},{4,6},{5,7},{6,4},{7,5},{8,10},{9,11},{10,... | collective-permute-start | bytes 1990664 | tf_op jit(solution)/shard_map/ppermute | solution.py:39
  568.7 44.8 %all-to-all-start.4 = ((bf16[4,144,1152]{2,1,0:T(8,128)(2,1)}), bf16[4,144,1152]{2,1,0:T(8,128)(2,1)}, u32[]{:S(2)}, u32[]{:S(2)}) async-start(bf16[4,144,1152]{2,1,0:T(8,128)(2,1)} %shard_map.286.refs_4_), calls=%async_computation.4 | async-start | bytes 2654208 | tf_op jit(solution)/shard_map/all_to_all | solution.py:56
  576.8 44.9 %collective-permute-start.55 = (bf16[2,144,1152]{2,1,0:T(8,128)(2,1)}, bf16[2,144,1152]{2,1,0:T(8,128)(2,1)}, u32[]{:S(2)}, u32[]{:S(2)}) collective-permute-start(bf16[2,144,1152]{2,1,0:T(8,128)(2,1)} %copy-done.125), channel_id=1, source_target_pairs={{0,2},{1,3},{2,0},{3,1},{4,6},{5,7},{6,4},{7,5},{8,10},{9,11},{10,... | collective-permute-start | bytes 1990664 | tf_op jit(solution)/shard_map/ppermute | solution.py:39
  578.6 43.1 %collective-permute-start.56 = (bf16[2,144,1152]{2,1,0:T(8,128)(2,1)}, bf16[2,144,1152]{2,1,0:T(8,128)(2,1)}, u32[]{:S(2)}, u32[]{:S(2)}) collective-permute-start(bf16[2,144,1152]{2,1,0:T(8,128)(2,1)} %copy-done.124), channel_id=1, source_target_pairs={{0,1},{1,0},{2,3},{3,2},{4,5},{5,4},{6,7},{7,6},{8,9},{9,8},{10,11... | collective-permute-start | bytes 1990664 | tf_op jit(solution)/shard_map/ppermute | solution.py:39
  587.7 79.0 %collective-permute-start.63 = (bf16[2,2,144,1152]{3,2,1,0:T(8,128)(2,1)}, bf16[2,2,144,1152]{3,2,1,0:T(8,128)(2,1)}, u32[]{:S(2)}, u32[]{:S(2)}) collective-permute-start(bf16[2,2,144,1152]{3,2,1,0:T(8,128)(2,1)} %get-tuple-element.224), channel_id=1, source_target_pairs={{0,1},{1,0},{2,3},{3,2},{4,5},{5,4},{6,7},{7,6},{8,9},{9,8},{10,11... | collective-permute-start | bytes 3981320 | tf_op jit(solution)/shard_map/ppermute | solution.py:39
  605.7 60.9 %collective-permute-start.64 = (bf16[2,2,144,1152]{3,2,1,0:T(8,128)(2,1)}, bf16[2,2,144,1152]{3,2,1,0:T(8,128)(2,1)}, u32[]{:S(2)}, u32[]{:S(2)}) collective-permute-start(bf16[2,2,144,1152]{3,2,1,0:T(8,128)(2,1)} %get-tuple-element.225), channel_id=1, source_target_pairs={{0,2},{1,3},{2,0},{3,1},{4,6},{5,7},{6,4},{7,5},{8,10},{9,11},{10,... | collective-permute-start | bytes 3981320 | tf_op jit(solution)/shard_map/ppermute | solution.py:39
  625.1 53.7 %all-to-all-start.6 = ((bf16[4,144,1152]{2,1,0:T(8,128)(2,1)}), bf16[4,144,1152]{2,1,0:T(8,128)(2,1)}, u32[]{:S(2)}, u32[]{:S(2)}) async-start(bf16[4,144,1152]{2,1,0:T(8,128)(2,1)} %shard_map.290.refs_2_), calls=%async_computation.6 | async-start | bytes 2654208 | tf_op jit(solution)/shard_map/all_to_all | solution.py:56
  752.3 78.2 %collective-permute-start.85 = (bf16[3,144,1152]{2,1,0:T(8,128)(2,1)}, bf16[3,144,1152]{2,1,0:T(8,128)(2,1)}, u32[]{:S(2)}, u32[]{:S(2)}) collective-permute-start(bf16[3,144,1152]{2,1,0:T(8,128)(2,1)} %slice.166), channel_id=1, source_target_pairs={{16,17},{17,16},{18,19},{19,18},{20,21},{21,20},{22,23},{23,22},{2... | collective-permute-start | bytes 2985992 | tf_op jit(solution)/shard_map/ppermute | solution.py:39
  764.3 43.1 %collective-permute-start.77 = (bf16[2,2,144,1152]{3,2,1,0:T(8,128)(2,1)}, bf16[2,2,144,1152]{3,2,1,0:T(8,128)(2,1)}, u32[]{:S(2)}, u32[]{:S(2)}) collective-permute-start(bf16[2,2,144,1152]{3,2,1,0:T(8,128)(2,1)} %shard_map.305.refs_1_.refs_0_), channel_id=1, source_target_pairs={{0,1},{1,0},{2,3},{3,2},{4,5},{5,4},{6,7},{7,6},{8,9},{9,8},{10,11... | collective-permute-start | bytes 3981320 | tf_op jit(solution)/shard_map/ppermute | solution.py:39
  (239 other events, 2552.5 us)
Sparse Core Ops, SparseCore 0:
  19.2 37.0 all-gather.8
  58.5 58.8 all-gather.10
  119.6 31.6 all-gather.12
  176.8 53.9 all-gather.14

commit v5 on v4

--- a/solution.py
+++ b/solution.py
@@ -1182,12 +1182,12 @@
     reducer.spread(0, block0)
     reducer.third(5)
     reducer.unite(0, last)
+    reducer.spread_on(0, block0)
+    reducer.spread(0, last)
     (hop,) = reducer.hold(hop)
     small = jnp.concatenate([small, hop])
     for bit in bits[2:]:
         small = jnp.concatenate([small, cross(small, bit)])
-    reducer.spread_on(0, block0)
-    reducer.spread(0, last)
     reducer.spread_on(0, last)
     reducer.finish(1, block1)
     reducer.finish(0, block0)

time: 864 us -> 862 us (level)
  starting transfers between devices: 140 us -> 130 us
    ppermute x87, starting transfers between devices: 91.7 us -> 81.5 us  [move(): return lax.ppermute(value, ALL, pairs)]
    all_to_all x10, waiting for transfers between devices: 19.6 us -> 28.8 us  [trade(): return lax.all_to_all(value, Z, split_axis=0, concat_axis=0, tiled=True)]
    unnamed x328 -> x330, local copies, waits for them, and re-layouts: 80.6 us -> 80 us
  transfers between devices with their start and end apart: 101 -> 101, of which waited for: 37 -> 39; matrix products, arithmetic and copies ran while one was open for 9% -> 9% of each run, Pallas kernels for 29% -> 29%
where the time goes in v5:
time: 862 us; the launch traced here: 853 us
  Pallas kernels  302 us (35%)
  waiting for transfers between devices  244 us (28%)
  starting transfers between devices  130 us (15%)
  local copies, waits for them, and re-layouts  124 us (14%)
  other arithmetic  26.7 us (3%)
  between operations  15.6 us (2%)
  matrix products  10.6 us (1%)
    ppermute x87, waiting for transfers between devices, move(): return lax.ppermute(value, ALL, pairs)  206 us
    ppermute x87, starting transfers between devices, move(): return lax.ppermute(value, ALL, pairs)  81.5 us
    unnamed x330, local copies, waits for them, and re-layouts  80 us
    pallas_call x6, Pallas kernels, wgrad(): pl.pallas_call(functools.partial(wgrad_kernel, kind, mode), out_shape=(pa...  50.2 us
    all_to_all x10, starting transfers between devices, trade(): return lax.all_to_all(value, Z, split_axis=0, concat_axis=0, tiled=True)  48.1 us
    pallas_call x2, Pallas kernels, mlp(): pl.pallas_call(functools.partial(mlp_kernel, block), out_shape=(shape_of(...  43.5 us
    pallas_call x2, Pallas kernels, attend(): pl.pallas_call(functools.partial(attend_kernel, block), out_shape=(shape_...  37.6 us
    pallas_call x2, Pallas kernels, attend_back(): pl.pallas_call(attend_back_kernel, out_shape=(shape_of(BF, 2, t, HALF), s...  37.5 us
  transfers between devices with their start and end apart: 101, of which 39 were waited for; matrix products, arithmetic and copies ran while one was open for 9% of the time, Pallas kernels for 29%

profile of v5, /device:TPU:0, one launch (start us, length us, event | category | flops | bytes accessed | tf_op | source)
XLA Modules:
  0.0 852.9 jit_solution(1066720051603958603)
XLA Ops:
  64.1 21.0 %collective-permute-done.9 = s32[2,4,2,2]{1,3,2,0:T(2,128)S(1)} collective-permute-done((s32[2,4,2,2]{1,3,2,0:T(2,128)S(1)}, s32[2,4,2,2]{1,3,2,0:T(2,128)S(1)}, u32[]{:S(2)}, u32[]{:S(2)}) %collective-permute-start.9) | collective-permute-done | bytes 160 | tf_op jit(solution)/shard_map/ppermute | solution.py:39
  105.9 9.4 %all-to-all-done.1 = f32[4,2,6912]{2,1,0:T(2,128)S(1)} async-done(((f32[4,2,6912]{2,1,0:T(2,128)}), f32[4,2,6912]{2,1,0:T(2,128)S(1)}, u32[]{:S(2)}, u32[]{:S(2)}) %all-to-all-start.1) | async-done | bytes 221216 | tf_op jit(solution)/shard_map/all_to_all | solution.py:56
  126.6 18.8 %shard_map.255 = (bf16[1152,4608]{1,0:T(8,128)(2,1)}, bf16[2,256,1152]{2,1,0:T(8,128)(2,1)}, bf16[256,1152]{1,0:T(8,128)(2,1)S(1)}, bf16[256,1152]{1,0:T(8,128)(...) custom-call(bf16[256,1152]{1,0:T(8,128)(2,1)S(1)} %copy-done.25, ...), custom_call_target="tpu_custom_call" | custom-call | flops 2717908992 | bytes 21233664 | tf_op jit(solution)/shard_map/pallas_call | solution.py:762
  155.7 11.9 %collective-permute-done.14.p1 = bf16[2,3,144,1152]{3,2,1,0:T(8,128)(2,1)} collective-permute-done((bf16[2,3,144,1152]{3,2,1,0:T(8,128)(2,1)}, bf16[2,3,144,1152]{3,2,1,0:T(8,128)(2,1)}, u32[]{:S(2)}, u32[]{:S(2)}) %collective-permute-start.14) | collective-permute-done | bytes 1990688 | tf_op jit(solution)/shard_map/ppermute | solution.py:39
  180.8 21.0 %collective-permute-done.18.pa = bf16[1,3,144,1152]{3,2,1,0:T(8,128)(2,1)S(1)} collective-permute-done((bf16[1,3,144,1152]{3,2,1,0:T(8,128)(2,1)}, bf16[1,3,144,1152]{3,2,1,0:T(8,128)(2,1)S(1)}, u32[]{:S(2)}, u32[]{:S(2)}) %collective-permute-start.18) | collective-permute-done | bytes 995360 | tf_op jit(solution)/shard_map/ppermute | solution.py:39
  206.2 16.5 %collective-permute-done.22.p1 = bf16[1,3,144,1152]{3,2,1,0:T(8,128)(2,1)S(1)} collective-permute-done((bf16[1,3,144,1152]{3,2,1,0:T(8,128)(2,1)S(1)}, bf16[1,3,144,1152]{3,2,1,0:T(8,128)(2,1)S(1)}, u32[]{:S(2)}, u32[]{:S(2)}) %collective-permute-start.22) | collective-permute-done | bytes 995360 | tf_op jit(solution)/shard_map/ppermute | solution.py:39
  239.8 22.0 %shard_map.262 = (bf16[1152,4608]{1,0:T(8,128)(2,1)}, bf16[4608,1152]{1,0:T(8,128)(2,1)}, f32[256,4608]{1,0:T(8,128)}, bf16[2,4,576,256]{3,2,1,0:T(8,128)(2,1)},...) custom-call(f32[256,1152]{1,0:T(8,128)S(1)} %copy-done.38, bf16[256,1152]{1,0:T(8,128)(2,1)S(1)} %copy-done.34, ...), custom_call_target="tpu_custom_call" | custom-call | flops 5435817984 | bytes 42467328 | tf_op jit(solution)/shard_map/pallas_call | solution.py:802
  271.6 18.8 %shard_map.265 = (bf16[1152,4608]{1,0:T(8,128)(2,1)}, bf16[2,256,1152]{2,1,0:T(8,128)(2,1)}, bf16[256,1152]{1,0:T(8,128)(2,1)S(1)}, bf16[256,1152]{1,0:T(8,128)(...) custom-call(bf16[256,1152]{1,0:T(8,128)(2,1)S(1)} %get-tuple-element, ...), custom_call_target="tpu_custom_call" | custom-call | flops 2717908992 | bytes 21233664 | tf_op jit(solution)/shard_map/pallas_call | solution.py:762
  306.9 17.2 %collective-permute-done.32.pa = bf16[1,3,144,1152]{3,2,1,0:T(8,128)(2,1)} collective-permute-done((bf16[1,3,144,1152]{3,2,1,0:T(8,128)(2,1)}, bf16[1,3,144,1152]{3,2,1,0:T(8,128)(2,1)}, u32[]{:S(2)}, u32[]{:S(2)}) %collective-permute-start.32) | collective-permute-done | bytes 995360 | tf_op jit(solution)/shard_map/ppermute | solution.py:39
  334.1 21.5 %shard_map.269 = (bf16[1152,4608]{1,0:T(8,128)(2,1)}, bf16[4608,1152]{1,0:T(8,128)(2,1)}, f32[256,4608]{1,0:T(8,128)}, bf16[2,4,576,256]{3,2,1,0:T(8,128)(2,1)},...) custom-call(f32[256,1152]{1,0:T(8,128)S(1)} %copy-done.39, ...), custom_call_target="tpu_custom_call" | custom-call | flops 5435817984 | bytes 42467328 | tf_op jit(solution)/shard_map/pallas_call | solution.py:802
  358.6 16.9 %shard_map.270 = (bf16[2,256,2304]{2,1,0:T(8,128)(2,1)}, f32[256,1152]{1,0:T(8,128)S(1)}, bf16[256,1152]{1,0:T(8,128)(2,1)S(1)}, f32[16,1152]{1,0:T(8,128)S(1)}) custom-call(bf16[256,1152]{1,0:T(8,128)(2,1)S(1)} %copy-done.60, bf16[256,1152]{1,0:T(8,128)(2,1)} %get-tuple-element.303.refs_1_.refs_2_, f32[6,1152]{1,0:T(8,128)S(1)} %reshape.341.refs_1_.refs_2_.refs_3_, ...), custom_call_target="tpu_custom_call" | custom-call | tf_op jit(solution)/shard_map/pallas_call | solution.py:882
  378.0 8.2 shard_map.271.refs_4_
  396.5 8.5 %shard_map.272 = (bf16[2,2,144,1152]{3,2,1,0:T(8,128)(2,1)S(1)}, bf16[2,2,144,1152]{3,2,1,0:T(8,128)(2,1)}, bf16[2,2,144,1152]{3,2,1,0:T(8,128)(2,1)}, bf16[2,2,144,1152]{3,2,1,0:T(8,128)(2,1)}) custom-call(bf16[256,1152]{1,0:T(8,128)(2,1)S(1)} %get-tuple-element.147._.refs_1_.refs_0_, bf16[256,1152]{1,0:T(8,128)(2,1)S(1)} %collective-permute-done.38.refs_1_, ...), custom_call_target="tpu_custom_call" | custom-call | tf_op jit(solution)/shard_map/pallas_call | solution.py:516
  407.6 18.7 %shard_map.273 = (bf16[2,256,2304]{2,1,0:T(8,128)(2,1)}, f32[256,1152]{1,0:T(8,128)}, bf16[256,1152]{1,0:T(8,128)(2,1)S(1)}, bf16[16,1152]{1,0:T(8,128)(2,1)S(1)}) custom-call(bf16[256,1152]{1,0:T(8,128)(2,1)S(1)} %get-tuple-element.141._.refs_0_, f32[256,1152]{1,0:T(8,128)} %copy-done.67, bf16[256,1152]{1,0:T(8,128)(2,1)S(1)} %copy-done.101, ...), custom_call_target="tpu_custom_call" | custom-call | tf_op jit(solution)/shard_map/pallas_call | solution.py:946
  429.1 8.6 %collective-permute-done.42.refs_2_ = bf16[2,2,144,1152]{3,2,1,0:T(8,128)(2,1)S(1)} collective-permute-done((bf16[2,2,144,1152]{3,2,1,0:T(8,128)(2,1)}, bf16[2,2,144,1152]{3,2,1,0:T(8,128)(2,1)S(1)}, u32[]{:S(2)}, u32[]{:S(2)}) %collective-permute-start.42) | collective-permute-done | bytes 1327136 | tf_op jit(solution)/shard_map/ppermute | solution.py:39
  444.0 9.0 %shard_map.275 = (bf16[2,2,144,1152]{3,2,1,0:T(8,128)(2,1)}, bf16[2,2,144,1152]{3,2,1,0:T(8,128)(2,1)}, bf16[2,2,144,1152]{3,2,1,0:T(8,128)(2,1)}, bf16[2,2,144,1152]{3,2,1,0:T(8,128)(2,1)}) custom-call(bf16[2,256,1152]{2,1,0:T(8,128)(2,1)S(1)} %copy-done.71, bf16[2,256,1152]{2,1,0:T(8,128)(2,1)} %shard_map.267._.refs_1_, ...), custom_call_target="tpu_custom_call" | custom-call | tf_op jit(solution)/shard_map/pallas_call | solution.py:516
  454.7 16.6 %shard_map.276 = (bf16[2,256,2304]{2,1,0:T(8,128)(2,1)}, f32[256,1152]{1,0:T(8,128)S(1)}, bf16[256,1152]{1,0:T(8,128)(2,1)S(1)}, f32[16,1152]{1,0:T(8,128)S(1)}) custom-call(bf16[256,1152]{1,0:T(8,128)(2,1)S(1)} %get-tuple-element.169.refs_4_.refs_0_, bf16[256,1152]{1,0:T(8,128)(2,1)S(1)} %fusion.4.refs_1_.refs_2_, f32[6,1152]{1,0:T(8,128)S(1)} %copy-done.75, ...), custom_call_target="tpu_custom_call" | custom-call | tf_op jit(solution)/shard_map/pallas_call | solution.py:882
  476.9 8.2 shard_map.277
  500.3 8.1 shard_map.280
  530.9 18.9 %shard_map.283 = (bf16[2,256,2304]{2,1,0:T(8,128)(2,1)}, f32[256,1152]{1,0:T(8,128)}, bf16[256,1152]{1,0:T(8,128)(2,1)S(1)}, bf16[16,1152]{1,0:T(8,128)(2,1)S(1)}) custom-call(bf16[256,1152]{1,0:T(8,128)(2,1)S(1)} %copy-done.26, f32[256,1152]{1,0:T(8,128)} %copy-done.66, bf16[256,1152]{1,0:T(8,128)(2,1)S(1)} %copy-done.99, f32[6,1152]{1,0:T(8,128)S(1)} %copy-done.75, ...), custom_call_target="tpu_custom_call" | custom-call | tf_op jit(solution)/shard_map/pallas_call | solution.py:946
  579.6 8.1 shard_map.287
  588.7 17.0 %collective-permute-done.59.refs_2_ = bf16[2,2,144,1152]{3,2,1,0:T(8,128)(2,1)S(1)} collective-permute-done((bf16[2,2,144,1152]{3,2,1,0:T(8,128)(2,1)}, bf16[2,2,144,1152]{3,2,1,0:T(8,128)(2,1)S(1)}, u32[]{:S(2)}, u32[]{:S(2)}) %collective-permute-start.59) | collective-permute-done | bytes 1327136 | tf_op jit(solution)/shard_map/ppermute | solution.py:39
  630.8 28.3 %collective-permute-done.52.refs_1_ = bf16[2,144,1152]{2,1,0:T(8,128)(2,1)S(1)} collective-permute-done((bf16[2,144,1152]{2,1,0:T(8,128)(2,1)}, bf16[2,144,1152]{2,1,0:T(8,128)(2,1)S(1)}, u32[]{:S(2)}, u32[]{:S(2)}) %collective-permute-start.52) | collective-permute-done | bytes 663584 | tf_op jit(solution)/shard_map/ppermute | solution.py:39
  712.7 8.7 %collective-permute-done.71.refs_2_ = bf16[2,144,1152]{2,1,0:T(8,128)(2,1)} collective-permute-done((bf16[2,144,1152]{2,1,0:T(8,128)(2,1)}, bf16[2,144,1152]{2,1,0:T(8,128)(2,1)}, u32[]{:S(2)}, u32[]{:S(2)}) %collective-permute-start.71) | collective-permute-done | bytes 663584 | tf_op jit(solution)/shard_map/ppermute | solution.py:39
  (698 shorter events, 475.3 us)
Async XLA Ops:
  7.2 49.1 %all-gather.9.cloned.1.call-start = ((), (), s32[]{:S(2)}) async-start(), calls=%async_computation.10 | async-start | bytes 1658880 | tf_op jit(solution)/shard_map/all_gather | solution.py:422
  19.1 99.2 %all-gather.11.cloned.1.call-start = ((), (), s32[]{:S(2)}) async-start(), calls=%async_computation.11 | async-start | bytes 3317760 | tf_op jit(solution)/shard_map/all_gather | solution.py:422
  100.3 51.0 %all-gather.13.cloned.1.call-start = ((), (), s32[]{:S(2)}) async-start(), calls=%async_computation.12 | async-start | bytes 1658880 | tf_op jit(solution)/shard_map/all_gather | solution.py:422
  116.0 114.7 %all-gather.15.cloned.1.call-start = ((), (), s32[]{:S(2)}) async-start(), calls=%async_computation.13 | async-start | bytes 3317760 | tf_op jit(solution)/shard_map/all_gather | solution.py:422
  121.5 46.0 %collective-permute-start.14 = (bf16[2,3,144,1152]{3,2,1,0:T(8,128)(2,1)}, bf16[2,3,144,1152]{3,2,1,0:T(8,128)(2,1)}, u32[]{:S(2)}, u32[]{:S(2)}) collective-permute-start(bf16[2,3,144,1152]{3,2,1,0:T(8,128)(2,1)} %shard_map.254.refs_12_.p0), channel_id=1, source_target_pairs={{0,1},{1,0},{2,3},{3,2},{4,5},{5,4},{6,7},{7,6},{8,9},{9,8},{10,11... | collective-permute-start | bytes 5971976 | tf_op jit(solution)/shard_map/ppermute | solution.py:39
  122.1 45.5 %collective-permute-start.15 = (bf16[2,3,144,1152]{3,2,1,0:T(8,128)(2,1)}, bf16[2,3,144,1152]{3,2,1,0:T(8,128)(2,1)}, u32[]{:S(2)}, u32[]{:S(2)}) collective-permute-start(bf16[2,3,144,1152]{3,2,1,0:T(8,128)(2,1)} %shard_map.254.refs_12_.p0), channel_id=1, source_target_pairs={{0,2},{1,3},{2,0},{3,1},{4,6},{5,7},{6,4},{7,5},{8,10},{9,11},{10,... | collective-permute-start | bytes 5971976 | tf_op jit(solution)/shard_map/ppermute | solution.py:39
  176.7 62.0 %collective-permute-start.20 = (bf16[3,2,3,144,1152]{4,3,2,1,0:T(8,128)(2,1)}, bf16[3,2,3,144,1152]{4,3,2,1,0:T(8,128)(2,1)}, u32[]{:S(2)}, u32[]{:S(2)}) collective-permute-start(bf16[3,2,3,144,1152]{4,3,2,1,0:T(8,128)(2,1)} %get-tuple-element.137.refs_5_), channel_id=1, source_target_pairs={{0,16},{1,17},{2,18},{3,19},{4,20},{5,21},{6,22},{7,23},{8,24},{9,... | collective-permute-start | bytes 17915912 | tf_op jit(solution)/shard_map/ppermute | solution.py:39
  178.8 43.9 %collective-permute-start.22 = (bf16[1,3,144,1152]{3,2,1,0:T(8,128)(2,1)S(1)}, bf16[1,3,144,1152]{3,2,1,0:T(8,128)(2,1)S(1)}, u32[]{:S(2)}, u32[]{:S(2)}) collective-permute-start(bf16[1,3,144,1152]{3,2,1,0:T(8,128)(2,1)S(1)} %copy-done.16), channel_id=1, source_target_pairs={{0,1},{1,0},{2,3},{3,2},{4,5},{5,4},{6,7},{7,6},{8,9},{9,8},{10,11... | collective-permute-start | bytes 2985992 | tf_op jit(solution)/shard_map/ppermute | solution.py:39
  179.8 44.4 %collective-permute-start.23 = (bf16[1,3,144,1152]{3,2,1,0:T(8,128)(2,1)S(1)}, bf16[1,3,144,1152]{3,2,1,0:T(8,128)(2,1)S(1)}, u32[]{:S(2)}, u32[]{:S(2)}) collective-permute-start(bf16[1,3,144,1152]{3,2,1,0:T(8,128)(2,1)S(1)} %copy-done.16), channel_id=1, source_target_pairs={{0,2},{1,3},{2,0},{3,1},{4,6},{5,7},{6,4},{7,5},{8,10},{9,11},{10,... | collective-permute-start | bytes 2985992 | tf_op jit(solution)/shard_map/ppermute | solution.py:39
  226.4 42.5 %collective-permute-start.26 = (bf16[3,1,3,144,1152]{4,3,2,1,0:T(8,128)(2,1)}, bf16[3,1,3,144,1152]{4,3,2,1,0:T(8,128)(2,1)}, u32[]{:S(2)}, u32[]{:S(2)}) collective-permute-start(bf16[3,1,3,144,1152]{4,3,2,1,0:T(8,128)(2,1)} %get-tuple-element.142.refs_4_), channel_id=1, source_target_pairs={{0,16},{1,17},{2,18},{3,19},{4,20},{5,21},{6,22},{7,23},{8,24},{9,... | collective-permute-start | bytes 8957960 | tf_op jit(solution)/shard_map/ppermute | solution.py:39
  237.7 55.3 %collective-permute-start.30 = (bf16[2,3,144,1152]{3,2,1,0:T(8,128)(2,1)}, bf16[2,3,144,1152]{3,2,1,0:T(8,128)(2,1)}, u32[]{:S(2)}, u32[]{:S(2)}) collective-permute-start(bf16[2,3,144,1152]{3,2,1,0:T(8,128)(2,1)} %shard_map.261.refs_13_.p0), channel_id=1, source_target_pairs={{0,1},{1,0},{2,3},{3,2},{4,5},{5,4},{6,7},{7,6},{8,9},{9,8},{10,11... | collective-permute-start | bytes 5971976 | tf_op jit(solution)/shard_map/ppermute | solution.py:39
  238.7 54.2 %collective-permute-start.31 = (bf16[2,3,144,1152]{3,2,1,0:T(8,128)(2,1)}, bf16[2,3,144,1152]{3,2,1,0:T(8,128)(2,1)}, u32[]{:S(2)}, u32[]{:S(2)}) collective-permute-start(bf16[2,3,144,1152]{3,2,1,0:T(8,128)(2,1)} %shard_map.261.refs_13_.p0), channel_id=1, source_target_pairs={{0,2},{1,3},{2,0},{3,1},{4,6},{5,7},{6,4},{7,5},{8,10},{9,11},{10,... | collective-permute-start | bytes 5971976 | tf_op jit(solution)/shard_map/ppermute | solution.py:39
  386.3 123.2 %all-to-all-start.2 = ((bf16[4,4,144,1152]{3,2,1,0:T(8,128)(2,1)}), bf16[4,4,144,1152]{3,2,1,0:T(8,128)(2,1)}, u32[]{:S(2)}, u32[]{:S(2)}) async-start(bf16[4,4,144,1152]{3,2,1,0:T(8,128)(2,1)} %shard_map.271.refs_4_), calls=%async_computation.2 | async-start | bytes 10616832 | tf_op jit(solution)/shard_map/all_to_all | solution.py:56
  428.6 47.6 %collective-permute-start.48 = (bf16[256,1152]{1,0:T(8,128)(2,1)S(1)}, bf16[256,1152]{1,0:T(8,128)(2,1)S(1)}, u32[]{:S(2)}, u32[]{:S(2)}) collective-permute-start(bf16[256,1152]{1,0:T(8,128)(2,1)S(1)} %fusion.4.refs_1_.refs_2_), channel_id=1, source_target_pairs={{0,16},{1,17},{2,18},{3,19},{4,20},{5,21},{6,22},{7,23},{8,24},{9,... | collective-permute-start | bytes 1769480 | tf_op jit(solution)/shard_map/ppermute | solution.py:39
  515.7 45.8 %all-to-all-start.3 = ((bf16[4,144,1152]{2,1,0:T(8,128)(2,1)}), bf16[4,144,1152]{2,1,0:T(8,128)(2,1)}, u32[]{:S(2)}, u32[]{:S(2)}) async-start(bf16[4,144,1152]{2,1,0:T(8,128)(2,1)} %shard_map.282.refs_9_), calls=%async_computation.3 | async-start | bytes 2654208 | tf_op jit(solution)/shard_map/all_to_all | solution.py:56
  522.1 43.1 %collective-permute-start.57 = (bf16[2,144,1152]{2,1,0:T(8,128)(2,1)}, bf16[2,144,1152]{2,1,0:T(8,128)(2,1)}, u32[]{:S(2)}, u32[]{:S(2)}) collective-permute-start(bf16[2,144,1152]{2,1,0:T(8,128)(2,1)} %copy-done.121), channel_id=1, source_target_pairs={{0,2},{1,3},{2,0},{3,1},{4,6},{5,7},{6,4},{7,5},{8,10},{9,11},{10,... | collective-permute-start | bytes 1990664 | tf_op jit(solution)/shard_map/ppermute | solution.py:39
  568.6 44.9 %all-to-all-start.4 = ((bf16[4,144,1152]{2,1,0:T(8,128)(2,1)}), bf16[4,144,1152]{2,1,0:T(8,128)(2,1)}, u32[]{:S(2)}, u32[]{:S(2)}) async-start(bf16[4,144,1152]{2,1,0:T(8,128)(2,1)} %shard_map.286.refs_4_), calls=%async_computation.4 | async-start | bytes 2654208 | tf_op jit(solution)/shard_map/all_to_all | solution.py:56
  576.8 44.9 %collective-permute-start.55 = (bf16[2,144,1152]{2,1,0:T(8,128)(2,1)}, bf16[2,144,1152]{2,1,0:T(8,128)(2,1)}, u32[]{:S(2)}, u32[]{:S(2)}) collective-permute-start(bf16[2,144,1152]{2,1,0:T(8,128)(2,1)} %copy-done.123), channel_id=1, source_target_pairs={{0,2},{1,3},{2,0},{3,1},{4,6},{5,7},{6,4},{7,5},{8,10},{9,11},{10,... | collective-permute-start | bytes 1990664 | tf_op jit(solution)/shard_map/ppermute | solution.py:39
  578.5 43.1 %collective-permute-start.56 = (bf16[2,144,1152]{2,1,0:T(8,128)(2,1)}, bf16[2,144,1152]{2,1,0:T(8,128)(2,1)}, u32[]{:S(2)}, u32[]{:S(2)}) collective-permute-start(bf16[2,144,1152]{2,1,0:T(8,128)(2,1)} %copy-done.122), channel_id=1, source_target_pairs={{0,1},{1,0},{2,3},{3,2},{4,5},{5,4},{6,7},{7,6},{8,9},{9,8},{10,11... | collective-permute-start | bytes 1990664 | tf_op jit(solution)/shard_map/ppermute | solution.py:39
  587.7 79.0 %collective-permute-start.63 = (bf16[2,2,144,1152]{3,2,1,0:T(8,128)(2,1)}, bf16[2,2,144,1152]{3,2,1,0:T(8,128)(2,1)}, u32[]{:S(2)}, u32[]{:S(2)}) collective-permute-start(bf16[2,2,144,1152]{3,2,1,0:T(8,128)(2,1)} %get-tuple-element.224), channel_id=1, source_target_pairs={{0,1},{1,0},{2,3},{3,2},{4,5},{5,4},{6,7},{7,6},{8,9},{9,8},{10,11... | collective-permute-start | bytes 3981320 | tf_op jit(solution)/shard_map/ppermute | solution.py:39
  605.7 61.0 %collective-permute-start.64 = (bf16[2,2,144,1152]{3,2,1,0:T(8,128)(2,1)}, bf16[2,2,144,1152]{3,2,1,0:T(8,128)(2,1)}, u32[]{:S(2)}, u32[]{:S(2)}) collective-permute-start(bf16[2,2,144,1152]{3,2,1,0:T(8,128)(2,1)} %get-tuple-element.225), channel_id=1, source_target_pairs={{0,2},{1,3},{2,0},{3,1},{4,6},{5,7},{6,4},{7,5},{8,10},{9,11},{10,... | collective-permute-start | bytes 3981320 | tf_op jit(solution)/shard_map/ppermute | solution.py:39
  625.0 53.8 %all-to-all-start.6 = ((bf16[4,144,1152]{2,1,0:T(8,128)(2,1)}), bf16[4,144,1152]{2,1,0:T(8,128)(2,1)}, u32[]{:S(2)}, u32[]{:S(2)}) async-start(bf16[4,144,1152]{2,1,0:T(8,128)(2,1)} %shard_map.290.refs_2_), calls=%async_computation.6 | async-start | bytes 2654208 | tf_op jit(solution)/shard_map/all_to_all | solution.py:56
  777.8 51.6 %collective-permute-start.85 = (bf16[3,144,1152]{2,1,0:T(8,128)(2,1)}, bf16[3,144,1152]{2,1,0:T(8,128)(2,1)}, u32[]{:S(2)}, u32[]{:S(2)}) collective-permute-start(bf16[3,144,1152]{2,1,0:T(8,128)(2,1)} %slice.166), channel_id=1, source_target_pairs={{16,17},{17,16},{18,19},{19,18},{20,21},{21,20},{22,23},{23,22},{2... | collective-permute-start | bytes 2985992 | tf_op jit(solution)/shard_map/ppermute | solution.py:39
  781.6 54.1 %collective-permute-start.86 = (bf16[3,144,1152]{2,1,0:T(8,128)(2,1)}, bf16[3,144,1152]{2,1,0:T(8,128)(2,1)}, u32[]{:S(2)}, u32[]{:S(2)}) collective-permute-start(bf16[3,144,1152]{2,1,0:T(8,128)(2,1)} %slice.167), channel_id=1, source_target_pairs={{16,18},{17,19},{18,16},{19,17},{20,22},{21,23},{22,20},{23,21},{2... | collective-permute-start | bytes 2985992 | tf_op jit(solution)/shard_map/ppermute | solution.py:39
  (240 other events, 2513.0 us)
Sparse Core Ops, SparseCore 0:
  19.2 37.0 all-gather.8
  58.5 58.8 all-gather.10
  119.6 31.6 all-gather.12
  176.8 53.9 all-gather.14
